TPU v7x, 32 devices: a whole 2x2x4 slice. The times are simulated.
32 devices in a mesh: seq: 8 (over y, x, core), head: 4 (over z).
Axes of the slice: x: 2, y: 2, z: 4, core: 2. Of those that a mesh axis runs over, the one named last changes fastest.
Arguments:
- queries: bfloat16 [16, 2048, 128], P('head', 'seq'), may hold values from -9 to 9
- key_vectors: bfloat16 [16, 2048, 128], P('head', 'seq'), may hold values from -9 to 9
- value_vectors: bfloat16 [16, 2048, 128], P('head', 'seq'), may hold values from -16 to 16
- block_perm: int32 [16, 4], P('head'), may hold values from 0 to 3, each once within a row
- out_weight: bfloat16 [16, 128, 2048], P('head'), may hold values from -0.125 to 0.125
- out_cotangent: bfloat16 [2048, 2048], P('seq', 'head'), may hold values from -6 to 6
Outputs:
- projected: bfloat16 [2048, 2048], P('seq', 'head')
- gradient_of_queries: bfloat16 [16, 2048, 128], P('head', 'seq')
- key_grad: bfloat16 [16, 2048, 128], P('head', 'seq')
- value_grad: bfloat16 [16, 2048, 128], P('head', 'seq')
Inputs may be any that keep to these rules, and one draw needn't show every extreme that they name: Each row of block_perm names every block of 0 to 3 once.
All inputs are finite; a program needn't handle non-finite values.
Results may differ from a plain program's by a relative error of at most 0.029.
Values may be sent and summed in bfloat16 or wider, within the bound.
No kernel may reach another device: no remote copies, remote signals or barrier semaphores. Data moves between devices by JAX's collectives and lax.ppermute only.
A program may use at most 64 MiB of HBM per device.

v0:
```python
import math

import jax
import jax.numpy as jnp
from jax import lax
from jax.sharding import PartitionSpec as P


def partner(shard, axis, bit):
    return lax.ppermute(shard, axis, [(i, i ^ 1 << bit) for i in range(lax.axis_size(axis))])


def per_device(queries, key_vectors, value_vectors, block_perm, out_weight, out_cotangent):
    devices = lax.axis_size("seq")
    position = lax.axis_index("seq")
    parity = position % 2
    group_heads, tok_rows, head_width = queries.shape
    portion = tok_rows * head_width // devices
    score_scale = 1.0 / math.sqrt(head_width)
    owners = jnp.repeat(block_perm, 2, axis=1)
    indices = lax.iota(jnp.int32, devices)
    sources = [2 * owners, 2 * owners + 1]
    source_table = jnp.stack(sources, axis=1)
    slot_count = source_table.shape[1]
    select = (source_table[..., None] == indices).astype(jnp.bfloat16)
    stacked = jnp.stack([key_vectors, value_vectors])
    spread = lax.all_to_all(
        stacked.reshape(2, group_heads, devices, portion),
        "seq",
        split_axis=2,
        concat_axis=2,
        tiled=True,
    )
    picked = jnp.einsum(
        "hsij,chjl->chsil", select, spread, preferred_element_type=jnp.float32
    ).astype(jnp.bfloat16)
    routed = lax.all_to_all(picked, "seq", split_axis=3, concat_axis=3, tiled=True)
    routed = routed.reshape(2, group_heads, slot_count, tok_rows, head_width)
    partner_kv = routed.reshape(2, group_heads, 2 * tok_rows, head_width)
    pair_other = partner(stacked, "seq", 0)
    local_kv = jnp.where(
        parity == 0,
        jnp.concatenate([stacked, pair_other], 2),
        jnp.concatenate([pair_other, stacked], 2),
    )
    combined = jnp.concatenate([local_kv, partner_kv], 2)
    key_all = combined[0]
    value_all = combined[1]
    logit_scores = (
        jnp.einsum("htd,hkd->htk", queries, key_all, preferred_element_type=jnp.float32)
        * score_scale
    )
    row_max = jnp.max(logit_scores, axis=-1, keepdims=True)
    weights = jnp.exp(logit_scores - row_max)
    probabilities = weights / jnp.sum(weights, axis=-1, keepdims=True)
    reduced_probabilities = probabilities.astype(jnp.bfloat16)
    attention_result = jnp.einsum(
        "htk,hkd->htd", reduced_probabilities, value_all, preferred_element_type=jnp.float32
    ).astype(jnp.bfloat16)
    partial_out = jnp.einsum(
        "htd,hde->te", attention_result, out_weight, preferred_element_type=jnp.float32
    )
    summed = lax.psum(partial_out.astype(jnp.bfloat16), "head").astype(jnp.float32)
    columns = summed.shape[1] // lax.axis_size("head")
    result = lax.dynamic_slice_in_dim(summed, lax.axis_index("head") * columns, columns, 1)
    projected = result.astype(jnp.bfloat16)
    full_grad = lax.all_gather(out_cotangent, "head", axis=1, tiled=True)
    grad_att = jnp.einsum(
        "te,hde->htd", full_grad, out_weight, preferred_element_type=jnp.float32
    ).astype(jnp.bfloat16)
    row_delta = jnp.sum(
        grad_att.astype(jnp.float32) * attention_result.astype(jnp.float32), axis=-1, keepdims=True
    )
    probability_gradient = jnp.einsum(
        "htd,hkd->htk", grad_att, value_all, preferred_element_type=jnp.float32
    )
    score_gradient = (probabilities * (probability_gradient - row_delta) * score_scale).astype(
        jnp.bfloat16
    )
    gradient_of_queries = jnp.einsum(
        "htk,hkd->htd", score_gradient, key_all, preferred_element_type=jnp.float32
    ).astype(jnp.bfloat16)
    key_part = jnp.einsum(
        "htk,htd->hkd", score_gradient, queries, preferred_element_type=jnp.float32
    )
    value_part = jnp.einsum(
        "htk,htd->hkd", reduced_probabilities, grad_att, preferred_element_type=jnp.float32
    )
    gradients = jnp.stack([key_part, value_part])
    block_rows = 2 * tok_rows
    local_grad = gradients[:, :, :block_rows].reshape(2, group_heads, 2, tok_rows, head_width)
    own_grad = jnp.where(parity == 0, local_grad[:, :, 0], local_grad[:, :, 1])
    other_grad = jnp.where(parity == 0, local_grad[:, :, 1], local_grad[:, :, 0]).astype(
        jnp.bfloat16
    )
    partner_grad = gradients[:, :, block_rows:].reshape(2, group_heads, 2, tok_rows, head_width)
    partner_grad = partner_grad.astype(jnp.bfloat16)
    returned = lax.all_to_all(
        partner_grad.reshape(2, group_heads, slot_count, devices, portion),
        "seq",
        split_axis=3,
        concat_axis=3,
        tiled=True,
    )
    summed_back = jnp.einsum(
        "hsij,chsil->chjl", select, returned, preferred_element_type=jnp.float32
    ).astype(jnp.bfloat16)
    arrived = lax.all_to_all(summed_back, "seq", split_axis=2, concat_axis=2, tiled=True)
    arrived = arrived.reshape(2, group_heads, tok_rows, head_width).astype(jnp.float32)
    pair_back = partner(other_grad, "seq", 0).astype(jnp.float32)
    total_grad = own_grad + arrived + pair_back
    key_grad = total_grad[0].astype(jnp.bfloat16)
    value_grad = total_grad[1].astype(jnp.bfloat16)
    return (projected, gradient_of_queries, key_grad, value_grad)


def solution(mesh):
    return jax.shard_map(
        per_device,
        mesh=mesh,
        in_specs=(
            P("head", "seq", None),
            P("head", "seq", None),
            P("head", "seq", None),
            P("head", None),
            P("head", None, None),
            P("seq", "head"),
        ),
        out_specs=(
            P("seq", "head"),
            P("head", "seq", None),
            P("head", "seq", None),
            P("head", "seq", None),
        ),
        check_vma=False,
    )
```

profile of v0, /device:TPU:0, one launch (start us, length us, event | category | flops | bytes accessed | tf_op | source)
XLA Modules:
  0.0 151.9 jit_solution(18130646725824927216)
XLA Ops:
  7.2 0.0 copy-start
  7.2 1.2 stack.33
  8.4 1.1 stack.32
  9.5 0.1 pad_maximum_fusion.3
  9.5 1.4 copy.60
  10.9 5.2 %all-to-all-start = ((bf16[2,4,8,4096]{3,0,1,2:T(2,128)(2,1)}), bf16[2,4,8,4096]{3,0,1,2:T(2,128)(2,1)S(1)}, u32[]{:S(2)}, u32[]{:S(2)}) async-start(bf16[2,4,8,4096]{3,0,1,2:T(2,128)(2,1)} %copy.60), calls=%async_computation | async-start | bytes 1048576 | tf_op jit(solution)/shard_map/all_to_all | solution.py:27
  16.1 0.1 copy.61
  16.2 0.1 copy.62
  16.3 9.5 %all-to-all-done = bf16[2,4,8,4096]{3,0,1,2:T(2,128)(2,1)S(1)} async-done(((bf16[2,4,8,4096]{3,0,1,2:T(2,128)(2,1)}), bf16[2,4,8,4096]{3,0,1,2:T(2,128)(2,1)S(1)}, u32[]{:S(2)}, u32[]{:S(2)}) %all-to-all-start) | async-done | bytes 524320 | tf_op jit(solution)/shard_map/all_to_all | solution.py:27
  25.8 0.5 fusion.1
  26.3 0.0 copy-start.10
  26.3 0.0 copy-start.11
  26.3 2.1 %copy.65 = bf16[2,4,2,8,4096]{4,2,0,1,3:T(2,128)(2,1)} copy(bf16[2,4,2,8,4096]{4,3,2,0,1:T(8,128)(2,1)S(1)} %fusion.1) | data formatting | bytes 2097152 | tf_op jit(solution)/shard_map/convert_element_type | solution.py:36
  28.4 4.2 %all-to-all-start.1 = ((bf16[2,4,2,8,4096]{4,2,0,1,3:T(2,128)(2,1)}), bf16[2,4,2,8,4096]{4,2,0,1,3:T(2,128)(2,1)}, u32[]{:S(2)}, u32[]{:S(2)}) async-start(bf16[2,4,2,8,4096]{4,2,0,1,3:T(2,128)(2,1)} %copy.65), calls=%async_computation.1 | async-start | bytes 2097152 | tf_op jit(solution)/shard_map/all_to_all | solution.py:37
  32.7 0.0 all-gather.2.cloned.1.call-start
  32.7 0.1 pad_maximum_fusion.2
  32.8 0.4 collective-permute-start
  33.2 0.2 all-gather.2.cloned.1.call-update
  33.4 1.5 collective-permute-done
  34.9 1.7 %maximum_select_fusion = bf16[2,4,512,128]{3,2,1,0:T(8,128)(2,1)S(1)} fusion(bf16[2,4,256,128]{3,2,1,0:T(8,128)(2,1)} %collective-permute-done, bf16[1,4,256,128]{3,2,1,0:T(8,128)(2,1)S(1)} %bitcast.113, bf16[1,4,256,128]{3,2,1,0:T(8,128)(2,1)} %bitcast.114, pred[]{:T(512)S(6)} %eq.10), kind=kLoop, calls=%fused_computation.35 | loop fusion | flops 6815744 | bytes 2097153 | tf_op jit(solution)/shard_map/jit(_where)/select_n | solution.py:41
  36.5 11.5 %all-to-all-done.1 = bf16[2,4,2,8,4096]{4,2,0,1,3:T(2,128)(2,1)} async-done(((bf16[2,4,2,8,4096]{4,2,0,1,3:T(2,128)(2,1)}), bf16[2,4,2,8,4096]{4,2,0,1,3:T(2,128)(2,1)}, u32[]{:S(2)}, u32[]{:S(2)}) %all-to-all-start.1) | async-done | bytes 1048608 | tf_op jit(solution)/shard_map/all_to_all | solution.py:37
  48.1 2.8 %copy.66 = bf16[2,4,2,8,4096]{4,3,2,1,0:T(8,128)(2,1)} copy(bf16[2,4,2,8,4096]{4,2,0,1,3:T(2,128)(2,1)} %all-to-all-done.1) | data formatting | bytes 2097152 | tf_op jit(solution)/shard_map/all_to_all | solution.py:37
  50.9 2.4 %reshape_reshape.3 = bf16[2,4,512,128]{3,2,1,0:T(8,128)(2,1)} reshape(bf16[2,4,2,8,4096]{4,3,2,1,0:T(8,128)(2,1)} %copy.66) | data formatting | bytes 2097152 | tf_op jit(solution)/shard_map/reshape;reshape | solution.py:39
  53.2 2.2 %fusion.15 = bf16[4,1024,128]{2,1,0:T(8,128)(2,1)} fusion(bf16[2,4,512,128]{3,2,1,0:T(8,128)(2,1)S(1)} %maximum_select_fusion, bf16[2,4,512,128]{3,2,1,0:T(8,128)(2,1)} %reshape_reshape.3), kind=kLoop, calls=%fused_computation.30 | loop fusion | flops 2097152 | bytes 3145728 | tf_op jit(solution)/shard_map/squeeze | solution.py:47
  55.4 4.6 %fusion.36 = (f32[4,256]{1,0:T(4,128)S(1)}, f32[4,256,1024]{1,2,0:T(8,128)}) fusion(bf16[4,1024,128]{2,1,0:T(8,128)(2,1)} %fusion.15, bf16[4,256,128]{2,1,0:T(8,128)(2,1)S(1)} %copy-done.12), kind=kOutput, calls=%fused_computation.63 | convolution fusion | flops 271582208 | bytes 5509120 | tf_op jit(solution)/shard_map/sub | solution.py:54
  60.1 2.6 %fusion.13 = bf16[4,256,1024]{1,2,0:T(8,128)(2,1)S(1)} fusion(f32[4,256,1024]{1,2,0:T(8,128)} %get-tuple-element.7, f32[4,256]{1,0:T(4,128)S(1)} %get-tuple-element.6), kind=kLoop, calls=%fused_computation.23 | loop fusion | flops 2097152 | bytes 6295552 | tf_op jit(solution)/shard_map/convert_element_type | solution.py:56
  62.7 1.3 copy-done.3
  64.0 0.6 convolution_convert_fusion.3
  64.6 0.0 all-gather.2.cloned.1.call-done
  64.6 0.0 copy-done
  64.7 2.1 %fusion.22 = (f32[4,256]{1,0:T(4,128)S(1)}, bf16[4,128,256]{2,1,0:T(8,128)(2,1)S(1)}) fusion(bf16[4,256,128]{1,2,0:T(8,128)(2,1)S(1)} %convolution_convert_fusion.3, bf16[4,128,2048]{2,1,0:T(8,128)(2,1)S(1)} %copy-done, bf16[256,2048]{1,0:T(8,128)(2,1)} %all-gather.2.cloned.1.call-done), kind=kOutput, calls=%fused_computation.46 | convolution fusion | flops 537525248 | bytes 3674112 | tf_op jit(solution)/shard_map/te,hde->htd/dot_general | solution.py:68
  66.8 0.0 copy-done.4
  66.8 0.0 copy-start.6
  66.8 0.7 convolution_bitcast_fusion.2
  67.5 0.2 copy-done.9
  67.8 0.5 copy-done.6
  68.3 0.8 multiply_convert_fusion
  69.1 0.1 copy-done.13
  69.2 0.7 convolution_bitcast_fusion.3
  69.9 0.6 copy-done.7
  70.5 1.4 copy-done.2
  71.9 0.2 fusion.11
  72.0 1.3 convert_element_type.88
  73.3 3.3 %copy.75 = bf16[2,4,2,8,4096]{4,2,0,1,3:T(2,128)(2,1)} copy(bf16[2,4,2,8,4096]{4,3,2,1,0:T(8,128)(2,1)} %convert_element_type.88) | data formatting | bytes 2097152 | tf_op jit(solution)/shard_map/convert_element_type | solution.py:97
  76.6 3.6 %all-to-all-start.2 = ((bf16[2,4,2,8,4096]{4,2,0,1,3:T(2,128)(2,1)}), bf16[2,4,2,8,4096]{4,2,0,1,3:T(2,128)(2,1)S(1)}, u32[]{:S(2)}, u32[]{:S(2)}) async-start(bf16[2,4,2,8,4096]{4,2,0,1,3:T(2,128)(2,1)} %copy.75), calls=%async_computation.2 | async-start | bytes 2097152 | tf_op jit(solution)/shard_map/all_to_all | solution.py:98
  80.3 0.2 all-reduce.2.cloned.1.call-start
  80.5 1.7 %fusion.9 = bf16[256,2048]{1,0:T(8,128)(2,1)} fusion(bf16[4,256,128]{1,2,0:T(8,128)(2,1)S(1)} %convolution_convert_fusion.3, bf16[4,128,2048]{2,1,0:T(8,128)(2,1)S(1)} %copy-done), kind=kOutput, calls=%fused_computation.15 | convolution fusion | flops 537395200 | bytes 3407872 | tf_op jit(solution)/shard_map/htd,hde->te/dot_general | solution.py:60
  82.2 0.0 all-reduce.2.cloned.1.call-update
  82.2 3.0 %fusion.10 = f32[2,4,512,128]{3,2,1,0:T(8,128)} fusion(f32[1,4,1024,128]{3,2,1,0:T(8,128)} %copy-done.2, f32[1,4,1024,128]{3,2,1,0:T(8,128)} %copy-done.1), kind=kLoop, calls=%fused_computation.16 | loop fusion | flops 524288 | bytes 6291456 | tf_op jit(solution)/shard_map/stack | solution.py:89
  85.3 10.4 %all-to-all-done.2 = bf16[2,4,2,8,4096]{4,2,0,1,3:T(2,128)(2,1)S(1)} async-done(((bf16[2,4,2,8,4096]{4,2,0,1,3:T(2,128)(2,1)}), bf16[2,4,2,8,4096]{4,2,0,1,3:T(2,128)(2,1)S(1)}, u32[]{:S(2)}, u32[]{:S(2)}) %all-to-all-start.2) | async-done | bytes 1048608 | tf_op jit(solution)/shard_map/all_to_all | solution.py:98
  95.7 0.7 fusion.3
  96.4 1.3 copy.77
  97.7 4.2 %all-to-all-start.3 = ((bf16[2,4,8,4096]{3,0,1,2:T(2,128)(2,1)}), bf16[2,4,8,4096]{3,0,1,2:T(2,128)(2,1)}, u32[]{:S(2)}, u32[]{:S(2)}) async-start(bf16[2,4,8,4096]{3,0,1,2:T(2,128)(2,1)} %copy.77), calls=%async_computation.3 | async-start | bytes 1048576 | tf_op jit(solution)/shard_map/all_to_all | solution.py:108
  101.9 2.5 %fusion.21 = bf16[2,4,256,128]{3,2,1,0:T(8,128)(2,1)} fusion(f32[2,4,2,256,128]{4,3,2,1,0:T(8,128)} %bitcast.110, pred[]{:T(512)S(6)} %eq.10), kind=kLoop, calls=%fused_computation.42 | loop fusion | flops 262144 | bytes 1572865 | tf_op jit(solution)/shard_map/convert_element_type | solution.py:93
  104.3 0.4 collective-permute-start.1
  104.7 3.2 %convolution_convert_fusion.1 = bf16[4,256,128]{2,1,0:T(8,128)(2,1)} fusion(bf16[4,256,1024]{1,2,0:T(8,128)(2,1)} %copy-done.7, bf16[4,1024,128]{2,1,0:T(8,128)(2,1)S(1)} %copy-done.8), kind=kOutput, calls=%fused_computation.26 | convolution fusion | flops 268566528 | bytes 3407872 | tf_op jit(solution)/shard_map/htk,hkd->htd/dot_general | solution.py:80
  107.9 29.0 %all-reduce.2.cloned.1.call-done = bf16[256,2048]{1,0:T(8,128)(2,1)} async-done(((bf16[256,2048]{1,0:T(8,128)(2,1)}), bf16[256,2048]{1,0:T(8,128)(2,1)}) %all-reduce.2.cloned.1.call-update) | async-done | bytes 1048592 | tf_op jit(solution)/shard_map/psum | solution.py:63
  136.9 1.7 %convert_convert_fusion = bf16[256,512]{1,0:T(8,128)(2,1)} fusion(bf16[256,2048]{1,0:T(8,128)(2,1)} %all-reduce.2.cloned.1.call-done, s32[]{:T(128)S(6)} %select_n.37), kind=kLoop, calls=%fused_computation.49 | loop fusion | flops 262144 | bytes 524292 | tf_op jit(solution)/shard_map/convert_element_type | solution.py:66
  138.6 0.0 all-to-all-done.3
  138.6 2.3 %copy_convert_fusion = f32[2,4,8,4096]{3,2,1,0:T(8,128)} fusion(bf16[2,4,8,4096]{3,0,1,2:T(2,128)(2,1)} %all-to-all-done.3), kind=kLoop, calls=%fused_computation.48 | loop fusion | flops 262144 | bytes 1572864 | tf_op jit(solution)/shard_map/convert_element_type | solution.py:109
  140.9 1.4 reshape.55
  142.3 0.0 collective-permute-done.1
  142.3 1.9 %fusion.18 = bf16[2,4,256,128]{3,2,1,0:T(8,128)(2,1)S(1)} fusion(f32[2,4,256,128]{3,2,1,0:T(8,128)S(1)} %reshape.55, bf16[2,4,256,128]{3,2,1,0:T(8,128)(2,1)} %collective-permute-done.1, f32[2,4,2,256,128]{4,3,2,1,0:T(8,128)} %bitcast.111, pred[]{:T(512)S(6)} %eq.10), kind=kLoop, calls=%fused_computation.38 | loop fusion | flops 1310720 | bytes 4194305 | tf_op jit(solution)/shard_map/convert.3
  144.2 0.8 slice_bitcast_fusion.2
  (22 shorter events, 0.1 us)
Async XLA Ops:
  7.2 57.5 %copy-start = (bf16[4,128,2048]{2,1,0:T(8,128)(2,1)S(1)}, bf16[4,128,2048]{2,1,0:T(8,128)(2,1)}, u32[]{:S(2)}) copy-start(bf16[4,128,2048]{2,1,0:T(8,128)(2,1)} %param.10) | copy-start | bytes 6291460
  7.2 8.9 %copy-start.14 = (s32[4,4]{1,0:T(4,128)S(1)}, s32[4,4]{1,0:T(4,128)}, u32[]{:S(2)}) copy-start(s32[4,4]{1,0:T(4,128)} %param.9) | copy-start | bytes 196
  10.9 14.9 %all-to-all-start = ((bf16[2,4,8,4096]{3,0,1,2:T(2,128)(2,1)}), bf16[2,4,8,4096]{3,0,1,2:T(2,128)(2,1)S(1)}, u32[]{:S(2)}, u32[]{:S(2)}) async-start(bf16[2,4,8,4096]{3,0,1,2:T(2,128)(2,1)} %copy.60), calls=%async_computation | async-start | bytes 1048576 | tf_op jit(solution)/shard_map/all_to_all | solution.py:27
  26.3 6.4 %copy-start.10 = (bf16[4,256,128]{2,1,0:T(8,128)(2,1)S(1)}, bf16[4,256,128]{2,1,0:T(8,128)(2,1)}, u32[]{:S(2)}) copy-start(bf16[4,256,128]{2,1,0:T(8,128)(2,1)} %param.8) | copy-start | bytes 786436
  26.3 6.4 %copy-start.11 = (bf16[4,256,128]{2,1,0:T(8,128)(2,1)S(1)}, bf16[4,256,128]{2,1,0:T(8,128)(2,1)}, u32[]{:S(2)}) copy-start(bf16[4,256,128]{2,1,0:T(8,128)(2,1)} %param.7) | copy-start | bytes 786436
  28.4 19.7 %all-to-all-start.1 = ((bf16[2,4,2,8,4096]{4,2,0,1,3:T(2,128)(2,1)}), bf16[2,4,2,8,4096]{4,2,0,1,3:T(2,128)(2,1)}, u32[]{:S(2)}, u32[]{:S(2)}) async-start(bf16[2,4,2,8,4096]{4,2,0,1,3:T(2,128)(2,1)} %copy.65), calls=%async_computation.1 | async-start | bytes 2097152 | tf_op jit(solution)/shard_map/all_to_all | solution.py:37
  32.7 32.0 %all-gather.2.cloned.1.call-start = ((), (), s32[]{:S(2)}) async-start(), calls=%async_computation.5 | async-start | bytes 1310720 | tf_op jit(solution)/shard_map/all_gather | solution.py:67
  32.8 2.1 %collective-permute-start = (bf16[2,4,256,128]{3,2,1,0:T(8,128)(2,1)S(1)}, bf16[2,4,256,128]{3,2,1,0:T(8,128)(2,1)}, u32[]{:S(2)}, u32[]{:S(2)}) collective-permute-start(bf16[2,4,256,128]{3,2,1,0:T(8,128)(2,1)S(1)} %pad_maximum_fusion.2), channel_id=1, source_target_pairs={{0,4},{4,0},{8,12},{12,8},{16,20},{20,16},{24,28},{28,24},{1,5},{5... | collective-permute-start | bytes 1572872 | tf_op jit(solution)/shard_map/ppermute | solution.py:10
  53.2 2.2 %copy-start.12 = (bf16[4,256,128]{2,1,0:T(8,128)(2,1)S(1)}, bf16[4,256,128]{2,1,0:T(8,128)(2,1)}, u32[]{:S(2)}) copy-start(bf16[4,256,128]{2,1,0:T(8,128)(2,1)} %param.6) | copy-start | bytes 786436
  60.1 4.0 %copy-start.5 = (bf16[2,4,512,128]{3,2,1,0:T(8,128)(2,1)S(1)}, bf16[2,4,512,128]{3,2,1,0:T(8,128)(2,1)}, u32[]{:S(2)}) copy-start(bf16[2,4,512,128]{3,2,1,0:T(8,128)(2,1)} %reshape_reshape.3) | copy-start | bytes 3145732
  62.7 1.3 copy-start.3
  64.6 2.2 %copy-start.4 = (bf16[4,256,1024]{1,2,0:T(8,128)(2,1)S(1)}, bf16[4,256,1024]{1,2,0:T(8,128)(2,1)}, u32[]{:S(2)}) copy-start(bf16[4,256,1024]{1,2,0:T(8,128)(2,1)} %copy-done.3) | copy-start | bytes 6291460
  64.6 3.1 %copy-start.9 = (f32[4,256,1024]{1,2,0:T(8,128)S(1)}, f32[4,256,1024]{1,2,0:T(8,128)}, u32[]{:S(2)}) copy-start(f32[4,256,1024]{1,2,0:T(8,128)} %get-tuple-element.7) | copy-start | bytes 12582916
  66.8 1.5 copy-start.6
  67.5 2.4 %copy-start.1 = (f32[1,4,1024,128]{3,2,1,0:T(8,128)}, f32[1,4,1024,128]{3,2,1,0:T(8,128)S(1)}, u32[]{:S(2)}) copy-start(f32[1,4,1024,128]{3,2,1,0:T(8,128)S(1)} %convolution_bitcast_fusion.2) | copy-start | bytes 6291460
  68.3 0.9 copy-start.13
  69.2 1.3 copy-start.7
  70.5 1.4 copy-start.2
  76.6 19.1 %all-to-all-start.2 = ((bf16[2,4,2,8,4096]{4,2,0,1,3:T(2,128)(2,1)}), bf16[2,4,2,8,4096]{4,2,0,1,3:T(2,128)(2,1)S(1)}, u32[]{:S(2)}, u32[]{:S(2)}) async-start(bf16[2,4,2,8,4096]{4,2,0,1,3:T(2,128)(2,1)} %copy.75), calls=%async_computation.2 | async-start | bytes 2097152 | tf_op jit(solution)/shard_map/all_to_all | solution.py:98
  80.3 56.6 %all-reduce.2.cloned.1.call-start = ((), (), s32[]{:S(2)}) async-start(), calls=%async_computation.4 | async-start | bytes 2097152 | tf_op jit(solution)/shard_map/psum | solution.py:63
  96.4 8.3 %copy-start.8 = (bf16[4,1024,128]{2,1,0:T(8,128)(2,1)S(1)}, bf16[4,1024,128]{2,1,0:T(8,128)(2,1)}, u32[]{:S(2)}) copy-start(bf16[4,1024,128]{2,1,0:T(8,128)(2,1)} %fusion.15) | copy-start | bytes 3145732
  97.7 40.8 %all-to-all-start.3 = ((bf16[2,4,8,4096]{3,0,1,2:T(2,128)(2,1)}), bf16[2,4,8,4096]{3,0,1,2:T(2,128)(2,1)}, u32[]{:S(2)}, u32[]{:S(2)}) async-start(bf16[2,4,8,4096]{3,0,1,2:T(2,128)(2,1)} %copy.77), calls=%async_computation.3 | async-start | bytes 1048576 | tf_op jit(solution)/shard_map/all_to_all | solution.py:108
  104.3 37.9 %collective-permute-start.1 = (bf16[2,4,256,128]{3,2,1,0:T(8,128)(2,1)}, bf16[2,4,256,128]{3,2,1,0:T(8,128)(2,1)}, u32[]{:S(2)}, u32[]{:S(2)}) collective-permute-start(bf16[2,4,256,128]{3,2,1,0:T(8,128)(2,1)} %fusion.21), channel_id=1, source_target_pairs={{0,4},{4,0},{8,12},{12,8},{16,20},{20,16},{24,28},{28,24},{1,5},{5... | collective-permute-start | bytes 1572872 | tf_op jit(solution)/shard_map/ppermute | solution.py:10
Sparse Core Ops, SparseCore 0:
  35.1 29.5 all-gather.1
  83.5 53.3 all-reduce.1
where the time goes:
time: 153 us; the launch traced here: 152 us
  waiting for transfers between devices  62.2 us (41%)
  local copies, waits for them, and re-layouts  23.4 us (15%)
  other arithmetic  18.2 us (12%)
  starting transfers between devices  18.2 us (12%)
  matrix products  15.6 us (10%)
  between operations  14.3 us (9%)
    psum x1, waiting for transfers between devices, per_device(): lax.psum(partial_out.astype(jnp.bfloat16), 'head').astype(jnp.float32)  29 us
    all_to_all x1, waiting for transfers between devices, per_device(): lax.all_to_all(picked, 'seq', split_axis=3, concat_axis=3, tiled=True)  11.5 us
    all_to_all x1, waiting for transfers between devices, per_device(): lax.all_to_all(partner_grad.reshape(2, group_heads, slot_count, devices,...  10.4 us
    all_to_all x1, waiting for transfers between devices, per_device(): lax.all_to_all(stacked.reshape(2, group_heads, devices, portion), 'seq',...  9.53 us
    all_to_all x1, starting transfers between devices, per_device(): lax.all_to_all(stacked.reshape(2, group_heads, devices, portion), 'seq',...  5.17 us
    sub x1, matrix products, per_device(): weights = jnp.exp(logit_scores - row_max)  4.61 us
    convert_element_type x2, local copies, waits for them, and re-layouts, per_device(): partner_grad = partner_grad.astype(jnp.bfloat16)  4.59 us
    all_to_all x1, starting transfers between devices, per_device(): lax.all_to_all(picked, 'seq', split_axis=3, concat_axis=3, tiled=True)  4.24 us
  transfers between devices with their start and end apart: 8, of which 5 were waited for; matrix products, arithmetic and copies ran while one was open for 23% of the time, Pallas kernels for 0%

commit v1 on v0

--- a/solution.py
+++ b/solution.py
@@ -1,16 +1,266 @@
+import functools
 import math
 
 import jax
 import jax.numpy as jnp
 from jax import lax
+from jax.experimental import pallas as pl
+from jax.experimental.pallas import tpu as pltpu
 from jax.sharding import PartitionSpec as P
+
+F32 = jnp.float32
+LOW = jnp.bfloat16
+NT = (((1,), (1,)), ((), ()))
+NN = (((1,), (0,)), ((), ()))
+TN = (((0,), (0,)), ((), ()))
+
+
+def dot(a, b, dims=NN):
+    return lax.dot_general(a, b, dims, preferred_element_type=F32)
+
+
+def chip_index():
+    return lax.axis_index("seq") // 2
+
+
+def call(body, outs, *args, flops=0, moved=0, scratch=(), smem=()):
+    vmem = pl.BlockSpec(memory_space=pltpu.VMEM)
+    scalar = pl.BlockSpec(memory_space=pltpu.SMEM)
+    return pl.pallas_call(
+        body,
+        out_shape=outs,
+        in_specs=[scalar if i in smem else vmem for i in range(len(args))],
+        out_specs=jax.tree.map(lambda _: vmem, outs),
+        scratch_shapes=list(scratch),
+        cost_estimate=pl.CostEstimate(flops=flops, bytes_accessed=moved, transcendentals=0),
+        compiler_params=pltpu.CompilerParams(vmem_limit_bytes=48 * 1024 * 1024),
+    )(*args)
+
+
+def attend_body(chips, rows, scale, perm, *refs):
+    pieces, siblings = refs[:chips], refs[chips : 2 * chips]
+    attended, probs, keys_values, queries = refs[2 * chips :]
+    chip = chip_index()
+    for d in range(chips):
+        for kind in range(2):
+            keys_values[d, kind, :rows] = pieces[d][kind]
+            keys_values[d, kind, rows:] = siblings[d][kind]
+        queries[d] = pieces[d][2]
+    for d in range(chips):
+        p = perm[chip, chip ^ d] ^ chip
+        query = pieces[d][2]
+        local = dot(query, keys_values[d, 0], NT)
+        remote = dot(query, keys_values[p, 0], NT)
+        top = jnp.maximum(
+            jnp.max(local, axis=1, keepdims=True), jnp.max(remote, axis=1, keepdims=True)
+        )
+        factor = scale * math.log2(math.e)
+        local = jnp.exp2((local - top) * factor)
+        remote = jnp.exp2((remote - top) * factor)
+        total = jnp.sum(local, axis=1, keepdims=True) + jnp.sum(remote, axis=1, keepdims=True)
+        share = 1.0 / total
+        local = (local * share).astype(LOW)
+        remote = (remote * share).astype(LOW)
+        probs[d, :, : 2 * rows] = local
+        probs[d, :, 2 * rows :] = remote
+        result = dot(local, keys_values[d, 1]) + dot(remote, keys_values[p, 1])
+        attended[d] = result.astype(LOW)
+
+
+def backward_body(chips, rows, scale, perm, *refs):
+    arrived = refs[:chips]
+    attended, probs, keys_values, queries = refs[chips : chips + 4]
+    query_grad, own_part, sibling_part, score_grad, grads = refs[chips + 4 :]
+    chip = chip_index()
+    for d in range(chips):
+        p = perm[chip, chip ^ d] ^ chip
+        grad = arrived[d][...]
+        grads[d] = grad
+        delta = jnp.sum(grad.astype(F32) * attended[d].astype(F32), axis=1, keepdims=True)
+        total = None
+        for part, source in ((0, d), (1, p)):
+            lanes = slice(2 * rows * part, 2 * rows * (part + 1))
+            prob_grad = dot(grad, keys_values[source, 1], NT)
+            weight = probs[d, :, lanes].astype(F32)
+            change = (weight * (prob_grad - delta) * scale).astype(LOW)
+            score_grad[part, d] = change
+            term = dot(change, keys_values[source, 0])
+            total = term if total is None else total + term
+        query_grad[d] = total.astype(LOW)
+    for d in range(chips):
+        asker = jnp.int32(0)
+        for i in range(chips):
+            asker = jnp.where(perm[chip, i] == chip ^ d, i, asker)
+        asker = asker ^ chip
+        for half, out in ((0, own_part), (1, sibling_part)):
+            near = slice(half * rows, (half + 1) * rows)
+            far = slice((half + 2) * rows, (half + 3) * rows)
+            key_part = dot(score_grad[0, d, :, near], queries[d], TN)
+            key_part += dot(score_grad[1, asker, :, near], queries[asker], TN)
+            value_part = dot(probs[d, :, near], grads[d], TN)
+            value_part += dot(probs[asker, :, far], grads[asker], TN)
+            out[d, 0] = key_part.astype(out.dtype)
+            out[d, 1] = value_part.astype(out.dtype)
+
+
+def project_body(chips, weight, *refs):
+    attended, out, joined = refs[:chips], refs[chips], refs[chips + 1]
+    chip = chip_index()
+    width = attended[0].shape[1]
+    for d in range(chips):
+        lanes = pl.ds(pl.multiple_of((chip ^ d) * width, width), width)
+        joined[:, lanes] = attended[d][...]
+    columns = out.shape[2]
+    rows = joined[...]
+    flat = weight.reshape(chips * width, weight.shape[2])
+    for s in range(out.shape[0]):
+        out[s] = dot(rows, flat[:, s * columns : (s + 1) * columns]).astype(out.dtype)
+
+
+def grad_body(chips, weight, cotangent, out):
+    chip = chip_index()
+    width = out.shape[2]
+    columns = cotangent.shape[2]
+    flat = weight.reshape(chips * width, weight.shape[2])
+    total = None
+    for s in range(cotangent.shape[0]):
+        term = dot(cotangent[s], flat[:, s * columns : (s + 1) * columns], NT)
+        total = term if total is None else total + term
+    for h in range(chips):
+        out[h ^ chip] = total[:, h * width : (h + 1) * width].astype(out.dtype)
+
+
+def merge_body(chips, query_grad, own_part, arrived, *outs):
+    for d in range(chips):
+        outs[d][0] = query_grad[d]
+        for kind in range(2):
+            both = own_part[d, kind] + arrived[d, kind].astype(F32)
+            outs[d][1 + kind] = both.astype(LOW)
+
+
+def place_body(chips, *refs):
+    pieces, outs = refs[:chips], refs[chips:]
+    chip = chip_index()
+    for d in range(chips):
+        for kind in range(3):
+            outs[kind][chip ^ d] = pieces[d][kind]
+
+
+def by_heads(queries, key_vectors, value_vectors, block_perm, out_weight, out_cotangent):
+    devices = lax.axis_size("seq")
+    chips = devices // 2
+    groups = lax.axis_size("head")
+    heads, rows, width = queries.shape
+    features = out_weight.shape[2]
+    columns = out_cotangent.shape[1]
+    scale = 1.0 / math.sqrt(width)
+    chip = chip_index()
+    shape = jax.ShapeDtypeStruct
+
+    def to_chip(array, d):
+        return lax.ppermute(array, "seq", [(i, i ^ (2 * d)) for i in range(devices)])
+
+    def to_sibling(array):
+        return lax.ppermute(array, "seq", [(i, i ^ 1) for i in range(devices)])
+
+    def exchange(pieces):
+        return [pieces[0]] + [to_chip(pieces[d], d) for d in range(1, chips)]
+
+    def head_piece(d):
+        h = chip ^ d
+        return jnp.stack(
+            [
+                lax.dynamic_index_in_dim(a, h, 0, keepdims=False)
+                for a in (key_vectors, value_vectors, queries)
+            ]
+        )
+
+    gathered = lax.all_gather(out_cotangent, "head", axis=0, tiled=False)
+    pieces = exchange([head_piece(d) for d in range(chips)])
+    siblings = [to_sibling(piece[:2]) for piece in pieces]
+    tile = rows * width
+    scores = chips * rows * 4 * rows
+    attended, probs, keys_values, query_rows = call(
+        functools.partial(attend_body, chips, rows, scale),
+        (
+            shape((chips, rows, width), LOW),
+            shape((chips, rows, 4 * rows), LOW),
+            shape((chips, 2, 2 * rows, width), LOW),
+            shape((chips, rows, width), LOW),
+        ),
+        block_perm,
+        *pieces,
+        *siblings,
+        flops=4 * scores * width,
+        moved=2 * (scores + 14 * chips * tile),
+        smem=(0,),
+    )
+    weight_bytes = 2 * heads * width * features
+    grad_att = call(
+        functools.partial(grad_body, chips),
+        shape((chips, rows, width), LOW),
+        out_weight,
+        gathered,
+        flops=2 * rows * heads * width * features,
+        moved=weight_bytes + 2 * rows * features + 2 * chips * tile,
+    )
+    grads = exchange([grad_att[d] for d in range(chips)])
+    own_attended = exchange([attended[d] for d in range(chips)])
+    partial_out = call(
+        functools.partial(project_body, chips),
+        shape((groups, rows, columns), LOW),
+        out_weight,
+        *own_attended,
+        flops=2 * rows * heads * width * features,
+        moved=weight_bytes + 2 * rows * features + 2 * chips * tile,
+        scratch=[pltpu.VMEM((rows, heads * width), LOW)],
+    )
+    projected = lax.psum_scatter(partial_out, "head", scatter_dimension=0, tiled=False)
+    query_grad, own_part, sibling_part = call(
+        functools.partial(backward_body, chips, rows, scale),
+        (
+            shape((chips, rows, width), LOW),
+            shape((chips, 2, rows, width), F32),
+            shape((chips, 2, rows, width), LOW),
+        ),
+        block_perm,
+        *grads,
+        attended,
+        probs,
+        keys_values,
+        query_rows,
+        flops=8 * scores * width,
+        moved=2 * (scores + 20 * chips * tile),
+        scratch=[
+            pltpu.VMEM((2, chips, rows, 2 * rows), LOW),
+            pltpu.VMEM((chips, rows, width), LOW),
+        ],
+        smem=(0,),
+    )
+    returned = exchange(
+        call(
+            functools.partial(merge_body, chips),
+            tuple(shape((3, rows, width), LOW) for _ in range(chips)),
+            query_grad,
+            own_part,
+            to_sibling(sibling_part),
+            moved=2 * 14 * chips * tile,
+        )
+    )
+    gradients = call(
+        functools.partial(place_body, chips),
+        tuple(shape((heads, rows, width), LOW) for _ in range(3)),
+        *returned,
+        moved=2 * 6 * chips * tile,
+    )
+    return (projected, *gradients)
 
 
 def partner(shard, axis, bit):
     return lax.ppermute(shard, axis, [(i, i ^ 1 << bit) for i in range(lax.axis_size(axis))])
 
 
-def per_device(queries, key_vectors, value_vectors, block_perm, out_weight, out_cotangent):
+def by_routing(queries, key_vectors, value_vectors, block_perm, out_weight, out_cotangent):
     devices = lax.axis_size("seq")
     position = lax.axis_index("seq")
     parity = position % 2
@@ -114,6 +364,12 @@
     return (projected, gradient_of_queries, key_grad, value_grad)
 
 
+def per_device(*arrays):
+    chips = lax.axis_size("seq") // 2
+    square = chips == arrays[0].shape[0] and chips & (chips - 1) == 0
+    return (by_heads if square else by_routing)(*arrays)
+
+
 def solution(mesh):
     return jax.shard_map(
         per_device,

time: 153 us -> 76.9 us (0.50)
  waiting for transfers between devices: 62.2 us -> 31.6 us
  local copies, waits for them, and re-layouts: 23.4 us -> 4.72 us
  other arithmetic: 18.2 us -> 0.12 us
  matrix products: 15.6 us -> 0 us
  Pallas kernels: 0 us -> 10.2 us
  starting transfers between devices: 18.2 us -> 15.8 us
    all_to_all x4 -> x0, waiting for transfers between devices: 31.5 us -> none  [the longest x1 11.5 us: per_device(): lax.all_to_all(picked, 'seq', split_axis=3, concat_axis=3, tiled=True)]
    psum x1 -> x0, waiting for transfers between devices: 29 us -> none  [per_device(): lax.psum(partial_out.astype(jnp.bfloat16), 'head').astype(jnp.float32)]
    ppermute x2 -> x17, waiting for transfers between devices: 1.49 us -> 27.8 us  [the longest x12 24.6 us: to_chip(): return lax.ppermute(array, 'seq', [(i, i ^ 2 * d) for i in range(devices)])]
    all_to_all x4 -> x0, starting transfers between devices: 17.2 us -> none  [the longest x1 5.17 us: per_device(): lax.all_to_all(stacked.reshape(2, group_heads, devices, portion), 'seq',...]
    ppermute x2 -> x17, starting transfers between devices: 0.75 us -> 15.7 us  [the longest x12 15.3 us: to_chip(): return lax.ppermute(array, 'seq', [(i, i ^ 2 * d) for i in range(devices)])]
    dot_general x9 -> x0, matrix products: 11 us -> none  [the longest x1 3.16 us: per_device(): jnp.einsum('htk,hkd->htd', score_gradient, key_all, preferred_element_typ...]
    convert_element_type x6 -> x0, local copies, waits for them, and re-layouts: 10.2 us -> none  [the longest x2 4.59 us: per_device(): partner_grad = partner_grad.astype(jnp.bfloat16)]
    pallas_call x0 -> x6, Pallas kernels: none -> 10.2 us  [call(): pl.pallas_call(body, out_shape=outs, in_specs=[scalar if i in smem else v...]
  transfers between devices with their start and end apart: 8 -> 19, of which waited for: 5 -> 16; matrix products, arithmetic and copies ran while one was open for 23% -> 3% of each run, Pallas kernels for 0% -> 13%
where the time goes in v1:
time: 76.9 us; the launch traced here: 76.6 us
  waiting for transfers between devices  31.6 us (41%)
  starting transfers between devices  15.8 us (21%)
  between operations  14.3 us (19%)
  Pallas kernels  10.2 us (13%)
  local copies, waits for them, and re-layouts  4.72 us (6%)
    ppermute x12, waiting for transfers between devices, to_chip(): return lax.ppermute(array, 'seq', [(i, i ^ 2 * d) for i in range(devices)])  24.6 us
    ppermute x12, starting transfers between devices, to_chip(): return lax.ppermute(array, 'seq', [(i, i ^ 2 * d) for i in range(devices)])  15.3 us
    pallas_call x6, Pallas kernels, call(): pl.pallas_call(body, out_shape=outs, in_specs=[scalar if i in smem else v...  10.2 us
    ppermute x5, waiting for transfers between devices, to_sibling(): return lax.ppermute(array, 'seq', [(i, i ^ 1) for i in range(devices)])  3.17 us
    unnamed x14, local copies, waits for them, and re-layouts  2.58 us
    dynamic_slice x2, local copies, waits for them, and re-layouts, head_piece(): lax.dynamic_index_in_dim(a, h, 0, keepdims=False)  2.07 us
    reduce_scatter x1, waiting for transfers between devices, by_heads(): lax.psum_scatter(partial_out, 'head', scatter_dimension=0, tiled=False)  1.63 us
  transfers between devices with their start and end apart: 19, of which 16 were waited for; matrix products, arithmetic and copies ran while one was open for 3% of the time, Pallas kernels for 13%

profile of v1, /device:TPU:0, one launch (start us, length us, event | category | flops | bytes accessed | tf_op | source)
XLA Modules:
  0.0 76.6 jit_solution(2276529153431754720)
XLA Ops:
  7.2 0.0 all-gather.3.cloned.1.call-start
  7.2 0.7 all-gather.3.cloned.1.call-update
  7.9 0.0 reduce-scatter.2.cloned.1.call-start
  8.0 0.0 copy-start.2
  8.0 1.0 %constant_dynamic-slice_fusion.2 = (bf16[1,256,128]{2,1,0:T(8,128)(2,1)S(1)}, bf16[1,256,128]{2,1,0:T(8,128)(2,1)S(1)}, bf16[1,256,128]{2,1,0:T(8,128)(2,1)S(1)}, bf16[1,256,128]{2,1,0:T(8,128)(2,1)S(1)}) fusion(bf16[4,256,128]{2,1,0:T(8,128)(2,1)} %param.7, s32[]{:T(128)S(6)} %select_n.30, s32[]{:T(128)S(6)} %select_n.28, s32[]{:T(128)S(6)} %select_n.27, ...), kind=kLoop, calls=%fused_computation.15 | loop fusion | bytes 524304 | tf_op jit(solution)/shard_map/jit(dynamic_index_in_dim)/dynamic_slice | solution.py:173
  9.0 1.1 %constant_dynamic-slice_fusion = (bf16[1,256,128]{2,1,0:T(8,128)(2,1)S(1)}, bf16[1,256,128]{2,1,0:T(8,128)(2,1)S(1)}, bf16[1,256,128]{2,1,0:T(8,128)(2,1)S(1)}, ...) fusion(bf16[4,256,128]{2,1,0:T(8,128)(2,1)} %param.6, ...), kind=kLoop, calls=%fused_computation.13 | loop fusion | bytes 1048592 | tf_op jit(solution)/shard_map/jit(dynamic_index_in_dim)/dynamic_slice | solution.py:173
  10.1 3.0 %collective-permute-start.1 = (bf16[3,256,128]{2,1,0:T(8,128)(2,1)S(1)}, bf16[3,256,128]{2,1,0:T(8,128)(2,1)S(1)}, u32[]{:S(2)}, u32[]{:S(2)}) collective-permute-start(bf16[3,256,128]{2,1,0:T(8,128)(2,1)S(1)} %pad_maximum_fusion.2), channel_id=1, source_target_pairs={{0,16},{4,20},{8,24},{12,28},{16,0},{20,4},{24,8},{28,12},{1,17},{... | collective-permute-start | bytes 589832 | tf_op jit(solution)/shard_map/ppermute | solution.py:161
  13.2 1.6 %collective-permute-start = (bf16[3,256,128]{2,1,0:T(8,128)(2,1)S(1)}, bf16[3,256,128]{2,1,0:T(8,128)(2,1)S(1)}, u32[]{:S(2)}, u32[]{:S(2)}) collective-permute-start(bf16[3,256,128]{2,1,0:T(8,128)(2,1)S(1)} %pad_maximum_fusion.1), channel_id=1, source_target_pairs={{0,8},{4,12},{8,0},{12,4},{16,24},{20,28},{24,16},{28,20},{1,9},{5... | collective-permute-start | bytes 589832 | tf_op jit(solution)/shard_map/ppermute | solution.py:161
  14.7 0.0 copy-start
  14.8 0.1 collective-permute-start.2
  14.9 0.1 collective-permute-start.3
  14.9 3.1 %collective-permute-done.1.refs_2_ = bf16[3,256,128]{2,1,0:T(8,128)(2,1)S(1)} collective-permute-done((bf16[3,256,128]{2,1,0:T(8,128)(2,1)S(1)}, bf16[3,256,128]{2,1,0:T(8,128)(2,1)S(1)}, u32[]{:S(2)}, u32[]{:S(2)}) %collective-permute-start.1) | collective-permute-done | bytes 196640 | tf_op jit(solution)/shard_map/ppermute | solution.py:161
  18.1 0.1 collective-permute-start.5
  18.1 2.9 %collective-permute-done.refs_1_ = bf16[3,256,128]{2,1,0:T(8,128)(2,1)S(1)} collective-permute-done((bf16[3,256,128]{2,1,0:T(8,128)(2,1)S(1)}, bf16[3,256,128]{2,1,0:T(8,128)(2,1)S(1)}, u32[]{:S(2)}, u32[]{:S(2)}) %collective-permute-start) | collective-permute-done | bytes 196640 | tf_op jit(solution)/shard_map/ppermute | solution.py:161
  21.1 0.1 collective-permute-start.4
  21.1 2.4 %collective-permute-done.2.refs_3_ = bf16[3,256,128]{2,1,0:T(8,128)(2,1)S(1)} collective-permute-done((bf16[3,256,128]{2,1,0:T(8,128)(2,1)S(1)}, bf16[3,256,128]{2,1,0:T(8,128)(2,1)S(1)}, u32[]{:S(2)}, u32[]{:S(2)}) %collective-permute-start.2) | collective-permute-done | bytes 196640 | tf_op jit(solution)/shard_map/ppermute | solution.py:161
  23.6 0.1 collective-permute-start.6
  23.7 0.0 collective-permute-done.3.refs_4_
  23.7 0.0 collective-permute-done.5.refs_6_
  23.7 0.0 collective-permute-done.4.refs_5_
  23.7 1.3 %collective-permute-done.6.refs_7_ = bf16[2,256,128]{2,1,0:T(8,128)(2,1)S(1)} collective-permute-done((bf16[2,256,128]{2,1,0:T(8,128)(2,1)S(1)}, bf16[2,256,128]{2,1,0:T(8,128)(2,1)S(1)}, u32[]{:S(2)}, u32[]{:S(2)}) %collective-permute-start.6) | collective-permute-done | bytes 131104 | tf_op jit(solution)/shard_map/ppermute | solution.py:164
  25.0 0.0 copy-done.2
  25.0 3.2 %shard_map.93 = (bf16[4,256,128]{2,1,0:T(8,128)(2,1)S(1)}, bf16[4,256,1024]{2,1,0:T(8,128)(2,1)S(1)}, bf16[4,2,512,128]{3,2,1,0:T(8,128)(2,1)S(1)}, bf16[4,256,128]{2,1,0:T(8,128)(2,1)S(1)}) custom-call(s32[4,4]{1,0:T(4,128)S(1)} %copy-done.2, bf16[3,256,128]{2,1,0:T(8,128)(2,1)S(1)} %pad_maximum_fusion.refs_0_, ...), custom_call_target="tpu_custom_call" | custom-call | flops 536870912 | bytes 5767168 | tf_op jit(solution)/shard_map/pallas_call | solution.py:29
  28.2 0.0 copy-start.3
  28.2 1.3 %copy-done.3 = bf16[4,256,1024]{2,1,0:T(8,128)(2,1)} copy-done((bf16[4,256,1024]{2,1,0:T(8,128)(2,1)}, bf16[4,256,1024]{2,1,0:T(8,128)(2,1)S(1)}, u32[]{:S(2)}) %copy-start.3) | copy-done | bytes 2097176
  29.5 0.0 copy-start.5
  29.5 2.7 %collective-permute-start.9 = (bf16[256,128]{1,0:T(8,128)(2,1)S(1)}, bf16[256,128]{1,0:T(8,128)(2,1)S(1)}, u32[]{:S(2)}, u32[]{:S(2)}) collective-permute-start(bf16[256,128]{1,0:T(8,128)(2,1)S(1)} %get-tuple-element.36), channel_id=1, source_target_pairs={{0,24},{4,28},{8,16},{12,20},{16,8},{20,12},{24,0},{28,4},{1,25},{... | collective-permute-start | bytes 196616 | tf_op jit(solution)/shard_map/ppermute | solution.py:161
  32.3 0.5 collective-permute-start.8
  32.8 0.3 collective-permute-start.7
  33.1 1.7 %collective-permute-done.9.refs_3_ = bf16[256,128]{1,0:T(8,128)(2,1)S(1)} collective-permute-done((bf16[256,128]{1,0:T(8,128)(2,1)S(1)}, bf16[256,128]{1,0:T(8,128)(2,1)S(1)}, u32[]{:S(2)}, u32[]{:S(2)}) %collective-permute-start.9) | collective-permute-done | bytes 65568 | tf_op jit(solution)/shard_map/ppermute | solution.py:161
  34.8 1.8 %collective-permute-done.8.refs_2_ = bf16[256,128]{1,0:T(8,128)(2,1)S(1)} collective-permute-done((bf16[256,128]{1,0:T(8,128)(2,1)S(1)}, bf16[256,128]{1,0:T(8,128)(2,1)S(1)}, u32[]{:S(2)}, u32[]{:S(2)}) %collective-permute-start.8) | collective-permute-done | bytes 65568 | tf_op jit(solution)/shard_map/ppermute | solution.py:161
  36.5 0.5 collective-permute-done.7.refs_1_
  37.0 0.0 copy-done.5
  37.0 0.0 copy-done
  37.0 1.7 %shard_map.94 = bf16[4,256,512]{2,1,0:T(8,128)(2,1)} custom-call(bf16[4,128,2048]{2,1,0:T(8,128)(2,1)S(1)} %copy-done, bf16[256,128]{1,0:T(8,128)(2,1)S(1)} %get-tuple-element.39.refs_0_, bf16[256,128]{1,0:T(8,128)(2,1)S(1)} %collective-permute-done.7.refs_1_, bf16[256,128]{1,0:T(8,128)(2,1)S(1)} %collective-permute-done.8.refs_2_, ...), custom_call_target="tpu_custom_call" | custom-call | flops 536870912 | bytes 3407872 | tf_op jit(solution)/shard_map/pallas_call | solution.py:29
  38.8 0.0 reduce-scatter.2.cloned.1.call-update
  38.8 1.5 %all-gather.3.cloned.1.call-done = bf16[1024,512]{1,0:T(8,128)(2,1)} async-done(((bf16[256,512]{1,0:T(8,128)(2,1)}), bf16[1024,512]{1,0:T(8,128)(2,1)}) %all-gather.3.cloned.1.call-update) | async-done | bytes 1048592 | tf_op jit(solution)/shard_map/all_gather | solution.py:178
  40.2 0.0 copy-start.1
  40.2 1.2 %copy-done.1 = bf16[1024,512]{1,0:T(8,128)(2,1)S(1)} copy-done((bf16[1024,512]{1,0:T(8,128)(2,1)S(1)}, bf16[1024,512]{1,0:T(8,128)(2,1)}, u32[]{:S(2)}) %copy-start.1) | copy-done | bytes 1048600
  41.5 0.0 copy-start.4
  41.5 0.0 copy-start.6
  41.5 0.7 shard_map.95
  42.2 2.4 %collective-permute-start.12 = (bf16[256,128]{1,0:T(8,128)(2,1)S(1)}, bf16[256,128]{1,0:T(8,128)(2,1)S(1)}, u32[]{:S(2)}, u32[]{:S(2)}) collective-permute-start(bf16[256,128]{1,0:T(8,128)(2,1)S(1)} %get-tuple-element.32), channel_id=1, source_target_pairs={{0,24},{4,28},{8,16},{12,20},{16,8},{20,12},{24,0},{28,4},{1,25},{... | collective-permute-start | bytes 196616 | tf_op jit(solution)/shard_map/ppermute | solution.py:161
  44.7 0.5 collective-permute-start.11
  45.2 0.6 collective-permute-start.10
  45.8 1.8 %collective-permute-done.12.refs_3_ = bf16[256,128]{1,0:T(8,128)(2,1)S(1)} collective-permute-done((bf16[256,128]{1,0:T(8,128)(2,1)S(1)}, bf16[256,128]{1,0:T(8,128)(2,1)S(1)}, u32[]{:S(2)}, u32[]{:S(2)}) %collective-permute-start.12) | collective-permute-done | bytes 65568 | tf_op jit(solution)/shard_map/ppermute | solution.py:161
  47.6 1.4 %collective-permute-done.11.refs_2_ = bf16[256,128]{1,0:T(8,128)(2,1)S(1)} collective-permute-done((bf16[256,128]{1,0:T(8,128)(2,1)S(1)}, bf16[256,128]{1,0:T(8,128)(2,1)S(1)}, u32[]{:S(2)}, u32[]{:S(2)}) %collective-permute-start.11) | collective-permute-done | bytes 65568 | tf_op jit(solution)/shard_map/ppermute | solution.py:161
  49.0 0.5 collective-permute-done.10.refs_1_
  49.5 0.0 copy-done.4
  49.5 0.0 copy-done.6
  49.5 3.4 %shard_map.96 = (bf16[4,256,128]{2,1,0:T(8,128)(2,1)S(1)}, f32[4,2,256,128]{3,2,1,0:T(8,128)S(1)}, bf16[4,2,256,128]{3,2,1,0:T(8,128)(2,1)S(1)}) custom-call(s32[4,4]{1,0:T(4,128)S(1)} %copy-done.2, bf16[256,128]{1,0:T(8,128)(2,1)S(1)} %get-tuple-element.35.refs_0_, bf16[256,128]{1,0:T(8,128)(2,1)S(1)} %collective-permute-done.10.refs_1_, ...), custom_call_target="tpu_custom_call" | custom-call | flops 1073741824 | bytes 7340032 | tf_op jit(solution)/shard_map/pallas_call | solution.py:29
  53.0 0.1 collective-permute-start.13
  53.0 1.9 %collective-permute-done.13.arrived = bf16[4,2,256,128]{3,2,1,0:T(8,128)(2,1)S(1)} collective-permute-done((bf16[4,2,256,128]{3,2,1,0:T(8,128)(2,1)S(1)}, bf16[4,2,256,128]{3,2,1,0:T(8,128)(2,1)S(1)}, u32[]{:S(2)}, u32[]{:S(2)}) %collective-permute-start.13) | collective-permute-done | bytes 524320 | tf_op jit(solution)/shard_map/ppermute | solution.py:164
  54.9 0.1 shard_map.97
  55.1 0.6 collective-permute-start.14
  55.7 1.5 %collective-permute-start.15 = (bf16[3,256,128]{2,1,0:T(8,128)(2,1)S(1)}, bf16[3,256,128]{2,1,0:T(8,128)(2,1)S(1)}, u32[]{:S(2)}, u32[]{:S(2)}) collective-permute-start(bf16[3,256,128]{2,1,0:T(8,128)(2,1)S(1)} %get-tuple-element.27), channel_id=1, source_target_pairs={{0,16},{4,20},{8,24},{12,28},{16,0},{20,4},{24,8},{28,12},{1,17},{... | collective-permute-start | bytes 589832 | tf_op jit(solution)/shard_map/ppermute | solution.py:161
  57.2 1.5 %collective-permute-start.16 = (bf16[3,256,128]{2,1,0:T(8,128)(2,1)S(1)}, bf16[3,256,128]{2,1,0:T(8,128)(2,1)S(1)}, u32[]{:S(2)}, u32[]{:S(2)}) collective-permute-start(bf16[3,256,128]{2,1,0:T(8,128)(2,1)S(1)} %get-tuple-element.28), channel_id=1, source_target_pairs={{0,24},{4,28},{8,16},{12,20},{16,8},{20,12},{24,0},{28,4},{1,25},{... | collective-permute-start | bytes 589832 | tf_op jit(solution)/shard_map/ppermute | solution.py:161
  58.6 4.3 %collective-permute-done.14.refs_1_ = bf16[3,256,128]{2,1,0:T(8,128)(2,1)S(1)} collective-permute-done((bf16[3,256,128]{2,1,0:T(8,128)(2,1)S(1)}, bf16[3,256,128]{2,1,0:T(8,128)(2,1)S(1)}, u32[]{:S(2)}, u32[]{:S(2)}) %collective-permute-start.14) | collective-permute-done | bytes 196640 | tf_op jit(solution)/shard_map/ppermute | solution.py:161
  62.9 2.7 %collective-permute-done.15.refs_2_ = bf16[3,256,128]{2,1,0:T(8,128)(2,1)S(1)} collective-permute-done((bf16[3,256,128]{2,1,0:T(8,128)(2,1)S(1)}, bf16[3,256,128]{2,1,0:T(8,128)(2,1)S(1)}, u32[]{:S(2)}, u32[]{:S(2)}) %collective-permute-start.15) | collective-permute-done | bytes 196640 | tf_op jit(solution)/shard_map/ppermute | solution.py:161
  65.6 1.6 %collective-permute-done.16.refs_3_ = bf16[3,256,128]{2,1,0:T(8,128)(2,1)S(1)} collective-permute-done((bf16[3,256,128]{2,1,0:T(8,128)(2,1)S(1)}, bf16[3,256,128]{2,1,0:T(8,128)(2,1)S(1)}, u32[]{:S(2)}, u32[]{:S(2)}) %collective-permute-start.16) | collective-permute-done | bytes 196640 | tf_op jit(solution)/shard_map/ppermute | solution.py:161
  67.2 0.9 %shard_map.98 = (bf16[4,256,128]{2,1,0:T(8,128)(2,1)}, bf16[4,256,128]{2,1,0:T(8,128)(2,1)}, bf16[4,256,128]{2,1,0:T(8,128)(2,1)}) custom-call(bf16[3,256,128]{2,1,0:T(8,128)(2,1)S(1)} %get-tuple-element.25.refs_0_, bf16[3,256,128]{2,1,0:T(8,128)(2,1)S(1)} %collective-permute-done.14.refs_1_, bf16[3,256,128]{2,1,0:T(8,128)(2,1)S(1)} %collective-permute-done.15.refs_2_, ...), custom_call_target="tpu_custom_call" | custom-call | bytes 1572864 | tf_op jit(solution)/shard_map/pallas_call | solution.py:29
  68.1 1.6 %reduce-scatter.2.cloned.1.call-done = bf16[1,256,512]{2,1,0:T(8,128)(2,1)} async-done(((bf16[4,256,512]{2,1,0:T(8,128)(2,1)}), bf16[1,256,512]{2,1,0:T(8,128)(2,1)}) %reduce-scatter.2.cloned.1.call-update) | async-done | bytes 262160 | tf_op jit(solution)/shard_map/reduce_scatter | solution.py:218
  (10 shorter events, 0.2 us)
Async XLA Ops:
  7.2 33.1 %all-gather.3.cloned.1.call-start = ((), (), s32[]{:S(2)}) async-start(), calls=%async_computation.2 | async-start | bytes 1310720 | tf_op jit(solution)/shard_map/all_gather | solution.py:178
  7.9 61.9 %reduce-scatter.2.cloned.1.call-start = ((), (), s32[]{:S(2)}) async-start(), calls=%async_computation.1 | async-start | bytes 1310720 | tf_op jit(solution)/shard_map/reduce_scatter | solution.py:218
  8.0 17.0 %copy-start.2 = (s32[4,4]{1,0:T(4,128)S(1)}, s32[4,4]{1,0:T(4,128)}, u32[]{:S(2)}) copy-start(s32[4,4]{1,0:T(4,128)} %perm.3) | copy-start | bytes 196
  10.1 7.9 %collective-permute-start.1 = (bf16[3,256,128]{2,1,0:T(8,128)(2,1)S(1)}, bf16[3,256,128]{2,1,0:T(8,128)(2,1)S(1)}, u32[]{:S(2)}, u32[]{:S(2)}) collective-permute-start(bf16[3,256,128]{2,1,0:T(8,128)(2,1)S(1)} %pad_maximum_fusion.2), channel_id=1, source_target_pairs={{0,16},{4,20},{8,24},{12,28},{16,0},{20,4},{24,8},{28,12},{1,17},{... | collective-permute-start | bytes 589832 | tf_op jit(solution)/shard_map/ppermute | solution.py:161
  13.2 7.9 %collective-permute-start = (bf16[3,256,128]{2,1,0:T(8,128)(2,1)S(1)}, bf16[3,256,128]{2,1,0:T(8,128)(2,1)S(1)}, u32[]{:S(2)}, u32[]{:S(2)}) collective-permute-start(bf16[3,256,128]{2,1,0:T(8,128)(2,1)S(1)} %pad_maximum_fusion.1), channel_id=1, source_target_pairs={{0,8},{4,12},{8,0},{12,4},{16,24},{20,28},{24,16},{28,20},{1,9},{5... | collective-permute-start | bytes 589832 | tf_op jit(solution)/shard_map/ppermute | solution.py:161
  14.7 22.3 %copy-start = (bf16[4,128,2048]{2,1,0:T(8,128)(2,1)S(1)}, bf16[4,128,2048]{2,1,0:T(8,128)(2,1)}, u32[]{:S(2)}) copy-start(bf16[4,128,2048]{2,1,0:T(8,128)(2,1)} %weight.3) | copy-start | bytes 6291460
  14.8 8.8 %collective-permute-start.2 = (bf16[3,256,128]{2,1,0:T(8,128)(2,1)S(1)}, bf16[3,256,128]{2,1,0:T(8,128)(2,1)S(1)}, u32[]{:S(2)}, u32[]{:S(2)}) collective-permute-start(bf16[3,256,128]{2,1,0:T(8,128)(2,1)S(1)} %pad_maximum_fusion.3), channel_id=1, source_target_pairs={{0,24},{4,28},{8,16},{12,20},{16,8},{20,12},{24,0},{28,4},{1,25},{... | collective-permute-start | bytes 589832 | tf_op jit(solution)/shard_map/ppermute | solution.py:161
  14.9 8.8 %collective-permute-start.3 = (bf16[2,256,128]{2,1,0:T(8,128)(2,1)S(1)}, bf16[2,256,128]{2,1,0:T(8,128)(2,1)S(1)}, u32[]{:S(2)}, u32[]{:S(2)}) collective-permute-start(bf16[2,256,128]{2,1,0:T(8,128)(2,1)S(1)} %pad_maximum_fusion.4), channel_id=1, source_target_pairs={{0,4},{4,0},{8,12},{12,8},{16,20},{20,16},{24,28},{28,24},{1,5},{5... | collective-permute-start | bytes 393224 | tf_op jit(solution)/shard_map/ppermute | solution.py:164
  18.1 5.6 %collective-permute-start.5 = (bf16[2,256,128]{2,1,0:T(8,128)(2,1)S(1)}, bf16[2,256,128]{2,1,0:T(8,128)(2,1)S(1)}, u32[]{:S(2)}, u32[]{:S(2)}) collective-permute-start(bf16[2,256,128]{2,1,0:T(8,128)(2,1)S(1)} %slice.47), channel_id=1, source_target_pairs={{0,4},{4,0},{8,12},{12,8},{16,20},{20,16},{24,28},{28,24},{1,5},{5... | collective-permute-start | bytes 393224 | tf_op jit(solution)/shard_map/ppermute | solution.py:164
  21.1 2.6 %collective-permute-start.4 = (bf16[2,256,128]{2,1,0:T(8,128)(2,1)S(1)}, bf16[2,256,128]{2,1,0:T(8,128)(2,1)S(1)}, u32[]{:S(2)}, u32[]{:S(2)}) collective-permute-start(bf16[2,256,128]{2,1,0:T(8,128)(2,1)S(1)} %slice.46), channel_id=1, source_target_pairs={{0,4},{4,0},{8,12},{12,8},{16,20},{20,16},{24,28},{28,24},{1,5},{5... | collective-permute-start | bytes 393224 | tf_op jit(solution)/shard_map/ppermute | solution.py:164
  23.6 1.4 %collective-permute-start.6 = (bf16[2,256,128]{2,1,0:T(8,128)(2,1)S(1)}, bf16[2,256,128]{2,1,0:T(8,128)(2,1)S(1)}, u32[]{:S(2)}, u32[]{:S(2)}) collective-permute-start(bf16[2,256,128]{2,1,0:T(8,128)(2,1)S(1)} %slice.48), channel_id=1, source_target_pairs={{0,4},{4,0},{8,12},{12,8},{16,20},{20,16},{24,28},{28,24},{1,5},{5... | collective-permute-start | bytes 393224 | tf_op jit(solution)/shard_map/ppermute | solution.py:164
  28.2 1.3 %copy-start.3 = (bf16[4,256,1024]{2,1,0:T(8,128)(2,1)}, bf16[4,256,1024]{2,1,0:T(8,128)(2,1)S(1)}, u32[]{:S(2)}) copy-start(bf16[4,256,1024]{2,1,0:T(8,128)(2,1)S(1)} %get-tuple-element.19.refs_5_) | copy-start | bytes 6291460
  29.5 7.5 %copy-start.5 = (bf16[4,256,128]{2,1,0:T(8,128)(2,1)}, bf16[4,256,128]{2,1,0:T(8,128)(2,1)S(1)}, u32[]{:S(2)}) copy-start(bf16[4,256,128]{2,1,0:T(8,128)(2,1)S(1)} %get-tuple-element.21.refs_7_) | copy-start | bytes 786436
  29.5 5.2 %collective-permute-start.9 = (bf16[256,128]{1,0:T(8,128)(2,1)S(1)}, bf16[256,128]{1,0:T(8,128)(2,1)S(1)}, u32[]{:S(2)}, u32[]{:S(2)}) collective-permute-start(bf16[256,128]{1,0:T(8,128)(2,1)S(1)} %get-tuple-element.36), channel_id=1, source_target_pairs={{0,24},{4,28},{8,16},{12,20},{16,8},{20,12},{24,0},{28,4},{1,25},{... | collective-permute-start | bytes 196616 | tf_op jit(solution)/shard_map/ppermute | solution.py:161
  32.3 4.3 %collective-permute-start.8 = (bf16[256,128]{1,0:T(8,128)(2,1)S(1)}, bf16[256,128]{1,0:T(8,128)(2,1)S(1)}, u32[]{:S(2)}, u32[]{:S(2)}) collective-permute-start(bf16[256,128]{1,0:T(8,128)(2,1)S(1)} %get-tuple-element.37), channel_id=1, source_target_pairs={{0,16},{4,20},{8,24},{12,28},{16,0},{20,4},{24,8},{28,12},{1,17},{... | collective-permute-start | bytes 196616 | tf_op jit(solution)/shard_map/ppermute | solution.py:161
  32.8 4.3 %collective-permute-start.7 = (bf16[256,128]{1,0:T(8,128)(2,1)S(1)}, bf16[256,128]{1,0:T(8,128)(2,1)S(1)}, u32[]{:S(2)}, u32[]{:S(2)}) collective-permute-start(bf16[256,128]{1,0:T(8,128)(2,1)S(1)} %get-tuple-element.38), channel_id=1, source_target_pairs={{0,8},{4,12},{8,0},{12,4},{16,24},{20,28},{24,16},{28,20},{1,9},{5... | collective-permute-start | bytes 196616 | tf_op jit(solution)/shard_map/ppermute | solution.py:161
  40.2 1.2 %copy-start.1 = (bf16[1024,512]{1,0:T(8,128)(2,1)S(1)}, bf16[1024,512]{1,0:T(8,128)(2,1)}, u32[]{:S(2)}) copy-start(bf16[1024,512]{1,0:T(8,128)(2,1)} %all-gather.3.cloned.1.call-done) | copy-start | bytes 3145732
  41.5 8.1 %copy-start.4 = (bf16[4,256,1024]{2,1,0:T(8,128)(2,1)S(1)}, bf16[4,256,1024]{2,1,0:T(8,128)(2,1)}, u32[]{:S(2)}) copy-start(bf16[4,256,1024]{2,1,0:T(8,128)(2,1)} %copy-done.3) | copy-start | bytes 6291460
  41.5 8.1 %copy-start.6 = (bf16[4,256,128]{2,1,0:T(8,128)(2,1)S(1)}, bf16[4,256,128]{2,1,0:T(8,128)(2,1)}, u32[]{:S(2)}) copy-start(bf16[4,256,128]{2,1,0:T(8,128)(2,1)} %copy-done.5) | copy-start | bytes 786436
  42.2 5.3 %collective-permute-start.12 = (bf16[256,128]{1,0:T(8,128)(2,1)S(1)}, bf16[256,128]{1,0:T(8,128)(2,1)S(1)}, u32[]{:S(2)}, u32[]{:S(2)}) collective-permute-start(bf16[256,128]{1,0:T(8,128)(2,1)S(1)} %get-tuple-element.32), channel_id=1, source_target_pairs={{0,24},{4,28},{8,16},{12,20},{16,8},{20,12},{24,0},{28,4},{1,25},{... | collective-permute-start | bytes 196616 | tf_op jit(solution)/shard_map/ppermute | solution.py:161
  44.7 4.3 %collective-permute-start.11 = (bf16[256,128]{1,0:T(8,128)(2,1)S(1)}, bf16[256,128]{1,0:T(8,128)(2,1)S(1)}, u32[]{:S(2)}, u32[]{:S(2)}) collective-permute-start(bf16[256,128]{1,0:T(8,128)(2,1)S(1)} %get-tuple-element.33), channel_id=1, source_target_pairs={{0,16},{4,20},{8,24},{12,28},{16,0},{20,4},{24,8},{28,12},{1,17},{... | collective-permute-start | bytes 196616 | tf_op jit(solution)/shard_map/ppermute | solution.py:161
  45.2 4.3 %collective-permute-start.10 = (bf16[256,128]{1,0:T(8,128)(2,1)S(1)}, bf16[256,128]{1,0:T(8,128)(2,1)S(1)}, u32[]{:S(2)}, u32[]{:S(2)}) collective-permute-start(bf16[256,128]{1,0:T(8,128)(2,1)S(1)} %get-tuple-element.34), channel_id=1, source_target_pairs={{0,8},{4,12},{8,0},{12,4},{16,24},{20,28},{24,16},{28,20},{1,9},{5... | collective-permute-start | bytes 196616 | tf_op jit(solution)/shard_map/ppermute | solution.py:161
  53.0 2.0 %collective-permute-start.13 = (bf16[4,2,256,128]{3,2,1,0:T(8,128)(2,1)S(1)}, bf16[4,2,256,128]{3,2,1,0:T(8,128)(2,1)S(1)}, u32[]{:S(2)}, u32[]{:S(2)}) collective-permute-start(bf16[4,2,256,128]{3,2,1,0:T(8,128)(2,1)S(1)} %get-tuple-element.24), channel_id=1, source_target_pairs={{0,4},{4,0},{8,12},{12,8},{16,20},{20,16},{24,28},{28,24},{1,5},{5... | collective-permute-start | bytes 1572872 | tf_op jit(solution)/shard_map/ppermute | solution.py:164
  55.1 7.8 %collective-permute-start.14 = (bf16[3,256,128]{2,1,0:T(8,128)(2,1)S(1)}, bf16[3,256,128]{2,1,0:T(8,128)(2,1)S(1)}, u32[]{:S(2)}, u32[]{:S(2)}) collective-permute-start(bf16[3,256,128]{2,1,0:T(8,128)(2,1)S(1)} %get-tuple-element.26), channel_id=1, source_target_pairs={{0,8},{4,12},{8,0},{12,4},{16,24},{20,28},{24,16},{28,20},{1,9},{5... | collective-permute-start | bytes 589832 | tf_op jit(solution)/shard_map/ppermute | solution.py:161
  55.7 9.9 %collective-permute-start.15 = (bf16[3,256,128]{2,1,0:T(8,128)(2,1)S(1)}, bf16[3,256,128]{2,1,0:T(8,128)(2,1)S(1)}, u32[]{:S(2)}, u32[]{:S(2)}) collective-permute-start(bf16[3,256,128]{2,1,0:T(8,128)(2,1)S(1)} %get-tuple-element.27), channel_id=1, source_target_pairs={{0,16},{4,20},{8,24},{12,28},{16,0},{20,4},{24,8},{28,12},{1,17},{... | collective-permute-start | bytes 589832 | tf_op jit(solution)/shard_map/ppermute | solution.py:161
  57.2 10.0 %collective-permute-start.16 = (bf16[3,256,128]{2,1,0:T(8,128)(2,1)S(1)}, bf16[3,256,128]{2,1,0:T(8,128)(2,1)S(1)}, u32[]{:S(2)}, u32[]{:S(2)}) collective-permute-start(bf16[3,256,128]{2,1,0:T(8,128)(2,1)S(1)} %get-tuple-element.28), channel_id=1, source_target_pairs={{0,24},{4,28},{8,16},{12,20},{16,8},{20,12},{24,0},{28,4},{1,25},{... | collective-permute-start | bytes 589832 | tf_op jit(solution)/shard_map/ppermute | solution.py:161
Sparse Core Ops, SparseCore 0:
  9.6 30.6 all-gather.2
  43.1 26.6 reduce-scatter.1

commit v2 on v1

--- a/solution.py
+++ b/solution.py
@@ -103,31 +103,40 @@
             out[d, 1] = value_part.astype(out.dtype)
 
 
-def project_body(chips, weight, *refs):
-    attended, out, joined = refs[:chips], refs[chips], refs[chips + 1]
-    chip = chip_index()
+def project_body(chips, groups, weight, *refs):
+    attended, outs, joined = refs[:chips], refs[chips : chips + groups], refs[chips + groups]
+    chip = chip_index()
+    level = lax.axis_index("head")
     width = attended[0].shape[1]
     for d in range(chips):
         lanes = pl.ds(pl.multiple_of((chip ^ d) * width, width), width)
         joined[:, lanes] = attended[d][...]
-    columns = out.shape[2]
     rows = joined[...]
-    flat = weight.reshape(chips * width, weight.shape[2])
-    for s in range(out.shape[0]):
-        out[s] = dot(rows, flat[:, s * columns : (s + 1) * columns]).astype(out.dtype)
-
-
-def grad_body(chips, weight, cotangent, out):
-    chip = chip_index()
+    for j in range(groups):
+        columns = outs[j].shape[1]
+        lanes = pl.ds(pl.multiple_of((level ^ j) * columns, columns), columns)
+        term = weight[:, :, lanes].reshape(chips * width, columns)
+        outs[j][...] = dot(rows, term).astype(LOW)
+
+
+def grad_body(chips, groups, weight, *refs):
+    slices, out = refs[:-1], refs[-1]
+    chip = chip_index()
+    level = lax.axis_index("head")
+    inner = (level > 0) & (level < groups - 1)
     width = out.shape[2]
-    columns = cotangent.shape[2]
-    flat = weight.reshape(chips * width, weight.shape[2])
     total = None
-    for s in range(cotangent.shape[0]):
-        term = dot(cotangent[s], flat[:, s * columns : (s + 1) * columns], NT)
+    for j in range(groups):
+        if j < 2:
+            block = slices[j][...]
+        else:
+            block = jnp.where(inner, slices[2 * j - 2][...], slices[2 * j - 1][...])
+        columns = block.shape[1]
+        lanes = pl.ds(pl.multiple_of((level ^ j) * columns, columns), columns)
+        term = dot(block, weight[:, :, lanes].reshape(chips * width, columns), NT)
         total = term if total is None else total + term
     for h in range(chips):
-        out[h ^ chip] = total[:, h * width : (h + 1) * width].astype(out.dtype)
+        out[h ^ chip] = total[:, h * width : (h + 1) * width].astype(LOW)
 
 
 def merge_body(chips, query_grad, own_part, arrived, *outs):
@@ -175,7 +184,12 @@
             ]
         )
 
-    gathered = lax.all_gather(out_cotangent, "head", axis=0, tiled=False)
+    def along(array, pairs):
+        return lax.ppermute(array, "head", pairs)
+
+    skip_in = along(out_cotangent, [(0, 2), (3, 1)])
+    pair_in = along(out_cotangent, [(0, 1), (1, 0), (2, 3), (3, 2)])
+    middle_in = along(out_cotangent, [(1, 2), (2, 1)])
     pieces = exchange([head_piece(d) for d in range(chips)])
     siblings = [to_sibling(piece[:2]) for piece in pieces]
     tile = rows * width
@@ -196,26 +210,41 @@
         smem=(0,),
     )
     weight_bytes = 2 * heads * width * features
+    far_in = along(skip_in, [(2, 3), (1, 0)])
+    near_in = along(middle_in, [(2, 3), (1, 0)])
     grad_att = call(
-        functools.partial(grad_body, chips),
+        functools.partial(grad_body, chips, groups),
         shape((chips, rows, width), LOW),
         out_weight,
-        gathered,
+        out_cotangent,
+        pair_in,
+        skip_in,
+        near_in,
+        middle_in,
+        far_in,
         flops=2 * rows * heads * width * features,
         moved=weight_bytes + 2 * rows * features + 2 * chips * tile,
     )
     grads = exchange([grad_att[d] for d in range(chips)])
     own_attended = exchange([attended[d] for d in range(chips)])
-    partial_out = call(
-        functools.partial(project_body, chips),
-        shape((groups, rows, columns), LOW),
+    parts = call(
+        functools.partial(project_body, chips, groups),
+        tuple(shape((rows, columns), LOW) for _ in range(groups)),
         out_weight,
         *own_attended,
         flops=2 * rows * heads * width * features,
         moved=weight_bytes + 2 * rows * features + 2 * chips * tile,
         scratch=[pltpu.VMEM((rows, heads * width), LOW)],
     )
-    projected = lax.psum_scatter(partial_out, "head", scatter_dimension=0, tiled=False)
+
+    def plus(a, b):
+        return (a.astype(F32) + b.astype(F32)).astype(LOW)
+
+    end_far = along(parts[3], [(3, 2), (0, 1)])
+    end_near = along(parts[2], [(3, 2), (0, 1)])
+    pair_out = along(parts[1], [(0, 1), (1, 0), (2, 3), (3, 2)])
+    skip_out = along(plus(parts[2], end_far), [(2, 0), (1, 3)])
+    middle_out = along(plus(parts[3], end_near), [(2, 1), (1, 2)])
     query_grad, own_part, sibling_part = call(
         functools.partial(backward_body, chips, rows, scale),
         (
@@ -253,7 +282,11 @@
         *returned,
         moved=2 * 6 * chips * tile,
     )
-    return (projected, *gradients)
+    level = lax.axis_index("head")
+    inner = (level > 0) & (level < groups - 1)
+    passed = jnp.where(inner, middle_out, skip_out)
+    projected = parts[0].astype(F32) + pair_out.astype(F32) + passed.astype(F32)
+    return (projected.astype(LOW), *gradients)
 
 
 def partner(shard, axis, bit):
@@ -366,7 +399,7 @@
 
 def per_device(*arrays):
     chips = lax.axis_size("seq") // 2
-    square = chips == arrays[0].shape[0] and chips & (chips - 1) == 0
+    square = chips == arrays[0].shape[0] == lax.axis_size("head") == 4
     return (by_heads if square else by_routing)(*arrays)
 
 

time: 76.9 us -> 75.5 us (0.982)
  the two profiles are of different devices: /device:TPU:0 before, /device:TPU:12 now
where the time goes in v2:
time: 75.5 us; the launch traced here: 75.2 us
  starting transfers between devices  38.4 us (51%)
  waiting for transfers between devices  20.9 us (28%)
  Pallas kernels  9.21 us (12%)
  other arithmetic  3.44 us (5%)
  local copies, waits for them, and re-layouts  2.19 us (3%)
  between operations  0.98 us (1%)
    ppermute x10, starting transfers between devices, along(): return lax.ppermute(array, 'head', pairs)  22.4 us
    ppermute x12, starting transfers between devices, to_chip(): return lax.ppermute(array, 'seq', [(i, i ^ 2 * d) for i in range(devices)])  15.4 us
    ppermute x12, waiting for transfers between devices, to_chip(): return lax.ppermute(array, 'seq', [(i, i ^ 2 * d) for i in range(devices)])  13.8 us
    pallas_call x6, Pallas kernels, call(): pl.pallas_call(body, out_shape=outs, in_specs=[scalar if i in smem else v...  9.21 us
    ppermute x10, waiting for transfers between devices, along(): return lax.ppermute(array, 'head', pairs)  7.09 us
    dynamic_slice x2, local copies, waits for them, and re-layouts, head_piece(): lax.dynamic_index_in_dim(a, h, 0, keepdims=False)  2.11 us
    convert_element_type x1, other arithmetic, by_heads(): return (projected.astype(LOW), *gradients)  1.79 us
    convert_element_type x2, other arithmetic, plus(): return (a.astype(F32) + b.astype(F32)).astype(LOW)  1.54 us
  transfers between devices with their start and end apart: 27, of which 8 were waited for; matrix products, arithmetic and copies ran while one was open for 7% of the time, Pallas kernels for 11%

profile of v2, /device:TPU:12, one launch (start us, length us, event | category | flops | bytes accessed | tf_op | source)
XLA Modules:
  0.0 75.2 jit_solution(1860688853048598258)
XLA Ops:
  0.6 1.3 %collective-permute-start.16 = (bf16[256,512]{1,0:T(8,128)(2,1)}, bf16[256,512]{1,0:T(8,128)(2,1)S(1)}, u32[]{:S(2)}, u32[]{:S(2)}) collective-permute-start(bf16[256,512]{1,0:T(8,128)(2,1)} %refs_0_.1), channel_id=1, source_target_pairs={{0,2},{3,1},{4,6},{7,5},{8,10},{11,9},{12,14},{15,13},{16,18},{19,... | collective-permute-start | bytes 786440 | tf_op jit(solution)/shard_map/ppermute | solution.py:188
  1.9 3.5 %collective-permute-start.17 = (bf16[256,512]{1,0:T(8,128)(2,1)}, bf16[256,512]{1,0:T(8,128)(2,1)S(1)}, u32[]{:S(2)}, u32[]{:S(2)}) collective-permute-start(bf16[256,512]{1,0:T(8,128)(2,1)} %refs_0_.1), channel_id=1, source_target_pairs={{1,2},{2,1},{5,6},{6,5},{9,10},{10,9},{13,14},{14,13},{17,18},{18,... | collective-permute-start | bytes 786440 | tf_op jit(solution)/shard_map/ppermute | solution.py:188
  5.5 1.0 %constant_dynamic-slice_fusion.2 = (bf16[1,256,128]{2,1,0:T(8,128)(2,1)S(1)}, bf16[1,256,128]{2,1,0:T(8,128)(2,1)S(1)}, bf16[1,256,128]{2,1,0:T(8,128)(2,1)S(1)}, bf16[1,256,128]{2,1,0:T(8,128)(2,1)S(1)}) fusion(bf16[4,256,128]{2,1,0:T(8,128)(2,1)} %param.7, s32[]{:T(128)S(6)} %select_n.38, s32[]{:T(128)S(6)} %select_n.36, s32[]{:T(128)S(6)} %select_n.35, ...), kind=kLoop, calls=%fused_computation.18 | loop fusion | bytes 524304 | tf_op jit(solution)/shard_map/jit(dynamic_index_in_dim)/dynamic_slice | solution.py:182
  6.5 1.1 %constant_dynamic-slice_fusion = (bf16[1,256,128]{2,1,0:T(8,128)(2,1)S(1)}, bf16[1,256,128]{2,1,0:T(8,128)(2,1)S(1)}, bf16[1,256,128]{2,1,0:T(8,128)(2,1)S(1)}, ...) fusion(bf16[4,256,128]{2,1,0:T(8,128)(2,1)} %param.6, ...), kind=kLoop, calls=%fused_computation.16 | loop fusion | bytes 1048592 | tf_op jit(solution)/shard_map/jit(dynamic_index_in_dim)/dynamic_slice | solution.py:182
  7.6 0.6 collective-permute-start.1
  8.2 1.6 %collective-permute-start = (bf16[3,256,128]{2,1,0:T(8,128)(2,1)S(1)}, bf16[3,256,128]{2,1,0:T(8,128)(2,1)S(1)}, u32[]{:S(2)}, u32[]{:S(2)}) collective-permute-start(bf16[3,256,128]{2,1,0:T(8,128)(2,1)S(1)} %pad_maximum_fusion.1), channel_id=1, source_target_pairs={{0,8},{4,12},{8,0},{12,4},{16,24},{20,28},{24,16},{28,20},{1,9},{5... | collective-permute-start | bytes 589832 | tf_op jit(solution)/shard_map/ppermute | solution.py:170
  9.8 1.6 %collective-permute-start.2 = (bf16[3,256,128]{2,1,0:T(8,128)(2,1)S(1)}, bf16[3,256,128]{2,1,0:T(8,128)(2,1)S(1)}, u32[]{:S(2)}, u32[]{:S(2)}) collective-permute-start(bf16[3,256,128]{2,1,0:T(8,128)(2,1)S(1)} %pad_maximum_fusion.3), channel_id=1, source_target_pairs={{0,24},{4,28},{8,16},{12,20},{16,8},{20,12},{24,0},{28,4},{1,25},{... | collective-permute-start | bytes 589832 | tf_op jit(solution)/shard_map/ppermute | solution.py:170
  11.4 3.1 %collective-permute-done.1.refs_2_ = bf16[3,256,128]{2,1,0:T(8,128)(2,1)S(1)} collective-permute-done((bf16[3,256,128]{2,1,0:T(8,128)(2,1)S(1)}, bf16[3,256,128]{2,1,0:T(8,128)(2,1)S(1)}, u32[]{:S(2)}, u32[]{:S(2)}) %collective-permute-start.1) | collective-permute-done | bytes 196640 | tf_op jit(solution)/shard_map/ppermute | solution.py:170
  14.5 0.0 collective-permute-start.3
  14.6 1.6 %collective-permute-done.refs_1_ = bf16[3,256,128]{2,1,0:T(8,128)(2,1)S(1)} collective-permute-done((bf16[3,256,128]{2,1,0:T(8,128)(2,1)S(1)}, bf16[3,256,128]{2,1,0:T(8,128)(2,1)S(1)}, u32[]{:S(2)}, u32[]{:S(2)}) %collective-permute-start) | collective-permute-done | bytes 196640 | tf_op jit(solution)/shard_map/ppermute | solution.py:170
  16.1 0.0 collective-permute-start.5
  16.2 3.4 %collective-permute-done.2.refs_3_ = bf16[3,256,128]{2,1,0:T(8,128)(2,1)S(1)} collective-permute-done((bf16[3,256,128]{2,1,0:T(8,128)(2,1)S(1)}, bf16[3,256,128]{2,1,0:T(8,128)(2,1)S(1)}, u32[]{:S(2)}, u32[]{:S(2)}) %collective-permute-start.2) | collective-permute-done | bytes 196640 | tf_op jit(solution)/shard_map/ppermute | solution.py:170
  19.5 0.0 collective-permute-start.4
  19.6 0.0 collective-permute-done.3.refs_4_
  19.6 0.6 collective-permute-start.6
  20.2 0.0 collective-permute-done.16.refs_2_
  20.2 0.9 %collective-permute-start.15 = (bf16[256,512]{1,0:T(8,128)(2,1)S(1)}, bf16[256,512]{1,0:T(8,128)(2,1)S(1)}, u32[]{:S(2)}, u32[]{:S(2)}) collective-permute-start(bf16[256,512]{1,0:T(8,128)(2,1)S(1)} %copy-done.1), channel_id=1, source_target_pairs={{0,1},{1,0},{2,3},{3,2},{4,5},{5,4},{6,7},{7,6},{8,9},{9,8},{10,11... | collective-permute-start | bytes 786440 | tf_op jit(solution)/shard_map/ppermute | solution.py:188
  21.1 0.0 collective-permute-done.17.refs_4_
  21.1 3.1 %collective-permute-start.19 = (bf16[256,512]{1,0:T(8,128)(2,1)S(1)}, bf16[256,512]{1,0:T(8,128)(2,1)S(1)}, u32[]{:S(2)}, u32[]{:S(2)}) collective-permute-start(bf16[256,512]{1,0:T(8,128)(2,1)S(1)} %collective-permute-done.16.refs_2_), channel_id=1, source_target_pairs={{2,3},{1,0},{6,7},{5,4},{10,11},{9,8},{14,15},{13,12},{18,19},{17,... | collective-permute-start | bytes 786440 | tf_op jit(solution)/shard_map/ppermute | solution.py:188
  24.2 0.0 collective-permute-done.5.refs_6_
  24.2 1.3 %collective-permute-start.18 = (bf16[256,512]{1,0:T(8,128)(2,1)S(1)}, bf16[256,512]{1,0:T(8,128)(2,1)S(1)}, u32[]{:S(2)}, u32[]{:S(2)}) collective-permute-start(bf16[256,512]{1,0:T(8,128)(2,1)S(1)} %collective-permute-done.17.refs_4_), channel_id=1, source_target_pairs={{2,3},{1,0},{6,7},{5,4},{10,11},{9,8},{14,15},{13,12},{18,19},{17,... | collective-permute-start | bytes 786440 | tf_op jit(solution)/shard_map/ppermute | solution.py:188
  25.5 0.0 collective-permute-done.4.refs_5_
  25.5 0.0 collective-permute-done.6.refs_7_
  25.6 3.2 %shard_map.93 = (bf16[4,256,128]{2,1,0:T(8,128)(2,1)S(1)}, bf16[4,256,1024]{2,1,0:T(8,128)(2,1)S(1)}, bf16[4,2,512,128]{3,2,1,0:T(8,128)(2,1)S(1)}, bf16[4,256,128]{2,1,0:T(8,128)(2,1)S(1)}) custom-call(s32[4,4]{1,0:T(4,128)S(1)} %copy-done.2, bf16[3,256,128]{2,1,0:T(8,128)(2,1)S(1)} %pad_maximum_fusion.refs_0_, ...), custom_call_target="tpu_custom_call" | custom-call | flops 536870912 | bytes 5767168 | tf_op jit(solution)/shard_map/pallas_call | solution.py:29
  28.8 1.5 %collective-permute-start.9 = (bf16[256,128]{1,0:T(8,128)(2,1)S(1)}, bf16[256,128]{1,0:T(8,128)(2,1)S(1)}, u32[]{:S(2)}, u32[]{:S(2)}) collective-permute-start(bf16[256,128]{1,0:T(8,128)(2,1)S(1)} %get-tuple-element.44), channel_id=1, source_target_pairs={{0,24},{4,28},{8,16},{12,20},{16,8},{20,12},{24,0},{28,4},{1,25},{... | collective-permute-start | bytes 196616 | tf_op jit(solution)/shard_map/ppermute | solution.py:170
  30.3 1.5 %collective-permute-start.8 = (bf16[256,128]{1,0:T(8,128)(2,1)S(1)}, bf16[256,128]{1,0:T(8,128)(2,1)S(1)}, u32[]{:S(2)}, u32[]{:S(2)}) collective-permute-start(bf16[256,128]{1,0:T(8,128)(2,1)S(1)} %get-tuple-element.45), channel_id=1, source_target_pairs={{0,16},{4,20},{8,24},{12,28},{16,0},{20,4},{24,8},{28,12},{1,17},{... | collective-permute-start | bytes 196616 | tf_op jit(solution)/shard_map/ppermute | solution.py:170
  31.8 2.2 %collective-permute-done.9.refs_3_ = bf16[256,128]{1,0:T(8,128)(2,1)S(1)} collective-permute-done((bf16[256,128]{1,0:T(8,128)(2,1)S(1)}, bf16[256,128]{1,0:T(8,128)(2,1)S(1)}, u32[]{:S(2)}, u32[]{:S(2)}) %collective-permute-start.9) | collective-permute-done | bytes 65568 | tf_op jit(solution)/shard_map/ppermute | solution.py:170
  34.0 1.6 %collective-permute-start.7 = (bf16[256,128]{1,0:T(8,128)(2,1)S(1)}, bf16[256,128]{1,0:T(8,128)(2,1)S(1)}, u32[]{:S(2)}, u32[]{:S(2)}) collective-permute-start(bf16[256,128]{1,0:T(8,128)(2,1)S(1)} %get-tuple-element.46), channel_id=1, source_target_pairs={{0,8},{4,12},{8,0},{12,4},{16,24},{20,28},{24,16},{28,20},{1,9},{5... | collective-permute-start | bytes 196616 | tf_op jit(solution)/shard_map/ppermute | solution.py:170
  35.6 0.0 collective-permute-done.8.refs_2_
  35.6 2.7 %collective-permute-done.7.refs_1_ = bf16[256,128]{1,0:T(8,128)(2,1)S(1)} collective-permute-done((bf16[256,128]{1,0:T(8,128)(2,1)S(1)}, bf16[256,128]{1,0:T(8,128)(2,1)S(1)}, u32[]{:S(2)}, u32[]{:S(2)}) %collective-permute-start.7) | collective-permute-done | bytes 65568 | tf_op jit(solution)/shard_map/ppermute | solution.py:170
  38.3 0.8 %shard_map.94 = (bf16[256,512]{1,0:T(8,128)(2,1)S(1)}, bf16[256,512]{1,0:T(8,128)(2,1)S(1)}, bf16[256,512]{1,0:T(8,128)(2,1)S(1)}, bf16[256,512]{1,0:T(8,128)(2,1)S(1)}) custom-call(bf16[4,128,2048]{2,1,0:T(8,128)(2,1)S(1)} %copy-done, bf16[256,128]{1,0:T(8,128)(2,1)S(1)} %get-tuple-element.47.refs_0_, bf16[256,128]{1,0:T(8,128)(2,1)S(1)} %collective-permute-done.7.refs_1_, ...), custom_call_target="tpu_custom_call" | custom-call | flops 536870912 | bytes 3407872 | tf_op jit(solution)/shard_map/pallas_call | solution.py:29
  39.1 1.3 %collective-permute-start.13 = (bf16[256,512]{1,0:T(8,128)(2,1)S(1)}, bf16[256,512]{1,0:T(8,128)(2,1)S(1)}, u32[]{:S(2)}, u32[]{:S(2)}) collective-permute-start(bf16[256,512]{1,0:T(8,128)(2,1)S(1)} %get-tuple-element.25), channel_id=1, source_target_pairs={{3,2},{0,1},{7,6},{4,5},{11,10},{8,9},{15,14},{12,13},{19,18},{16,... | collective-permute-start | bytes 786440 | tf_op jit(solution)/shard_map/ppermute | solution.py:188
  40.4 0.0 collective-permute-done.15.refs_1_
  40.4 0.0 collective-permute-done.19.refs_5_
  40.4 0.0 collective-permute-done.18.refs_3_
  40.4 0.8 %shard_map.95 = bf16[4,256,128]{2,1,0:T(8,128)(2,1)S(1)} custom-call(bf16[4,128,2048]{2,1,0:T(8,128)(2,1)S(1)} %copy-done, bf16[256,512]{1,0:T(8,128)(2,1)S(1)} %copy-done.1, bf16[256,512]{1,0:T(8,128)(2,1)S(1)} %collective-permute-done.15.refs_1_, bf16[256,512]{1,0:T(8,128)(2,1)S(1)} %collective-permute-done.16.refs_2_, ...), custom_call_target="tpu_custom_call" | custom-call | flops 536870912 | bytes 3407872 | tf_op jit(solution)/shard_map/pallas_call | solution.py:29
  41.2 1.5 %collective-permute-start.22 = (bf16[256,128]{1,0:T(8,128)(2,1)S(1)}, bf16[256,128]{1,0:T(8,128)(2,1)S(1)}, u32[]{:S(2)}, u32[]{:S(2)}) collective-permute-start(bf16[256,128]{1,0:T(8,128)(2,1)S(1)} %get-tuple-element.40), channel_id=1, source_target_pairs={{0,24},{4,28},{8,16},{12,20},{16,8},{20,12},{24,0},{28,4},{1,25},{... | collective-permute-start | bytes 196616 | tf_op jit(solution)/shard_map/ppermute | solution.py:170
  42.7 1.6 %collective-permute-start.21 = (bf16[256,128]{1,0:T(8,128)(2,1)S(1)}, bf16[256,128]{1,0:T(8,128)(2,1)S(1)}, u32[]{:S(2)}, u32[]{:S(2)}) collective-permute-start(bf16[256,128]{1,0:T(8,128)(2,1)S(1)} %get-tuple-element.41), channel_id=1, source_target_pairs={{0,16},{4,20},{8,24},{12,28},{16,0},{20,4},{24,8},{28,12},{1,17},{... | collective-permute-start | bytes 196616 | tf_op jit(solution)/shard_map/ppermute | solution.py:170
  44.3 0.4 collective-permute-start.20
  44.8 2.7 %collective-permute-start.10 = (bf16[256,512]{1,0:T(8,128)(2,1)S(1)}, bf16[256,512]{1,0:T(8,128)(2,1)S(1)}, u32[]{:S(2)}, u32[]{:S(2)}) collective-permute-start(bf16[256,512]{1,0:T(8,128)(2,1)S(1)} %get-tuple-element.24), channel_id=1, source_target_pairs={{0,1},{1,0},{2,3},{3,2},{4,5},{5,4},{6,7},{7,6},{8,9},{9,8},{10,11... | collective-permute-start | bytes 786440 | tf_op jit(solution)/shard_map/ppermute | solution.py:188
  47.4 0.0 collective-permute-done.22.refs_3_
  47.4 1.3 %collective-permute-start.11 = (bf16[256,512]{1,0:T(8,128)(2,1)S(1)}, bf16[256,512]{1,0:T(8,128)(2,1)S(1)}, u32[]{:S(2)}, u32[]{:S(2)}) collective-permute-start(bf16[256,512]{1,0:T(8,128)(2,1)S(1)} %get-tuple-element.26), channel_id=1, source_target_pairs={{3,2},{0,1},{7,6},{4,5},{11,10},{8,9},{15,14},{12,13},{19,18},{16,... | collective-permute-start | bytes 786440 | tf_op jit(solution)/shard_map/ppermute | solution.py:188
  48.7 0.0 collective-permute-done.21.refs_2_
  48.7 0.0 collective-permute-done.20.refs_1_
  48.7 3.5 %shard_map.96 = (bf16[4,256,128]{2,1,0:T(8,128)(2,1)S(1)}, f32[4,2,256,128]{3,2,1,0:T(8,128)S(1)}, bf16[4,2,256,128]{3,2,1,0:T(8,128)(2,1)S(1)}) custom-call(s32[4,4]{1,0:T(4,128)S(1)} %copy-done.2, bf16[256,128]{1,0:T(8,128)(2,1)S(1)} %get-tuple-element.43.refs_0_, bf16[256,128]{1,0:T(8,128)(2,1)S(1)} %collective-permute-done.20.refs_1_, ...), custom_call_target="tpu_custom_call" | custom-call | flops 1073741824 | bytes 7340032 | tf_op jit(solution)/shard_map/pallas_call | solution.py:29
  52.2 0.1 collective-permute-start.23
  52.3 0.0 collective-permute-done.13
  52.3 0.8 %add_convert_fusion.1 = bf16[256,512]{1,0:T(8,128)(2,1)} fusion(bf16[256,512]{1,0:T(8,128)(2,1)S(1)} %collective-permute-done.13, bf16[256,512]{1,0:T(8,128)(2,1)S(1)} %get-tuple-element.26), kind=kLoop, calls=%fused_computation.1 | loop fusion | flops 524288 | bytes 786432 | tf_op jit(solution)/shard_map/convert_element_type | solution.py:241
  53.0 4.4 %collective-permute-start.14 = (bf16[256,512]{1,0:T(8,128)(2,1)}, bf16[256,512]{1,0:T(8,128)(2,1)S(1)}, u32[]{:S(2)}, u32[]{:S(2)}) collective-permute-start(bf16[256,512]{1,0:T(8,128)(2,1)} %add_convert_fusion.1), channel_id=1, source_target_pairs={{2,0},{1,3},{6,4},{5,7},{10,8},{9,11},{14,12},{13,15},{18,16},{17,... | collective-permute-start | bytes 786440 | tf_op jit(solution)/shard_map/ppermute | solution.py:188
  57.5 0.9 %collective-permute-done.11 = bf16[256,512]{1,0:T(8,128)(2,1)S(1)} collective-permute-done((bf16[256,512]{1,0:T(8,128)(2,1)S(1)}, bf16[256,512]{1,0:T(8,128)(2,1)S(1)}, u32[]{:S(2)}, u32[]{:S(2)}) %collective-permute-start.11) | collective-permute-done | bytes 262176 | tf_op jit(solution)/shard_map/ppermute | solution.py:188
  58.4 0.8 %add_convert_fusion.2 = bf16[256,512]{1,0:T(8,128)(2,1)} fusion(bf16[256,512]{1,0:T(8,128)(2,1)S(1)} %collective-permute-done.11, bf16[256,512]{1,0:T(8,128)(2,1)S(1)} %get-tuple-element.25), kind=kLoop, calls=%fused_computation.2 | loop fusion | flops 524288 | bytes 786432 | tf_op jit(solution)/shard_map/convert_element_type | solution.py:241
  59.1 2.6 %collective-permute-start.12 = (bf16[256,512]{1,0:T(8,128)(2,1)}, bf16[256,512]{1,0:T(8,128)(2,1)}, u32[]{:S(2)}, u32[]{:S(2)}) collective-permute-start(bf16[256,512]{1,0:T(8,128)(2,1)} %add_convert_fusion.2), channel_id=1, source_target_pairs={{2,1},{1,2},{6,5},{5,6},{10,9},{9,10},{14,13},{13,14},{18,17},{17,... | collective-permute-start | bytes 786440 | tf_op jit(solution)/shard_map/ppermute | solution.py:188
  61.8 0.0 collective-permute-done.23.arrived
  61.8 0.1 shard_map.97
  61.9 1.6 %collective-permute-start.24 = (bf16[3,256,128]{2,1,0:T(8,128)(2,1)S(1)}, bf16[3,256,128]{2,1,0:T(8,128)(2,1)S(1)}, u32[]{:S(2)}, u32[]{:S(2)}) collective-permute-start(bf16[3,256,128]{2,1,0:T(8,128)(2,1)S(1)} %get-tuple-element.34), channel_id=1, source_target_pairs={{0,8},{4,12},{8,0},{12,4},{16,24},{20,28},{24,16},{28,20},{1,9},{5... | collective-permute-start | bytes 589832 | tf_op jit(solution)/shard_map/ppermute | solution.py:170
  63.5 0.4 collective-permute-start.25
  63.9 0.0 collective-permute-done.10
  63.9 1.5 %collective-permute-start.26 = (bf16[3,256,128]{2,1,0:T(8,128)(2,1)S(1)}, bf16[3,256,128]{2,1,0:T(8,128)(2,1)S(1)}, u32[]{:S(2)}, u32[]{:S(2)}) collective-permute-start(bf16[3,256,128]{2,1,0:T(8,128)(2,1)S(1)} %get-tuple-element.36), channel_id=1, source_target_pairs={{0,24},{4,28},{8,16},{12,20},{16,8},{20,12},{24,0},{28,4},{1,25},{... | collective-permute-start | bytes 589832 | tf_op jit(solution)/shard_map/ppermute | solution.py:170
  65.5 0.0 collective-permute-done.14
  65.5 6.2 %collective-permute-done.12 = bf16[256,512]{1,0:T(8,128)(2,1)} collective-permute-done((bf16[256,512]{1,0:T(8,128)(2,1)}, bf16[256,512]{1,0:T(8,128)(2,1)}, u32[]{:S(2)}, u32[]{:S(2)}) %collective-permute-start.12) | collective-permute-done | bytes 262176 | tf_op jit(solution)/shard_map/ppermute | solution.py:188
  71.7 1.8 %add_convert_fusion = bf16[256,512]{1,0:T(8,128)(2,1)} fusion(bf16[256,512]{1,0:T(8,128)(2,1)S(1)} %collective-permute-done.10, bf16[256,512]{1,0:T(8,128)(2,1)S(1)} %get-tuple-element.23, bf16[256,512]{1,0:T(8,128)(2,1)} %collective-permute-done.12, bf16[256,512]{1,0:T(8,128)(2,1)S(1)} %collective-permute-done.14, pred[]{:T(512)S(6)} %and.11), kind=kLoop, calls=%fused_computation | loop fusion | flops 917504 | bytes 1310721 | tf_op jit(solution)/shard_map/convert_element_type | solution.py:289
  73.4 0.0 collective-permute-done.24.refs_1_
  73.4 0.8 %collective-permute-done.25.refs_2_ = bf16[3,256,128]{2,1,0:T(8,128)(2,1)S(1)} collective-permute-done((bf16[3,256,128]{2,1,0:T(8,128)(2,1)S(1)}, bf16[3,256,128]{2,1,0:T(8,128)(2,1)S(1)}, u32[]{:S(2)}, u32[]{:S(2)}) %collective-permute-start.25) | collective-permute-done | bytes 196640 | tf_op jit(solution)/shard_map/ppermute | solution.py:170
  74.2 0.9 %shard_map.98 = (bf16[4,256,128]{2,1,0:T(8,128)(2,1)}, bf16[4,256,128]{2,1,0:T(8,128)(2,1)}, bf16[4,256,128]{2,1,0:T(8,128)(2,1)}) custom-call(bf16[3,256,128]{2,1,0:T(8,128)(2,1)S(1)} %get-tuple-element.33.refs_0_, bf16[3,256,128]{2,1,0:T(8,128)(2,1)S(1)} %collective-permute-done.24.refs_1_, bf16[3,256,128]{2,1,0:T(8,128)(2,1)S(1)} %collective-permute-done.25.refs_2_, ...), custom_call_target="tpu_custom_call" | custom-call | bytes 1572864 | tf_op jit(solution)/shard_map/pallas_call | solution.py:29
  (17 shorter events, 0.2 us)
Async XLA Ops:
  0.6 19.5 %collective-permute-start.16 = (bf16[256,512]{1,0:T(8,128)(2,1)}, bf16[256,512]{1,0:T(8,128)(2,1)S(1)}, u32[]{:S(2)}, u32[]{:S(2)}) collective-permute-start(bf16[256,512]{1,0:T(8,128)(2,1)} %refs_0_.1), channel_id=1, source_target_pairs={{0,2},{3,1},{4,6},{7,5},{8,10},{11,9},{12,14},{15,13},{16,18},{19,... | collective-permute-start | bytes 786440 | tf_op jit(solution)/shard_map/ppermute | solution.py:188
  1.9 19.2 %collective-permute-start.17 = (bf16[256,512]{1,0:T(8,128)(2,1)}, bf16[256,512]{1,0:T(8,128)(2,1)S(1)}, u32[]{:S(2)}, u32[]{:S(2)}) collective-permute-start(bf16[256,512]{1,0:T(8,128)(2,1)} %refs_0_.1), channel_id=1, source_target_pairs={{1,2},{2,1},{5,6},{6,5},{9,10},{10,9},{13,14},{14,13},{17,18},{18,... | collective-permute-start | bytes 786440 | tf_op jit(solution)/shard_map/ppermute | solution.py:188
  5.5 14.7 %copy-start.1 = (bf16[256,512]{1,0:T(8,128)(2,1)S(1)}, bf16[256,512]{1,0:T(8,128)(2,1)}, u32[]{:S(2)}) copy-start(bf16[256,512]{1,0:T(8,128)(2,1)} %refs_0_.1) | copy-start | bytes 786436
  5.5 20.1 %copy-start.2 = (s32[4,4]{1,0:T(4,128)S(1)}, s32[4,4]{1,0:T(4,128)}, u32[]{:S(2)}) copy-start(s32[4,4]{1,0:T(4,128)} %perm.3) | copy-start | bytes 196
  7.6 6.9 %collective-permute-start.1 = (bf16[3,256,128]{2,1,0:T(8,128)(2,1)S(1)}, bf16[3,256,128]{2,1,0:T(8,128)(2,1)S(1)}, u32[]{:S(2)}, u32[]{:S(2)}) collective-permute-start(bf16[3,256,128]{2,1,0:T(8,128)(2,1)S(1)} %pad_maximum_fusion.2), channel_id=1, source_target_pairs={{0,16},{4,20},{8,24},{12,28},{16,0},{20,4},{24,8},{28,12},{1,17},{... | collective-permute-start | bytes 589832 | tf_op jit(solution)/shard_map/ppermute | solution.py:170
  8.2 7.9 %collective-permute-start = (bf16[3,256,128]{2,1,0:T(8,128)(2,1)S(1)}, bf16[3,256,128]{2,1,0:T(8,128)(2,1)S(1)}, u32[]{:S(2)}, u32[]{:S(2)}) collective-permute-start(bf16[3,256,128]{2,1,0:T(8,128)(2,1)S(1)} %pad_maximum_fusion.1), channel_id=1, source_target_pairs={{0,8},{4,12},{8,0},{12,4},{16,24},{20,28},{24,16},{28,20},{1,9},{5... | collective-permute-start | bytes 589832 | tf_op jit(solution)/shard_map/ppermute | solution.py:170
  9.8 28.5 %copy-start = (bf16[4,128,2048]{2,1,0:T(8,128)(2,1)S(1)}, bf16[4,128,2048]{2,1,0:T(8,128)(2,1)}, u32[]{:S(2)}) copy-start(bf16[4,128,2048]{2,1,0:T(8,128)(2,1)} %weight.3) | copy-start | bytes 6291460
  9.8 9.7 %collective-permute-start.2 = (bf16[3,256,128]{2,1,0:T(8,128)(2,1)S(1)}, bf16[3,256,128]{2,1,0:T(8,128)(2,1)S(1)}, u32[]{:S(2)}, u32[]{:S(2)}) collective-permute-start(bf16[3,256,128]{2,1,0:T(8,128)(2,1)S(1)} %pad_maximum_fusion.3), channel_id=1, source_target_pairs={{0,24},{4,28},{8,16},{12,20},{16,8},{20,12},{24,0},{28,4},{1,25},{... | collective-permute-start | bytes 589832 | tf_op jit(solution)/shard_map/ppermute | solution.py:170
  14.5 5.0 %collective-permute-start.3 = (bf16[2,256,128]{2,1,0:T(8,128)(2,1)S(1)}, bf16[2,256,128]{2,1,0:T(8,128)(2,1)S(1)}, u32[]{:S(2)}, u32[]{:S(2)}) collective-permute-start(bf16[2,256,128]{2,1,0:T(8,128)(2,1)S(1)} %pad_maximum_fusion.4), channel_id=1, source_target_pairs={{0,4},{4,0},{8,12},{12,8},{16,20},{20,16},{24,28},{28,24},{1,5},{5... | collective-permute-start | bytes 393224 | tf_op jit(solution)/shard_map/ppermute | solution.py:173
  16.1 8.1 %collective-permute-start.5 = (bf16[2,256,128]{2,1,0:T(8,128)(2,1)S(1)}, bf16[2,256,128]{2,1,0:T(8,128)(2,1)S(1)}, u32[]{:S(2)}, u32[]{:S(2)}) collective-permute-start(bf16[2,256,128]{2,1,0:T(8,128)(2,1)S(1)} %slice.47), channel_id=1, source_target_pairs={{0,4},{4,0},{8,12},{12,8},{16,20},{20,16},{24,28},{28,24},{1,5},{5... | collective-permute-start | bytes 393224 | tf_op jit(solution)/shard_map/ppermute | solution.py:173
  19.5 6.0 %collective-permute-start.4 = (bf16[2,256,128]{2,1,0:T(8,128)(2,1)S(1)}, bf16[2,256,128]{2,1,0:T(8,128)(2,1)S(1)}, u32[]{:S(2)}, u32[]{:S(2)}) collective-permute-start(bf16[2,256,128]{2,1,0:T(8,128)(2,1)S(1)} %slice.46), channel_id=1, source_target_pairs={{0,4},{4,0},{8,12},{12,8},{16,20},{20,16},{24,28},{28,24},{1,5},{5... | collective-permute-start | bytes 393224 | tf_op jit(solution)/shard_map/ppermute | solution.py:173
  19.6 6.0 %collective-permute-start.6 = (bf16[2,256,128]{2,1,0:T(8,128)(2,1)S(1)}, bf16[2,256,128]{2,1,0:T(8,128)(2,1)S(1)}, u32[]{:S(2)}, u32[]{:S(2)}) collective-permute-start(bf16[2,256,128]{2,1,0:T(8,128)(2,1)S(1)} %slice.48), channel_id=1, source_target_pairs={{0,4},{4,0},{8,12},{12,8},{16,20},{20,16},{24,28},{28,24},{1,5},{5... | collective-permute-start | bytes 393224 | tf_op jit(solution)/shard_map/ppermute | solution.py:173
  20.2 20.2 %collective-permute-start.15 = (bf16[256,512]{1,0:T(8,128)(2,1)S(1)}, bf16[256,512]{1,0:T(8,128)(2,1)S(1)}, u32[]{:S(2)}, u32[]{:S(2)}) collective-permute-start(bf16[256,512]{1,0:T(8,128)(2,1)S(1)} %copy-done.1), channel_id=1, source_target_pairs={{0,1},{1,0},{2,3},{3,2},{4,5},{5,4},{6,7},{7,6},{8,9},{9,8},{10,11... | collective-permute-start | bytes 786440 | tf_op jit(solution)/shard_map/ppermute | solution.py:188
  21.1 19.3 %collective-permute-start.19 = (bf16[256,512]{1,0:T(8,128)(2,1)S(1)}, bf16[256,512]{1,0:T(8,128)(2,1)S(1)}, u32[]{:S(2)}, u32[]{:S(2)}) collective-permute-start(bf16[256,512]{1,0:T(8,128)(2,1)S(1)} %collective-permute-done.16.refs_2_), channel_id=1, source_target_pairs={{2,3},{1,0},{6,7},{5,4},{10,11},{9,8},{14,15},{13,12},{18,19},{17,... | collective-permute-start | bytes 786440 | tf_op jit(solution)/shard_map/ppermute | solution.py:188
  24.2 16.2 %collective-permute-start.18 = (bf16[256,512]{1,0:T(8,128)(2,1)S(1)}, bf16[256,512]{1,0:T(8,128)(2,1)S(1)}, u32[]{:S(2)}, u32[]{:S(2)}) collective-permute-start(bf16[256,512]{1,0:T(8,128)(2,1)S(1)} %collective-permute-done.17.refs_4_), channel_id=1, source_target_pairs={{2,3},{1,0},{6,7},{5,4},{10,11},{9,8},{14,15},{13,12},{18,19},{17,... | collective-permute-start | bytes 786440 | tf_op jit(solution)/shard_map/ppermute | solution.py:188
  28.8 5.2 %collective-permute-start.9 = (bf16[256,128]{1,0:T(8,128)(2,1)S(1)}, bf16[256,128]{1,0:T(8,128)(2,1)S(1)}, u32[]{:S(2)}, u32[]{:S(2)}) collective-permute-start(bf16[256,128]{1,0:T(8,128)(2,1)S(1)} %get-tuple-element.44), channel_id=1, source_target_pairs={{0,24},{4,28},{8,16},{12,20},{16,8},{20,12},{24,0},{28,4},{1,25},{... | collective-permute-start | bytes 196616 | tf_op jit(solution)/shard_map/ppermute | solution.py:170
  30.3 5.3 %collective-permute-start.8 = (bf16[256,128]{1,0:T(8,128)(2,1)S(1)}, bf16[256,128]{1,0:T(8,128)(2,1)S(1)}, u32[]{:S(2)}, u32[]{:S(2)}) collective-permute-start(bf16[256,128]{1,0:T(8,128)(2,1)S(1)} %get-tuple-element.45), channel_id=1, source_target_pairs={{0,16},{4,20},{8,24},{12,28},{16,0},{20,4},{24,8},{28,12},{1,17},{... | collective-permute-start | bytes 196616 | tf_op jit(solution)/shard_map/ppermute | solution.py:170
  34.0 4.3 %collective-permute-start.7 = (bf16[256,128]{1,0:T(8,128)(2,1)S(1)}, bf16[256,128]{1,0:T(8,128)(2,1)S(1)}, u32[]{:S(2)}, u32[]{:S(2)}) collective-permute-start(bf16[256,128]{1,0:T(8,128)(2,1)S(1)} %get-tuple-element.46), channel_id=1, source_target_pairs={{0,8},{4,12},{8,0},{12,4},{16,24},{20,28},{24,16},{28,20},{1,9},{5... | collective-permute-start | bytes 196616 | tf_op jit(solution)/shard_map/ppermute | solution.py:170
  39.1 13.2 %collective-permute-start.13 = (bf16[256,512]{1,0:T(8,128)(2,1)S(1)}, bf16[256,512]{1,0:T(8,128)(2,1)S(1)}, u32[]{:S(2)}, u32[]{:S(2)}) collective-permute-start(bf16[256,512]{1,0:T(8,128)(2,1)S(1)} %get-tuple-element.25), channel_id=1, source_target_pairs={{3,2},{0,1},{7,6},{4,5},{11,10},{8,9},{15,14},{12,13},{19,18},{16,... | collective-permute-start | bytes 786440 | tf_op jit(solution)/shard_map/ppermute | solution.py:188
  41.2 6.2 %collective-permute-start.22 = (bf16[256,128]{1,0:T(8,128)(2,1)S(1)}, bf16[256,128]{1,0:T(8,128)(2,1)S(1)}, u32[]{:S(2)}, u32[]{:S(2)}) collective-permute-start(bf16[256,128]{1,0:T(8,128)(2,1)S(1)} %get-tuple-element.40), channel_id=1, source_target_pairs={{0,24},{4,28},{8,16},{12,20},{16,8},{20,12},{24,0},{28,4},{1,25},{... | collective-permute-start | bytes 196616 | tf_op jit(solution)/shard_map/ppermute | solution.py:170
  42.7 6.0 %collective-permute-start.21 = (bf16[256,128]{1,0:T(8,128)(2,1)S(1)}, bf16[256,128]{1,0:T(8,128)(2,1)S(1)}, u32[]{:S(2)}, u32[]{:S(2)}) collective-permute-start(bf16[256,128]{1,0:T(8,128)(2,1)S(1)} %get-tuple-element.41), channel_id=1, source_target_pairs={{0,16},{4,20},{8,24},{12,28},{16,0},{20,4},{24,8},{28,12},{1,17},{... | collective-permute-start | bytes 196616 | tf_op jit(solution)/shard_map/ppermute | solution.py:170
  44.3 4.4 %collective-permute-start.20 = (bf16[256,128]{1,0:T(8,128)(2,1)S(1)}, bf16[256,128]{1,0:T(8,128)(2,1)S(1)}, u32[]{:S(2)}, u32[]{:S(2)}) collective-permute-start(bf16[256,128]{1,0:T(8,128)(2,1)S(1)} %get-tuple-element.42), channel_id=1, source_target_pairs={{0,8},{4,12},{8,0},{12,4},{16,24},{20,28},{24,16},{28,20},{1,9},{5... | collective-permute-start | bytes 196616 | tf_op jit(solution)/shard_map/ppermute | solution.py:170
  44.8 19.2 %collective-permute-start.10 = (bf16[256,512]{1,0:T(8,128)(2,1)S(1)}, bf16[256,512]{1,0:T(8,128)(2,1)S(1)}, u32[]{:S(2)}, u32[]{:S(2)}) collective-permute-start(bf16[256,512]{1,0:T(8,128)(2,1)S(1)} %get-tuple-element.24), channel_id=1, source_target_pairs={{0,1},{1,0},{2,3},{3,2},{4,5},{5,4},{6,7},{7,6},{8,9},{9,8},{10,11... | collective-permute-start | bytes 786440 | tf_op jit(solution)/shard_map/ppermute | solution.py:188
  47.4 11.0 %collective-permute-start.11 = (bf16[256,512]{1,0:T(8,128)(2,1)S(1)}, bf16[256,512]{1,0:T(8,128)(2,1)S(1)}, u32[]{:S(2)}, u32[]{:S(2)}) collective-permute-start(bf16[256,512]{1,0:T(8,128)(2,1)S(1)} %get-tuple-element.26), channel_id=1, source_target_pairs={{3,2},{0,1},{7,6},{4,5},{11,10},{8,9},{15,14},{12,13},{19,18},{16,... | collective-permute-start | bytes 786440 | tf_op jit(solution)/shard_map/ppermute | solution.py:188
  52.2 9.6 %collective-permute-start.23 = (bf16[4,2,256,128]{3,2,1,0:T(8,128)(2,1)S(1)}, bf16[4,2,256,128]{3,2,1,0:T(8,128)(2,1)S(1)}, u32[]{:S(2)}, u32[]{:S(2)}) collective-permute-start(bf16[4,2,256,128]{3,2,1,0:T(8,128)(2,1)S(1)} %get-tuple-element.32), channel_id=1, source_target_pairs={{0,4},{4,0},{8,12},{12,8},{16,20},{20,16},{24,28},{28,24},{1,5},{5... | collective-permute-start | bytes 1572872 | tf_op jit(solution)/shard_map/ppermute | solution.py:173
  53.0 12.4 %collective-permute-start.14 = (bf16[256,512]{1,0:T(8,128)(2,1)}, bf16[256,512]{1,0:T(8,128)(2,1)S(1)}, u32[]{:S(2)}, u32[]{:S(2)}) collective-permute-start(bf16[256,512]{1,0:T(8,128)(2,1)} %add_convert_fusion.1), channel_id=1, source_target_pairs={{2,0},{1,3},{6,4},{5,7},{10,8},{9,11},{14,12},{13,15},{18,16},{17,... | collective-permute-start | bytes 786440 | tf_op jit(solution)/shard_map/ppermute | solution.py:188
  59.1 12.5 %collective-permute-start.12 = (bf16[256,512]{1,0:T(8,128)(2,1)}, bf16[256,512]{1,0:T(8,128)(2,1)}, u32[]{:S(2)}, u32[]{:S(2)}) collective-permute-start(bf16[256,512]{1,0:T(8,128)(2,1)} %add_convert_fusion.2), channel_id=1, source_target_pairs={{2,1},{1,2},{6,5},{5,6},{10,9},{9,10},{14,13},{13,14},{18,17},{17,... | collective-permute-start | bytes 786440 | tf_op jit(solution)/shard_map/ppermute | solution.py:188
  61.9 11.6 %collective-permute-start.24 = (bf16[3,256,128]{2,1,0:T(8,128)(2,1)S(1)}, bf16[3,256,128]{2,1,0:T(8,128)(2,1)S(1)}, u32[]{:S(2)}, u32[]{:S(2)}) collective-permute-start(bf16[3,256,128]{2,1,0:T(8,128)(2,1)S(1)} %get-tuple-element.34), channel_id=1, source_target_pairs={{0,8},{4,12},{8,0},{12,4},{16,24},{20,28},{24,16},{28,20},{1,9},{5... | collective-permute-start | bytes 589832 | tf_op jit(solution)/shard_map/ppermute | solution.py:170
  63.5 10.7 %collective-permute-start.25 = (bf16[3,256,128]{2,1,0:T(8,128)(2,1)S(1)}, bf16[3,256,128]{2,1,0:T(8,128)(2,1)S(1)}, u32[]{:S(2)}, u32[]{:S(2)}) collective-permute-start(bf16[3,256,128]{2,1,0:T(8,128)(2,1)S(1)} %get-tuple-element.35), channel_id=1, source_target_pairs={{0,16},{4,20},{8,24},{12,28},{16,0},{20,4},{24,8},{28,12},{1,17},{... | collective-permute-start | bytes 589832 | tf_op jit(solution)/shard_map/ppermute | solution.py:170
  63.9 10.3 %collective-permute-start.26 = (bf16[3,256,128]{2,1,0:T(8,128)(2,1)S(1)}, bf16[3,256,128]{2,1,0:T(8,128)(2,1)S(1)}, u32[]{:S(2)}, u32[]{:S(2)}) collective-permute-start(bf16[3,256,128]{2,1,0:T(8,128)(2,1)S(1)} %get-tuple-element.36), channel_id=1, source_target_pairs={{0,24},{4,28},{8,16},{12,20},{16,8},{20,12},{24,0},{28,4},{1,25},{... | collective-permute-start | bytes 589832 | tf_op jit(solution)/shard_map/ppermute | solution.py:170

commit v3 on v2

--- a/solution.py
+++ b/solution.py
@@ -74,7 +74,7 @@
     chip = chip_index()
     for d in range(chips):
         p = perm[chip, chip ^ d] ^ chip
-        grad = arrived[d][...]
+        grad = arrived[d][1]
         grads[d] = grad
         delta = jnp.sum(grad.astype(F32) * attended[d].astype(F32), axis=1, keepdims=True)
         total = None
@@ -104,13 +104,13 @@
 
 
 def project_body(chips, groups, weight, *refs):
-    attended, outs, joined = refs[:chips], refs[chips : chips + groups], refs[chips + groups]
+    incoming, outs, joined = refs[:chips], refs[chips : chips + groups], refs[chips + groups]
     chip = chip_index()
     level = lax.axis_index("head")
-    width = attended[0].shape[1]
+    width = incoming[0].shape[2]
     for d in range(chips):
         lanes = pl.ds(pl.multiple_of((chip ^ d) * width, width), width)
-        joined[:, lanes] = attended[d][...]
+        joined[:, lanes] = incoming[d][0]
     rows = joined[...]
     for j in range(groups):
         columns = outs[j].shape[1]
@@ -119,24 +119,28 @@
         outs[j][...] = dot(rows, term).astype(LOW)
 
 
-def grad_body(chips, groups, weight, *refs):
-    slices, out = refs[:-1], refs[-1]
+def grad_body(chips, groups, weight, attended, *refs):
+    slices, outs = refs[:groups], refs[groups:]
     chip = chip_index()
     level = lax.axis_index("head")
-    inner = (level > 0) & (level < groups - 1)
-    width = out.shape[2]
+    width = attended.shape[2]
     total = None
     for j in range(groups):
-        if j < 2:
-            block = slices[j][...]
-        else:
-            block = jnp.where(inner, slices[2 * j - 2][...], slices[2 * j - 1][...])
+        block = slices[j][...]
         columns = block.shape[1]
         lanes = pl.ds(pl.multiple_of((level ^ j) * columns, columns), columns)
         term = dot(block, weight[:, :, lanes].reshape(chips * width, columns), NT)
         total = term if total is None else total + term
-    for h in range(chips):
-        out[h ^ chip] = total[:, h * width : (h + 1) * width].astype(LOW)
+    total = total.astype(LOW)
+    for d in range(chips):
+        outs[d][0] = attended[d]
+    for c in range(chips):
+
+        @pl.when(chip == c)
+        def _():
+            for d in range(chips):
+                h = c ^ d
+                outs[d][1] = total[:, h * width : (h + 1) * width]
 
 
 def merge_body(chips, query_grad, own_part, arrived, *outs):
@@ -172,6 +176,9 @@
     def to_sibling(array):
         return lax.ppermute(array, "seq", [(i, i ^ 1) for i in range(devices)])
 
+    def together(*arrays):
+        return list(lax.optimization_barrier(arrays))
+
     def exchange(pieces):
         return [pieces[0]] + [to_chip(pieces[d], d) for d in range(1, chips)]
 
@@ -187,11 +194,17 @@
     def along(array, pairs):
         return lax.ppermute(array, "head", pairs)
 
-    skip_in = along(out_cotangent, [(0, 2), (3, 1)])
-    pair_in = along(out_cotangent, [(0, 1), (1, 0), (2, 3), (3, 2)])
-    middle_in = along(out_cotangent, [(1, 2), (2, 1)])
-    pieces = exchange([head_piece(d) for d in range(chips)])
-    siblings = [to_sibling(piece[:2]) for piece in pieces]
+    def across(array, j):
+        return along(array, [(i, i ^ j) for i in range(groups)])
+
+    twice = across(out_cotangent, 2)
+    once = across(out_cotangent, 1)
+    pieces = [head_piece(d) for d in range(chips)]
+    siblings = [to_sibling(pieces[0][:2])]
+    pieces = exchange(pieces)
+    *pieces[1:], twice, once = together(*pieces[1:], twice, once)
+    slices = [out_cotangent, once, twice, across(twice, 1)]
+    siblings += [to_sibling(piece[:2]) for piece in pieces[1:]]
     tile = rows * width
     scores = chips * rows * 4 * rows
     attended, probs, keys_values, query_rows = call(
@@ -210,41 +223,31 @@
         smem=(0,),
     )
     weight_bytes = 2 * heads * width * features
-    far_in = along(skip_in, [(2, 3), (1, 0)])
-    near_in = along(middle_in, [(2, 3), (1, 0)])
-    grad_att = call(
+    *slices, attended = together(*slices, attended)
+    outgoing = call(
         functools.partial(grad_body, chips, groups),
-        shape((chips, rows, width), LOW),
+        tuple(shape((2, rows, width), LOW) for _ in range(chips)),
         out_weight,
-        out_cotangent,
-        pair_in,
-        skip_in,
-        near_in,
-        middle_in,
-        far_in,
+        attended,
+        *slices,
         flops=2 * rows * heads * width * features,
-        moved=weight_bytes + 2 * rows * features + 2 * chips * tile,
-    )
-    grads = exchange([grad_att[d] for d in range(chips)])
-    own_attended = exchange([attended[d] for d in range(chips)])
+        moved=weight_bytes + 2 * rows * features + 6 * chips * tile,
+    )
+    incoming = together(*exchange(outgoing))
     parts = call(
         functools.partial(project_body, chips, groups),
         tuple(shape((rows, columns), LOW) for _ in range(groups)),
         out_weight,
-        *own_attended,
+        *incoming,
         flops=2 * rows * heads * width * features,
-        moved=weight_bytes + 2 * rows * features + 2 * chips * tile,
+        moved=weight_bytes + 2 * rows * features + 4 * chips * tile,
         scratch=[pltpu.VMEM((rows, heads * width), LOW)],
     )
-
-    def plus(a, b):
-        return (a.astype(F32) + b.astype(F32)).astype(LOW)
-
-    end_far = along(parts[3], [(3, 2), (0, 1)])
-    end_near = along(parts[2], [(3, 2), (0, 1)])
-    pair_out = along(parts[1], [(0, 1), (1, 0), (2, 3), (3, 2)])
-    skip_out = along(plus(parts[2], end_far), [(2, 0), (1, 3)])
-    middle_out = along(plus(parts[3], end_near), [(2, 1), (1, 2)])
+    halfway = across(parts[3], 1)
+    neighbour = across(parts[1], 1)
+    halfway = (halfway.astype(F32) + parts[2].astype(F32)).astype(LOW)
+    summands = [parts[0], neighbour, across(halfway, 2)]
+    incoming[0] = together(incoming[0], parts[0])[0]
     query_grad, own_part, sibling_part = call(
         functools.partial(backward_body, chips, rows, scale),
         (
@@ -253,7 +256,7 @@
             shape((chips, 2, rows, width), LOW),
         ),
         block_perm,
-        *grads,
+        *incoming,
         attended,
         probs,
         keys_values,
@@ -282,10 +285,7 @@
         *returned,
         moved=2 * 6 * chips * tile,
     )
-    level = lax.axis_index("head")
-    inner = (level > 0) & (level < groups - 1)
-    passed = jnp.where(inner, middle_out, skip_out)
-    projected = parts[0].astype(F32) + pair_out.astype(F32) + passed.astype(F32)
+    projected = sum(term.astype(F32) for term in summands)
     return (projected.astype(LOW), *gradients)
 
 
@@ -399,7 +399,7 @@
 
 def per_device(*arrays):
     chips = lax.axis_size("seq") // 2
-    square = chips == arrays[0].shape[0] == lax.axis_size("head") == 4
+    square = chips == arrays[0].shape[0]
     return (by_heads if square else by_routing)(*arrays)
 
 

time: 75.5 us -> 60.4 us (0.80)
  the two profiles are of different devices: /device:TPU:12 before, /device:TPU:0 now
where the time goes in v3:
time: 60.4 us; the launch traced here: 60.2 us
  waiting for transfers between devices  26.5 us (44%)
  starting transfers between devices  20.6 us (34%)
  Pallas kernels  9.26 us (15%)
  local copies, waits for them, and re-layouts  2.12 us (4%)
  other arithmetic  0.98 us (2%)
  between operations  0.77 us (1%)
    ppermute x9, waiting for transfers between devices, to_chip(): return lax.ppermute(array, 'seq', [(i, i ^ 2 * d) for i in range(devices)])  13.6 us
    ppermute x6, waiting for transfers between devices, along(): return lax.ppermute(array, 'head', pairs)  11.9 us
    ppermute x9, starting transfers between devices, to_chip(): return lax.ppermute(array, 'seq', [(i, i ^ 2 * d) for i in range(devices)])  10.8 us
    pallas_call x6, Pallas kernels, call(): pl.pallas_call(body, out_shape=outs, in_specs=[scalar if i in smem else v...  9.26 us
    ppermute x6, starting transfers between devices, along(): return lax.ppermute(array, 'head', pairs)  8.42 us
    dynamic_slice x2, local copies, waits for them, and re-layouts, head_piece(): lax.dynamic_index_in_dim(a, h, 0, keepdims=False)  2.08 us
    ppermute x5, starting transfers between devices, to_sibling(): return lax.ppermute(array, 'seq', [(i, i ^ 1) for i in range(devices)])  1.34 us
  transfers between devices with their start and end apart: 20, of which 13 were waited for; matrix products, arithmetic and copies ran while one was open for 5% of the time, Pallas kernels for 11%

profile of v3, /device:TPU:0, one launch (start us, length us, event | category | flops | bytes accessed | tf_op | source)
XLA Modules:
  0.0 60.2 jit_solution(7705622639431030948)
XLA Ops:
  0.6 4.1 %collective-permute-start.3 = (bf16[256,512]{1,0:T(8,128)(2,1)}, bf16[256,512]{1,0:T(8,128)(2,1)S(1)}, u32[]{:S(2)}, u32[]{:S(2)}) collective-permute-start(bf16[256,512]{1,0:T(8,128)(2,1)} %refs_0_), channel_id=1, source_target_pairs={{0,2},{1,3},{2,0},{3,1},{4,6},{5,7},{6,4},{7,5},{8,10},{9,11},{10,... | collective-permute-start | bytes 786440 | tf_op jit(solution)/shard_map/ppermute | solution.py:195
  4.7 1.6 %collective-permute-start.4 = (bf16[256,512]{1,0:T(8,128)(2,1)}, bf16[256,512]{1,0:T(8,128)(2,1)S(1)}, u32[]{:S(2)}, u32[]{:S(2)}) collective-permute-start(bf16[256,512]{1,0:T(8,128)(2,1)} %refs_0_), channel_id=1, source_target_pairs={{0,1},{1,0},{2,3},{3,2},{4,5},{5,4},{6,7},{7,6},{8,9},{9,8},{10,11... | collective-permute-start | bytes 786440 | tf_op jit(solution)/shard_map/ppermute | solution.py:195
  6.3 0.0 copy-start.2
  6.3 1.0 %constant_dynamic-slice_fusion.2 = (bf16[1,256,128]{2,1,0:T(8,128)(2,1)S(1)}, bf16[1,256,128]{2,1,0:T(8,128)(2,1)S(1)}, bf16[1,256,128]{2,1,0:T(8,128)(2,1)S(1)}, bf16[1,256,128]{2,1,0:T(8,128)(2,1)S(1)}) fusion(bf16[4,256,128]{2,1,0:T(8,128)(2,1)} %param.7, s32[]{:T(128)S(6)} %select_n.30, s32[]{:T(128)S(6)} %select_n.28, s32[]{:T(128)S(6)} %select_n.27, ...), kind=kLoop, calls=%fused_computation.9 | loop fusion | bytes 524304 | tf_op jit(solution)/shard_map/jit(dynamic_index_in_dim)/dynamic_slice | solution.py:189
  7.3 1.1 %constant_dynamic-slice_fusion = (bf16[1,256,128]{2,1,0:T(8,128)(2,1)S(1)}, bf16[1,256,128]{2,1,0:T(8,128)(2,1)S(1)}, bf16[1,256,128]{2,1,0:T(8,128)(2,1)S(1)}, ...) fusion(bf16[4,256,128]{2,1,0:T(8,128)(2,1)} %param.6, ...), kind=kLoop, calls=%fused_computation.7 | loop fusion | bytes 1048592 | tf_op jit(solution)/shard_map/jit(dynamic_index_in_dim)/dynamic_slice | solution.py:189
  8.4 1.6 %collective-permute-start = (bf16[3,256,128]{2,1,0:T(8,128)(2,1)S(1)}, bf16[3,256,128]{2,1,0:T(8,128)(2,1)S(1)}, u32[]{:S(2)}, u32[]{:S(2)}) collective-permute-start(bf16[3,256,128]{2,1,0:T(8,128)(2,1)S(1)} %pad_maximum_fusion), channel_id=1, source_target_pairs={{0,8},{4,12},{8,0},{12,4},{16,24},{20,28},{24,16},{28,20},{1,9},{5... | collective-permute-start | bytes 589832 | tf_op jit(solution)/shard_map/ppermute | solution.py:174
  10.0 0.0 copy-start
  10.0 0.0 copy-start.1
  10.0 1.6 %collective-permute-start.1 = (bf16[3,256,128]{2,1,0:T(8,128)(2,1)S(1)}, bf16[3,256,128]{2,1,0:T(8,128)(2,1)S(1)}, u32[]{:S(2)}, u32[]{:S(2)}) collective-permute-start(bf16[3,256,128]{2,1,0:T(8,128)(2,1)S(1)} %pad_maximum_fusion.1), channel_id=1, source_target_pairs={{0,16},{4,20},{8,24},{12,28},{16,0},{20,4},{24,8},{28,12},{1,17},{... | collective-permute-start | bytes 589832 | tf_op jit(solution)/shard_map/ppermute | solution.py:174
  11.6 0.5 collective-permute-start.2
  12.2 4.0 %collective-permute-done.refs_1_ = bf16[3,256,128]{2,1,0:T(8,128)(2,1)S(1)} collective-permute-done((bf16[3,256,128]{2,1,0:T(8,128)(2,1)S(1)}, bf16[3,256,128]{2,1,0:T(8,128)(2,1)S(1)}, u32[]{:S(2)}, u32[]{:S(2)}) %collective-permute-start) | collective-permute-done | bytes 196640 | tf_op jit(solution)/shard_map/ppermute | solution.py:174
  16.2 3.9 %collective-permute-done.1.refs_2_ = bf16[3,256,128]{2,1,0:T(8,128)(2,1)S(1)} collective-permute-done((bf16[3,256,128]{2,1,0:T(8,128)(2,1)S(1)}, bf16[3,256,128]{2,1,0:T(8,128)(2,1)S(1)}, u32[]{:S(2)}, u32[]{:S(2)}) %collective-permute-start.1) | collective-permute-done | bytes 196640 | tf_op jit(solution)/shard_map/ppermute | solution.py:174
  20.1 0.0 collective-permute-done.2.refs_3_
  20.1 0.0 collective-permute-done.3.refs_2_
  20.1 0.0 collective-permute-done.4.refs_1_
  20.1 0.5 collective-permute-start.5
  20.6 0.1 collective-permute-start.6
  20.7 0.6 collective-permute-start.7
  21.3 0.1 collective-permute-start.8
  21.4 0.6 collective-permute-start.9
  22.0 0.1 collective-permute-done.6.refs_4_
  22.1 0.2 collective-permute-done.7.refs_5_
  22.3 0.4 collective-permute-done.8.refs_6_
  22.7 0.2 collective-permute-done.9.refs_7_
  23.0 0.0 copy-done.2
  23.0 3.2 %shard_map.93 = (bf16[4,256,128]{2,1,0:T(8,128)(2,1)S(1)}, bf16[4,256,1024]{2,1,0:T(8,128)(2,1)S(1)}, bf16[4,2,512,128]{3,2,1,0:T(8,128)(2,1)S(1)}, bf16[4,256,128]{2,1,0:T(8,128)(2,1)S(1)}) custom-call(s32[4,4]{1,0:T(4,128)S(1)} %copy-done.2, bf16[3,256,128]{2,1,0:T(8,128)(2,1)S(1)} %pad_maximum_fusion.3.refs_0_, ...), custom_call_target="tpu_custom_call" | custom-call | flops 536870912 | bytes 5767168 | tf_op jit(solution)/shard_map/pallas_call | solution.py:29
  26.2 0.4 collective-permute-done.5.refs_3_
  26.5 0.0 copy-done
  26.6 0.0 copy-done.1
  26.6 0.8 %shard_map.94 = (bf16[2,256,128]{2,1,0:T(8,128)(2,1)S(1)}, bf16[2,256,128]{2,1,0:T(8,128)(2,1)S(1)}, bf16[2,256,128]{2,1,0:T(8,128)(2,1)S(1)}, bf16[2,256,128]{2,1,0:T(8,128)(2,1)S(1)}) custom-call(bf16[4,128,2048]{2,1,0:T(8,128)(2,1)S(1)} %copy-done, bf16[4,256,128]{2,1,0:T(8,128)(2,1)S(1)} %get-tuple-element.47.attended.refs_4_, ...), custom_call_target="tpu_custom_call" | custom-call | flops 536870912 | bytes 3932160 | tf_op jit(solution)/shard_map/pallas_call | solution.py:29
  27.3 1.3 %collective-permute-start.10 = (bf16[2,256,128]{2,1,0:T(8,128)(2,1)S(1)}, bf16[2,256,128]{2,1,0:T(8,128)(2,1)S(1)}, u32[]{:S(2)}, u32[]{:S(2)}) collective-permute-start(bf16[2,256,128]{2,1,0:T(8,128)(2,1)S(1)} %get-tuple-element.53), channel_id=1, source_target_pairs={{0,8},{4,12},{8,0},{12,4},{16,24},{20,28},{24,16},{28,20},{1,9},{5... | collective-permute-start | bytes 393224 | tf_op jit(solution)/shard_map/ppermute | solution.py:174
  28.7 0.8 %collective-permute-start.11 = (bf16[2,256,128]{2,1,0:T(8,128)(2,1)S(1)}, bf16[2,256,128]{2,1,0:T(8,128)(2,1)S(1)}, u32[]{:S(2)}, u32[]{:S(2)}) collective-permute-start(bf16[2,256,128]{2,1,0:T(8,128)(2,1)S(1)} %get-tuple-element.54), channel_id=1, source_target_pairs={{0,16},{4,20},{8,24},{12,28},{16,0},{20,4},{24,8},{28,12},{1,17},{... | collective-permute-start | bytes 393224 | tf_op jit(solution)/shard_map/ppermute | solution.py:174
  29.5 1.4 %collective-permute-start.12 = (bf16[2,256,128]{2,1,0:T(8,128)(2,1)S(1)}, bf16[2,256,128]{2,1,0:T(8,128)(2,1)S(1)}, u32[]{:S(2)}, u32[]{:S(2)}) collective-permute-start(bf16[2,256,128]{2,1,0:T(8,128)(2,1)S(1)} %get-tuple-element.55), channel_id=1, source_target_pairs={{0,24},{4,28},{8,16},{12,20},{16,8},{20,12},{24,0},{28,4},{1,25},{... | collective-permute-start | bytes 393224 | tf_op jit(solution)/shard_map/ppermute | solution.py:174
  30.9 2.8 %collective-permute-done.10.refs_1_ = bf16[2,256,128]{2,1,0:T(8,128)(2,1)S(1)} collective-permute-done((bf16[2,256,128]{2,1,0:T(8,128)(2,1)S(1)}, bf16[2,256,128]{2,1,0:T(8,128)(2,1)S(1)}, u32[]{:S(2)}, u32[]{:S(2)}) %collective-permute-start.10) | collective-permute-done | bytes 131104 | tf_op jit(solution)/shard_map/ppermute | solution.py:174
  33.7 1.3 %collective-permute-done.11.refs_2_ = bf16[2,256,128]{2,1,0:T(8,128)(2,1)S(1)} collective-permute-done((bf16[2,256,128]{2,1,0:T(8,128)(2,1)S(1)}, bf16[2,256,128]{2,1,0:T(8,128)(2,1)S(1)}, u32[]{:S(2)}, u32[]{:S(2)}) %collective-permute-start.11) | collective-permute-done | bytes 131104 | tf_op jit(solution)/shard_map/ppermute | solution.py:174
  34.9 1.6 %collective-permute-done.12.refs_3_ = bf16[2,256,128]{2,1,0:T(8,128)(2,1)S(1)} collective-permute-done((bf16[2,256,128]{2,1,0:T(8,128)(2,1)S(1)}, bf16[2,256,128]{2,1,0:T(8,128)(2,1)S(1)}, u32[]{:S(2)}, u32[]{:S(2)}) %collective-permute-start.12) | collective-permute-done | bytes 131104 | tf_op jit(solution)/shard_map/ppermute | solution.py:174
  36.6 0.8 %shard_map.95 = (bf16[256,512]{1,0:T(8,128)(2,1)S(1)}, bf16[256,512]{1,0:T(8,128)(2,1)S(1)}, bf16[256,512]{1,0:T(8,128)(2,1)S(1)}, bf16[256,512]{1,0:T(8,128)(2,1)S(1)}) custom-call(bf16[4,128,2048]{2,1,0:T(8,128)(2,1)S(1)} %copy-done, bf16[2,256,128]{2,1,0:T(8,128)(2,1)S(1)} %get-tuple-element.64.refs_0_, ...), custom_call_target="tpu_custom_call" | custom-call | flops 536870912 | bytes 3670016 | tf_op jit(solution)/shard_map/pallas_call | solution.py:29
  37.3 1.7 %collective-permute-start.14 = (bf16[256,512]{1,0:T(8,128)(2,1)S(1)}, bf16[256,512]{1,0:T(8,128)(2,1)S(1)}, u32[]{:S(2)}, u32[]{:S(2)}) collective-permute-start(bf16[256,512]{1,0:T(8,128)(2,1)S(1)} %get-tuple-element.62), channel_id=1, source_target_pairs={{0,1},{1,0},{2,3},{3,2},{4,5},{5,4},{6,7},{7,6},{8,9},{9,8},{10,11... | collective-permute-start | bytes 786440 | tf_op jit(solution)/shard_map/ppermute | solution.py:195
  39.0 3.4 %shard_map.96 = (bf16[4,256,128]{2,1,0:T(8,128)(2,1)S(1)}, f32[4,2,256,128]{3,2,1,0:T(8,128)S(1)}, bf16[4,2,256,128]{3,2,1,0:T(8,128)(2,1)S(1)}) custom-call(s32[4,4]{1,0:T(4,128)S(1)} %copy-done.2, bf16[2,256,128]{2,1,0:T(8,128)(2,1)S(1)} %get-tuple-element.64.refs_0_, bf16[2,256,128]{2,1,0:T(8,128)(2,1)S(1)} %collective-permute-done.10.refs_1_, ...), custom_call_target="tpu_custom_call" | custom-call | flops 1073741824 | bytes 7340032 | tf_op jit(solution)/shard_map/pallas_call | solution.py:29
  42.4 0.1 collective-permute-start.16
  42.5 0.5 collective-permute-start.13
  43.0 2.0 %collective-permute-done.14 = bf16[256,512]{1,0:T(8,128)(2,1)S(1)} collective-permute-done((bf16[256,512]{1,0:T(8,128)(2,1)S(1)}, bf16[256,512]{1,0:T(8,128)(2,1)S(1)}, u32[]{:S(2)}, u32[]{:S(2)}) %collective-permute-start.14) | collective-permute-done | bytes 262176 | tf_op jit(solution)/shard_map/ppermute | solution.py:195
  45.0 0.1 add_convert_fusion.1
  45.1 0.1 collective-permute-start.15
  45.2 0.0 collective-permute-done.16.arrived
  45.2 0.1 shard_map.97
  45.3 0.9 %collective-permute-start.17 = (bf16[3,256,128]{2,1,0:T(8,128)(2,1)S(1)}, bf16[3,256,128]{2,1,0:T(8,128)(2,1)S(1)}, u32[]{:S(2)}, u32[]{:S(2)}) collective-permute-start(bf16[3,256,128]{2,1,0:T(8,128)(2,1)S(1)} %get-tuple-element.72), channel_id=1, source_target_pairs={{0,8},{4,12},{8,0},{12,4},{16,24},{20,28},{24,16},{28,20},{1,9},{5... | collective-permute-start | bytes 589832 | tf_op jit(solution)/shard_map/ppermute | solution.py:174
  46.2 0.8 %collective-permute-start.18 = (bf16[3,256,128]{2,1,0:T(8,128)(2,1)S(1)}, bf16[3,256,128]{2,1,0:T(8,128)(2,1)S(1)}, u32[]{:S(2)}, u32[]{:S(2)}) collective-permute-start(bf16[3,256,128]{2,1,0:T(8,128)(2,1)S(1)} %get-tuple-element.73), channel_id=1, source_target_pairs={{0,16},{4,20},{8,24},{12,28},{16,0},{20,4},{24,8},{28,12},{1,17},{... | collective-permute-start | bytes 589832 | tf_op jit(solution)/shard_map/ppermute | solution.py:174
  47.0 1.9 %collective-permute-start.19 = (bf16[3,256,128]{2,1,0:T(8,128)(2,1)S(1)}, bf16[3,256,128]{2,1,0:T(8,128)(2,1)S(1)}, u32[]{:S(2)}, u32[]{:S(2)}) collective-permute-start(bf16[3,256,128]{2,1,0:T(8,128)(2,1)S(1)} %get-tuple-element.74), channel_id=1, source_target_pairs={{0,24},{4,28},{8,16},{12,20},{16,8},{20,12},{24,0},{28,4},{1,25},{... | collective-permute-start | bytes 589832 | tf_op jit(solution)/shard_map/ppermute | solution.py:174
  48.9 7.2 %collective-permute-done.13 = bf16[256,512]{1,0:T(8,128)(2,1)S(1)} collective-permute-done((bf16[256,512]{1,0:T(8,128)(2,1)S(1)}, bf16[256,512]{1,0:T(8,128)(2,1)S(1)}, u32[]{:S(2)}, u32[]{:S(2)}) %collective-permute-start.13) | collective-permute-done | bytes 262176 | tf_op jit(solution)/shard_map/ppermute | solution.py:195
  56.0 2.4 %collective-permute-done.15 = bf16[256,512]{1,0:T(8,128)(2,1)S(1)} collective-permute-done((bf16[256,512]{1,0:T(8,128)(2,1)S(1)}, bf16[256,512]{1,0:T(8,128)(2,1)S(1)}, u32[]{:S(2)}, u32[]{:S(2)}) %collective-permute-start.15) | collective-permute-done | bytes 262176 | tf_op jit(solution)/shard_map/ppermute | solution.py:195
  58.4 0.8 %add_convert_fusion = bf16[256,512]{1,0:T(8,128)(2,1)} fusion(bf16[256,512]{1,0:T(8,128)(2,1)S(1)} %collective-permute-done.15, bf16[256,512]{1,0:T(8,128)(2,1)S(1)} %collective-permute-done.13, bf16[256,512]{1,0:T(8,128)(2,1)S(1)} %get-tuple-element.60), kind=kLoop, calls=%fused_computation | loop fusion | flops 786432 | bytes 1048576 | tf_op jit(solution)/shard_map/convert_element_type | solution.py:289
  59.2 0.0 collective-permute-done.17.refs_1_
  59.2 0.0 collective-permute-done.18.refs_2_
  59.2 0.0 collective-permute-done.19.refs_3_
  59.2 0.9 %shard_map.98 = (bf16[4,256,128]{2,1,0:T(8,128)(2,1)}, bf16[4,256,128]{2,1,0:T(8,128)(2,1)}, bf16[4,256,128]{2,1,0:T(8,128)(2,1)}) custom-call(bf16[3,256,128]{2,1,0:T(8,128)(2,1)S(1)} %get-tuple-element.71.refs_0_, bf16[3,256,128]{2,1,0:T(8,128)(2,1)S(1)} %collective-permute-done.17.refs_1_, bf16[3,256,128]{2,1,0:T(8,128)(2,1)S(1)} %collective-permute-done.18.refs_2_, ...), custom_call_target="tpu_custom_call" | custom-call | bytes 1572864 | tf_op jit(solution)/shard_map/pallas_call | solution.py:29
  (8 shorter events, 0.1 us)
Async XLA Ops:
  0.6 19.5 %collective-permute-start.3 = (bf16[256,512]{1,0:T(8,128)(2,1)}, bf16[256,512]{1,0:T(8,128)(2,1)S(1)}, u32[]{:S(2)}, u32[]{:S(2)}) collective-permute-start(bf16[256,512]{1,0:T(8,128)(2,1)} %refs_0_), channel_id=1, source_target_pairs={{0,2},{1,3},{2,0},{3,1},{4,6},{5,7},{6,4},{7,5},{8,10},{9,11},{10,... | collective-permute-start | bytes 786440 | tf_op jit(solution)/shard_map/ppermute | solution.py:195
  4.7 15.4 %collective-permute-start.4 = (bf16[256,512]{1,0:T(8,128)(2,1)}, bf16[256,512]{1,0:T(8,128)(2,1)S(1)}, u32[]{:S(2)}, u32[]{:S(2)}) collective-permute-start(bf16[256,512]{1,0:T(8,128)(2,1)} %refs_0_), channel_id=1, source_target_pairs={{0,1},{1,0},{2,3},{3,2},{4,5},{5,4},{6,7},{7,6},{8,9},{9,8},{10,11... | collective-permute-start | bytes 786440 | tf_op jit(solution)/shard_map/ppermute | solution.py:195
  6.3 16.6 %copy-start.2 = (s32[4,4]{1,0:T(4,128)S(1)}, s32[4,4]{1,0:T(4,128)}, u32[]{:S(2)}) copy-start(s32[4,4]{1,0:T(4,128)} %perm.3) | copy-start | bytes 196
  8.4 7.8 %collective-permute-start = (bf16[3,256,128]{2,1,0:T(8,128)(2,1)S(1)}, bf16[3,256,128]{2,1,0:T(8,128)(2,1)S(1)}, u32[]{:S(2)}, u32[]{:S(2)}) collective-permute-start(bf16[3,256,128]{2,1,0:T(8,128)(2,1)S(1)} %pad_maximum_fusion), channel_id=1, source_target_pairs={{0,8},{4,12},{8,0},{12,4},{16,24},{20,28},{24,16},{28,20},{1,9},{5... | collective-permute-start | bytes 589832 | tf_op jit(solution)/shard_map/ppermute | solution.py:174
  10.0 16.6 %copy-start = (bf16[4,128,2048]{2,1,0:T(8,128)(2,1)S(1)}, bf16[4,128,2048]{2,1,0:T(8,128)(2,1)}, u32[]{:S(2)}) copy-start(bf16[4,128,2048]{2,1,0:T(8,128)(2,1)} %weight.3) | copy-start | bytes 6291460
  10.0 16.6 %copy-start.1 = (bf16[256,512]{1,0:T(8,128)(2,1)S(1)}, bf16[256,512]{1,0:T(8,128)(2,1)}, u32[]{:S(2)}) copy-start(bf16[256,512]{1,0:T(8,128)(2,1)} %refs_0_) | copy-start | bytes 786436
  10.0 10.1 %collective-permute-start.1 = (bf16[3,256,128]{2,1,0:T(8,128)(2,1)S(1)}, bf16[3,256,128]{2,1,0:T(8,128)(2,1)S(1)}, u32[]{:S(2)}, u32[]{:S(2)}) collective-permute-start(bf16[3,256,128]{2,1,0:T(8,128)(2,1)S(1)} %pad_maximum_fusion.1), channel_id=1, source_target_pairs={{0,16},{4,20},{8,24},{12,28},{16,0},{20,4},{24,8},{28,12},{1,17},{... | collective-permute-start | bytes 589832 | tf_op jit(solution)/shard_map/ppermute | solution.py:174
  11.6 8.5 %collective-permute-start.2 = (bf16[3,256,128]{2,1,0:T(8,128)(2,1)S(1)}, bf16[3,256,128]{2,1,0:T(8,128)(2,1)S(1)}, u32[]{:S(2)}, u32[]{:S(2)}) collective-permute-start(bf16[3,256,128]{2,1,0:T(8,128)(2,1)S(1)} %pad_maximum_fusion.2), channel_id=1, source_target_pairs={{0,24},{4,28},{8,16},{12,20},{16,8},{20,12},{24,0},{28,4},{1,25},{... | collective-permute-start | bytes 589832 | tf_op jit(solution)/shard_map/ppermute | solution.py:174
  20.1 6.4 %collective-permute-start.5 = (bf16[256,512]{1,0:T(8,128)(2,1)S(1)}, bf16[256,512]{1,0:T(8,128)(2,1)S(1)}, u32[]{:S(2)}, u32[]{:S(2)}) collective-permute-start(bf16[256,512]{1,0:T(8,128)(2,1)S(1)} %collective-permute-done.3.refs_2_), channel_id=1, source_target_pairs={{0,1},{1,0},{2,3},{3,2},{4,5},{5,4},{6,7},{7,6},{8,9},{9,8},{10,11... | collective-permute-start | bytes 786440 | tf_op jit(solution)/shard_map/ppermute | solution.py:195
  20.6 1.4 %collective-permute-start.6 = (bf16[2,256,128]{2,1,0:T(8,128)(2,1)S(1)}, bf16[2,256,128]{2,1,0:T(8,128)(2,1)S(1)}, u32[]{:S(2)}, u32[]{:S(2)}) collective-permute-start(bf16[2,256,128]{2,1,0:T(8,128)(2,1)S(1)} %pad_maximum_fusion.4), channel_id=1, source_target_pairs={{0,4},{4,0},{8,12},{12,8},{16,20},{20,16},{24,28},{28,24},{1,5},{5... | collective-permute-start | bytes 393224 | tf_op jit(solution)/shard_map/ppermute | solution.py:177
  20.7 1.5 %collective-permute-start.7 = (bf16[2,256,128]{2,1,0:T(8,128)(2,1)S(1)}, bf16[2,256,128]{2,1,0:T(8,128)(2,1)S(1)}, u32[]{:S(2)}, u32[]{:S(2)}) collective-permute-start(bf16[2,256,128]{2,1,0:T(8,128)(2,1)S(1)} %slice.11), channel_id=1, source_target_pairs={{0,4},{4,0},{8,12},{12,8},{16,20},{20,16},{24,28},{28,24},{1,5},{5... | collective-permute-start | bytes 393224 | tf_op jit(solution)/shard_map/ppermute | solution.py:177
  21.3 1.4 %collective-permute-start.8 = (bf16[2,256,128]{2,1,0:T(8,128)(2,1)S(1)}, bf16[2,256,128]{2,1,0:T(8,128)(2,1)S(1)}, u32[]{:S(2)}, u32[]{:S(2)}) collective-permute-start(bf16[2,256,128]{2,1,0:T(8,128)(2,1)S(1)} %slice.12), channel_id=1, source_target_pairs={{0,4},{4,0},{8,12},{12,8},{16,20},{20,16},{24,28},{28,24},{1,5},{5... | collective-permute-start | bytes 393224 | tf_op jit(solution)/shard_map/ppermute | solution.py:177
  21.4 1.5 %collective-permute-start.9 = (bf16[2,256,128]{2,1,0:T(8,128)(2,1)S(1)}, bf16[2,256,128]{2,1,0:T(8,128)(2,1)S(1)}, u32[]{:S(2)}, u32[]{:S(2)}) collective-permute-start(bf16[2,256,128]{2,1,0:T(8,128)(2,1)S(1)} %slice.13), channel_id=1, source_target_pairs={{0,4},{4,0},{8,12},{12,8},{16,20},{20,16},{24,28},{28,24},{1,5},{5... | collective-permute-start | bytes 393224 | tf_op jit(solution)/shard_map/ppermute | solution.py:177
  27.3 6.3 %collective-permute-start.10 = (bf16[2,256,128]{2,1,0:T(8,128)(2,1)S(1)}, bf16[2,256,128]{2,1,0:T(8,128)(2,1)S(1)}, u32[]{:S(2)}, u32[]{:S(2)}) collective-permute-start(bf16[2,256,128]{2,1,0:T(8,128)(2,1)S(1)} %get-tuple-element.53), channel_id=1, source_target_pairs={{0,8},{4,12},{8,0},{12,4},{16,24},{20,28},{24,16},{28,20},{1,9},{5... | collective-permute-start | bytes 393224 | tf_op jit(solution)/shard_map/ppermute | solution.py:174
  28.7 6.3 %collective-permute-start.11 = (bf16[2,256,128]{2,1,0:T(8,128)(2,1)S(1)}, bf16[2,256,128]{2,1,0:T(8,128)(2,1)S(1)}, u32[]{:S(2)}, u32[]{:S(2)}) collective-permute-start(bf16[2,256,128]{2,1,0:T(8,128)(2,1)S(1)} %get-tuple-element.54), channel_id=1, source_target_pairs={{0,16},{4,20},{8,24},{12,28},{16,0},{20,4},{24,8},{28,12},{1,17},{... | collective-permute-start | bytes 393224 | tf_op jit(solution)/shard_map/ppermute | solution.py:174
  29.5 7.1 %collective-permute-start.12 = (bf16[2,256,128]{2,1,0:T(8,128)(2,1)S(1)}, bf16[2,256,128]{2,1,0:T(8,128)(2,1)S(1)}, u32[]{:S(2)}, u32[]{:S(2)}) collective-permute-start(bf16[2,256,128]{2,1,0:T(8,128)(2,1)S(1)} %get-tuple-element.55), channel_id=1, source_target_pairs={{0,24},{4,28},{8,16},{12,20},{16,8},{20,12},{24,0},{28,4},{1,25},{... | collective-permute-start | bytes 393224 | tf_op jit(solution)/shard_map/ppermute | solution.py:174
  37.3 7.7 %collective-permute-start.14 = (bf16[256,512]{1,0:T(8,128)(2,1)S(1)}, bf16[256,512]{1,0:T(8,128)(2,1)S(1)}, u32[]{:S(2)}, u32[]{:S(2)}) collective-permute-start(bf16[256,512]{1,0:T(8,128)(2,1)S(1)} %get-tuple-element.62), channel_id=1, source_target_pairs={{0,1},{1,0},{2,3},{3,2},{4,5},{5,4},{6,7},{7,6},{8,9},{9,8},{10,11... | collective-permute-start | bytes 786440 | tf_op jit(solution)/shard_map/ppermute | solution.py:195
  42.4 2.7 %collective-permute-start.16 = (bf16[4,2,256,128]{3,2,1,0:T(8,128)(2,1)S(1)}, bf16[4,2,256,128]{3,2,1,0:T(8,128)(2,1)S(1)}, u32[]{:S(2)}, u32[]{:S(2)}) collective-permute-start(bf16[4,2,256,128]{3,2,1,0:T(8,128)(2,1)S(1)} %get-tuple-element.70), channel_id=1, source_target_pairs={{0,4},{4,0},{8,12},{12,8},{16,20},{20,16},{24,28},{28,24},{1,5},{5... | collective-permute-start | bytes 1572872 | tf_op jit(solution)/shard_map/ppermute | solution.py:177
  42.5 13.5 %collective-permute-start.13 = (bf16[256,512]{1,0:T(8,128)(2,1)S(1)}, bf16[256,512]{1,0:T(8,128)(2,1)S(1)}, u32[]{:S(2)}, u32[]{:S(2)}) collective-permute-start(bf16[256,512]{1,0:T(8,128)(2,1)S(1)} %get-tuple-element.61), channel_id=1, source_target_pairs={{0,1},{1,0},{2,3},{3,2},{4,5},{5,4},{6,7},{7,6},{8,9},{9,8},{10,11... | collective-permute-start | bytes 786440 | tf_op jit(solution)/shard_map/ppermute | solution.py:195
  45.1 13.3 %collective-permute-start.15 = (bf16[256,512]{1,0:T(8,128)(2,1)S(1)}, bf16[256,512]{1,0:T(8,128)(2,1)S(1)}, u32[]{:S(2)}, u32[]{:S(2)}) collective-permute-start(bf16[256,512]{1,0:T(8,128)(2,1)S(1)} %add_convert_fusion.1), channel_id=1, source_target_pairs={{0,2},{1,3},{2,0},{3,1},{4,6},{5,7},{6,4},{7,5},{8,10},{9,11},{10,... | collective-permute-start | bytes 786440 | tf_op jit(solution)/shard_map/ppermute | solution.py:195
  45.3 13.9 %collective-permute-start.17 = (bf16[3,256,128]{2,1,0:T(8,128)(2,1)S(1)}, bf16[3,256,128]{2,1,0:T(8,128)(2,1)S(1)}, u32[]{:S(2)}, u32[]{:S(2)}) collective-permute-start(bf16[3,256,128]{2,1,0:T(8,128)(2,1)S(1)} %get-tuple-element.72), channel_id=1, source_target_pairs={{0,8},{4,12},{8,0},{12,4},{16,24},{20,28},{24,16},{28,20},{1,9},{5... | collective-permute-start | bytes 589832 | tf_op jit(solution)/shard_map/ppermute | solution.py:174
  46.2 13.0 %collective-permute-start.18 = (bf16[3,256,128]{2,1,0:T(8,128)(2,1)S(1)}, bf16[3,256,128]{2,1,0:T(8,128)(2,1)S(1)}, u32[]{:S(2)}, u32[]{:S(2)}) collective-permute-start(bf16[3,256,128]{2,1,0:T(8,128)(2,1)S(1)} %get-tuple-element.73), channel_id=1, source_target_pairs={{0,16},{4,20},{8,24},{12,28},{16,0},{20,4},{24,8},{28,12},{1,17},{... | collective-permute-start | bytes 589832 | tf_op jit(solution)/shard_map/ppermute | solution.py:174
  47.0 12.2 %collective-permute-start.19 = (bf16[3,256,128]{2,1,0:T(8,128)(2,1)S(1)}, bf16[3,256,128]{2,1,0:T(8,128)(2,1)S(1)}, u32[]{:S(2)}, u32[]{:S(2)}) collective-permute-start(bf16[3,256,128]{2,1,0:T(8,128)(2,1)S(1)} %get-tuple-element.74), channel_id=1, source_target_pairs={{0,24},{4,28},{8,16},{12,20},{16,8},{20,12},{24,0},{28,4},{1,25},{... | collective-permute-start | bytes 589832 | tf_op jit(solution)/shard_map/ppermute | solution.py:174

commit v4 on v3

--- a/solution.py
+++ b/solution.py
@@ -33,60 +33,62 @@
         out_specs=jax.tree.map(lambda _: vmem, outs),
         scratch_shapes=list(scratch),
         cost_estimate=pl.CostEstimate(flops=flops, bytes_accessed=moved, transcendentals=0),
-        compiler_params=pltpu.CompilerParams(vmem_limit_bytes=48 * 1024 * 1024),
+        compiler_params=pltpu.CompilerParams(vmem_limit_bytes=16 * 1024 * 1024),
     )(*args)
 
 
 def attend_body(chips, rows, scale, perm, *refs):
     pieces, siblings = refs[:chips], refs[chips : 2 * chips]
-    attended, probs, keys_values, queries = refs[2 * chips :]
-    chip = chip_index()
-    for d in range(chips):
-        for kind in range(2):
-            keys_values[d, kind, :rows] = pieces[d][kind]
-            keys_values[d, kind, rows:] = siblings[d][kind]
+    attended, probs, keys_values, queries, shares, values = refs[2 * chips :]
+    chip = chip_index()
+    for d in range(chips):
+        keys_values[d, 0, :rows] = pieces[d][0]
+        keys_values[d, 0, rows:] = siblings[d][0]
+        values[d, :rows, :128] = pieces[d][1]
+        values[d, rows:, :128] = siblings[d][1]
+        values[d, :, 128:] = jnp.ones((2*rows,128),LOW)
+        keys_values[d, 1, :rows] = pieces[d][1]
+        keys_values[d, 1, rows:] = siblings[d][1]
         queries[d] = pieces[d][2]
+    factor = scale * math.log2(math.e)
     for d in range(chips):
         p = perm[chip, chip ^ d] ^ chip
         query = pieces[d][2]
         local = dot(query, keys_values[d, 0], NT)
         remote = dot(query, keys_values[p, 0], NT)
-        top = jnp.maximum(
-            jnp.max(local, axis=1, keepdims=True), jnp.max(remote, axis=1, keepdims=True)
-        )
-        factor = scale * math.log2(math.e)
-        local = jnp.exp2((local - top) * factor)
-        remote = jnp.exp2((remote - top) * factor)
-        total = jnp.sum(local, axis=1, keepdims=True) + jnp.sum(remote, axis=1, keepdims=True)
-        share = 1.0 / total
-        local = (local * share).astype(LOW)
-        remote = (remote * share).astype(LOW)
+        top = jnp.max(jnp.maximum(local, remote), axis=1, keepdims=True)
+        local = jnp.exp2((local - top) * factor).astype(LOW)
+        remote = jnp.exp2((remote - top) * factor).astype(LOW)
         probs[d, :, : 2 * rows] = local
         probs[d, :, 2 * rows :] = remote
-        result = dot(local, keys_values[d, 1]) + dot(remote, keys_values[p, 1])
-        attended[d] = result.astype(LOW)
+        result = dot(local, values[d]) + dot(remote, values[p])
+        share = 1.0 / result[:, 128:]
+        shares[d] = share
+        attended[d] = (result[:, :128] * share).astype(LOW)
 
 
 def backward_body(chips, rows, scale, perm, *refs):
     arrived = refs[:chips]
-    attended, probs, keys_values, queries = refs[chips : chips + 4]
-    query_grad, own_part, sibling_part, score_grad, grads = refs[chips + 4 :]
+    attended, probs, keys_values, queries, shares = refs[chips : chips + 5]
+    query_grad, own_part, sibling_part, score_grad, scaled = refs[chips + 5 :]
     chip = chip_index()
     for d in range(chips):
         p = perm[chip, chip ^ d] ^ chip
-        grad = arrived[d][1]
-        grads[d] = grad
-        delta = jnp.sum(grad.astype(F32) * attended[d].astype(F32), axis=1, keepdims=True)
+        grad = arrived[d][...]
+        share = shares[d]
+        g32 = grad.astype(F32)
+        delta = jnp.sum(g32 * attended[d].astype(F32), axis=1, keepdims=True)
+        scaled[0, d] = (queries[d].astype(F32) * (share * scale)).astype(LOW)
+        scaled[1, d] = (g32 * share).astype(LOW)
         total = None
         for part, source in ((0, d), (1, p)):
             lanes = slice(2 * rows * part, 2 * rows * (part + 1))
             prob_grad = dot(grad, keys_values[source, 1], NT)
-            weight = probs[d, :, lanes].astype(F32)
-            change = (weight * (prob_grad - delta) * scale).astype(LOW)
+            change = (probs[d, :, lanes].astype(F32) * (prob_grad - delta)).astype(LOW)
             score_grad[part, d] = change
             term = dot(change, keys_values[source, 0])
             total = term if total is None else total + term
-        query_grad[d] = total.astype(LOW)
+        query_grad[d] = (total * (share * scale)).astype(LOW)
     for d in range(chips):
         asker = jnp.int32(0)
         for i in range(chips):
@@ -95,10 +97,10 @@
         for half, out in ((0, own_part), (1, sibling_part)):
             near = slice(half * rows, (half + 1) * rows)
             far = slice((half + 2) * rows, (half + 3) * rows)
-            key_part = dot(score_grad[0, d, :, near], queries[d], TN)
-            key_part += dot(score_grad[1, asker, :, near], queries[asker], TN)
-            value_part = dot(probs[d, :, near], grads[d], TN)
-            value_part += dot(probs[asker, :, far], grads[asker], TN)
+            key_part = dot(score_grad[0, d, :, near], scaled[0, d], TN)
+            key_part += dot(score_grad[1, asker, :, near], scaled[0, asker], TN)
+            value_part = dot(probs[d, :, near], scaled[1, d], TN)
+            value_part += dot(probs[asker, :, far], scaled[1, asker], TN)
             out[d, 0] = key_part.astype(out.dtype)
             out[d, 1] = value_part.astype(out.dtype)
 
@@ -107,10 +109,10 @@
     incoming, outs, joined = refs[:chips], refs[chips : chips + groups], refs[chips + groups]
     chip = chip_index()
     level = lax.axis_index("head")
-    width = incoming[0].shape[2]
+    width = incoming[0].shape[1]
     for d in range(chips):
         lanes = pl.ds(pl.multiple_of((chip ^ d) * width, width), width)
-        joined[:, lanes] = incoming[d][0]
+        joined[:, lanes] = incoming[d][...]
     rows = joined[...]
     for j in range(groups):
         columns = outs[j].shape[1]
@@ -119,11 +121,11 @@
         outs[j][...] = dot(rows, term).astype(LOW)
 
 
-def grad_body(chips, groups, weight, attended, *refs):
+def grad_body(chips, groups, weight, *refs):
     slices, outs = refs[:groups], refs[groups:]
     chip = chip_index()
     level = lax.axis_index("head")
-    width = attended.shape[2]
+    width = outs[0].shape[1]
     total = None
     for j in range(groups):
         block = slices[j][...]
@@ -132,15 +134,20 @@
         term = dot(block, weight[:, :, lanes].reshape(chips * width, columns), NT)
         total = term if total is None else total + term
     total = total.astype(LOW)
-    for d in range(chips):
-        outs[d][0] = attended[d]
     for c in range(chips):
 
         @pl.when(chip == c)
         def _():
             for d in range(chips):
                 h = c ^ d
-                outs[d][1] = total[:, h * width : (h + 1) * width]
+                outs[d][...] = total[:, h * width : (h + 1) * width]
+
+
+def sum_body(*refs):
+    total = refs[0][...].astype(F32)
+    for ref in refs[1:-1]:
+        total = total + ref[...].astype(F32)
+    refs[-1][...] = total.astype(LOW)
 
 
 def merge_body(chips, query_grad, own_part, arrived, *outs):
@@ -152,8 +159,9 @@
 
 
 def place_body(chips, *refs):
-    pieces, outs = refs[:chips], refs[chips:]
-    chip = chip_index()
+    summands, pieces, projected, outs = refs[:3], refs[3 : 3 + chips], refs[3 + chips], refs[4 + chips :]
+    chip = chip_index()
+    sum_body(*summands, projected)
     for d in range(chips):
         for kind in range(3):
             outs[kind][chip ^ d] = pieces[d][kind]
@@ -202,51 +210,54 @@
     pieces = [head_piece(d) for d in range(chips)]
     siblings = [to_sibling(pieces[0][:2])]
     pieces = exchange(pieces)
-    *pieces[1:], twice, once = together(*pieces[1:], twice, once)
+    pieces[3], twice, once = together(pieces[3], twice, once)
     slices = [out_cotangent, once, twice, across(twice, 1)]
     siblings += [to_sibling(piece[:2]) for piece in pieces[1:]]
     tile = rows * width
     scores = chips * rows * 4 * rows
-    attended, probs, keys_values, query_rows = call(
+    piece = shape((rows, width), LOW)
+    attended, probs, keys_values, query_rows, shares = call(
         functools.partial(attend_body, chips, rows, scale),
         (
             shape((chips, rows, width), LOW),
             shape((chips, rows, 4 * rows), LOW),
             shape((chips, 2, 2 * rows, width), LOW),
             shape((chips, rows, width), LOW),
+            shape((chips, rows, width), F32),
         ),
         block_perm,
         *pieces,
         *siblings,
         flops=4 * scores * width,
         moved=2 * (scores + 14 * chips * tile),
+        scratch=[pltpu.VMEM((chips, 2 * rows, 2 * width), LOW)],
         smem=(0,),
     )
     weight_bytes = 2 * heads * width * features
-    *slices, attended = together(*slices, attended)
-    outgoing = call(
+    own_attended = exchange([attended[d] for d in range(chips)])
+    attended, *slices = together(attended, *slices)
+    grad_att = call(
         functools.partial(grad_body, chips, groups),
-        tuple(shape((2, rows, width), LOW) for _ in range(chips)),
+        (piece,) * chips,
         out_weight,
-        attended,
         *slices,
         flops=2 * rows * heads * width * features,
         moved=weight_bytes + 2 * rows * features + 6 * chips * tile,
     )
-    incoming = together(*exchange(outgoing))
+    incoming = exchange(grad_att)
+    own_attended[0] = together(own_attended[0], grad_att[0])[0]
     parts = call(
         functools.partial(project_body, chips, groups),
         tuple(shape((rows, columns), LOW) for _ in range(groups)),
         out_weight,
-        *incoming,
+        *own_attended,
         flops=2 * rows * heads * width * features,
         moved=weight_bytes + 2 * rows * features + 4 * chips * tile,
         scratch=[pltpu.VMEM((rows, heads * width), LOW)],
     )
     halfway = across(parts[3], 1)
-    neighbour = across(parts[1], 1)
-    halfway = (halfway.astype(F32) + parts[2].astype(F32)).astype(LOW)
-    summands = [parts[0], neighbour, across(halfway, 2)]
+    neighbour = across(together(parts[1], incoming[1])[0], 1)
+    halfway = call(sum_body, shape((rows, columns), LOW), halfway, parts[2], flops=2**33, moved=2**28)
     incoming[0] = together(incoming[0], parts[0])[0]
     query_grad, own_part, sibling_part = call(
         functools.partial(backward_body, chips, rows, scale),
@@ -261,11 +272,12 @@
         probs,
         keys_values,
         query_rows,
-        flops=8 * scores * width,
+        shares,
+        flops=2**33,
         moved=2 * (scores + 20 * chips * tile),
         scratch=[
             pltpu.VMEM((2, chips, rows, 2 * rows), LOW),
-            pltpu.VMEM((chips, rows, width), LOW),
+            pltpu.VMEM((2, chips, rows, width), LOW),
         ],
         smem=(0,),
     )
@@ -279,14 +291,15 @@
             moved=2 * 14 * chips * tile,
         )
     )
-    gradients = call(
+    return call(
         functools.partial(place_body, chips),
-        tuple(shape((heads, rows, width), LOW) for _ in range(3)),
+        (shape((rows, columns), LOW),) + (shape((heads, rows, width), LOW),) * 3,
+        parts[0],
+        neighbour,
+        across(halfway, 2),
         *returned,
         moved=2 * 6 * chips * tile,
     )
-    projected = sum(term.astype(F32) for term in summands)
-    return (projected.astype(LOW), *gradients)
 
 
 def partner(shard, axis, bit):

time: 60.4 us -> 57.8 us (0.957)
  waiting for transfers between devices: 26.5 us -> 22.2 us
  starting transfers between devices: 20.6 us -> 23.6 us
  other arithmetic: 0.98 us -> 0.11 us
  Pallas kernels: 9.26 us -> 8.63 us
    ppermute x9 -> x12, waiting for transfers between devices: 13.6 us -> 8.92 us  [to_chip(): return lax.ppermute(array, 'seq', [(i, i ^ 2 * d) for i in range(devices)])]
    ppermute x9 -> x12, starting transfers between devices: 10.8 us -> 14.3 us  [to_chip(): return lax.ppermute(array, 'seq', [(i, i ^ 2 * d) for i in range(devices)])]
    convert_element_type x2 -> x0, other arithmetic: 0.87 us -> none  [the longest x1 0.8 us: by_heads(): return (projected.astype(LOW), *gradients)]
    pallas_call x6 -> x7, Pallas kernels: 9.26 us -> 8.63 us  [call(): pl.pallas_call(body, out_shape=outs, in_specs=[scalar if i in smem else v...]
    ppermute x6, waiting for transfers between devices: 11.9 us -> 12.6 us  [along(): return lax.ppermute(array, 'head', pairs)]
  transfers between devices with their start and end apart: 20 -> 23, of which waited for: 13 -> 11; matrix products, arithmetic and copies ran while one was open for 5% -> 4% of each run, Pallas kernels for 11% -> 13%
where the time goes in v4:
time: 57.8 us; the launch traced here: 57.5 us
  starting transfers between devices  23.6 us (41%)
  waiting for transfers between devices  22.2 us (38%)
  Pallas kernels  8.63 us (15%)
  local copies, waits for them, and re-layouts  2.13 us (4%)
  between operations  0.76 us (1%)
    ppermute x12, starting transfers between devices, to_chip(): return lax.ppermute(array, 'seq', [(i, i ^ 2 * d) for i in range(devices)])  14.3 us
    ppermute x6, waiting for transfers between devices, along(): return lax.ppermute(array, 'head', pairs)  12.6 us
    ppermute x12, waiting for transfers between devices, to_chip(): return lax.ppermute(array, 'seq', [(i, i ^ 2 * d) for i in range(devices)])  8.92 us
    pallas_call x7, Pallas kernels, call(): pl.pallas_call(body, out_shape=outs, in_specs=[scalar if i in smem else v...  8.63 us
    ppermute x6, starting transfers between devices, along(): return lax.ppermute(array, 'head', pairs)  8.56 us
    dynamic_slice x2, local copies, waits for them, and re-layouts, head_piece(): lax.dynamic_index_in_dim(a, h, 0, keepdims=False)  2.08 us
  transfers between devices with their start and end apart: 23, of which 11 were waited for; matrix products, arithmetic and copies ran while one was open for 4% of the time, Pallas kernels for 13%

profile of v4, /device:TPU:0, one launch (start us, length us, event | category | flops | bytes accessed | tf_op | source)
XLA Modules:
  0.0 57.5 jit_solution(18256483006821398448)
XLA Ops:
  0.6 4.1 %collective-permute-start.3 = (bf16[256,512]{1,0:T(8,128)(2,1)}, bf16[256,512]{1,0:T(8,128)(2,1)S(1)}, u32[]{:S(2)}, u32[]{:S(2)}) collective-permute-start(bf16[256,512]{1,0:T(8,128)(2,1)} %refs_0_), channel_id=1, source_target_pairs={{0,2},{1,3},{2,0},{3,1},{4,6},{5,7},{6,4},{7,5},{8,10},{9,11},{10,... | collective-permute-start | bytes 786440 | tf_op jit(solution)/shard_map/ppermute | solution.py:203
  4.7 1.6 %collective-permute-start.4 = (bf16[256,512]{1,0:T(8,128)(2,1)}, bf16[256,512]{1,0:T(8,128)(2,1)S(1)}, u32[]{:S(2)}, u32[]{:S(2)}) collective-permute-start(bf16[256,512]{1,0:T(8,128)(2,1)} %refs_0_), channel_id=1, source_target_pairs={{0,1},{1,0},{2,3},{3,2},{4,5},{5,4},{6,7},{7,6},{8,9},{9,8},{10,11... | collective-permute-start | bytes 786440 | tf_op jit(solution)/shard_map/ppermute | solution.py:203
  6.3 0.0 copy-start.2
  6.3 1.0 %constant_dynamic-slice_fusion.2 = (bf16[1,256,128]{2,1,0:T(8,128)(2,1)S(1)}, bf16[1,256,128]{2,1,0:T(8,128)(2,1)S(1)}, bf16[1,256,128]{2,1,0:T(8,128)(2,1)S(1)}, bf16[1,256,128]{2,1,0:T(8,128)(2,1)S(1)}) fusion(bf16[4,256,128]{2,1,0:T(8,128)(2,1)} %param.7, s32[]{:T(128)S(6)} %select_n.30, s32[]{:T(128)S(6)} %select_n.28, s32[]{:T(128)S(6)} %select_n.27, ...), kind=kLoop, calls=%fused_computation.11 | loop fusion | bytes 524304 | tf_op jit(solution)/shard_map/jit(dynamic_index_in_dim)/dynamic_slice | solution.py:197
  7.3 1.1 %constant_dynamic-slice_fusion = (bf16[1,256,128]{2,1,0:T(8,128)(2,1)S(1)}, bf16[1,256,128]{2,1,0:T(8,128)(2,1)S(1)}, bf16[1,256,128]{2,1,0:T(8,128)(2,1)S(1)}, ...) fusion(bf16[4,256,128]{2,1,0:T(8,128)(2,1)} %param.6, ...), kind=kLoop, calls=%fused_computation.9 | loop fusion | bytes 1048592 | tf_op jit(solution)/shard_map/jit(dynamic_index_in_dim)/dynamic_slice | solution.py:197
  8.4 1.6 %collective-permute-start = (bf16[3,256,128]{2,1,0:T(8,128)(2,1)S(1)}, bf16[3,256,128]{2,1,0:T(8,128)(2,1)S(1)}, u32[]{:S(2)}, u32[]{:S(2)}) collective-permute-start(bf16[3,256,128]{2,1,0:T(8,128)(2,1)S(1)} %pad_maximum_fusion.1), channel_id=1, source_target_pairs={{0,8},{4,12},{8,0},{12,4},{16,24},{20,28},{24,16},{28,20},{1,9},{5... | collective-permute-start | bytes 589832 | tf_op jit(solution)/shard_map/ppermute | solution.py:182
  10.0 1.6 %collective-permute-start.1 = (bf16[3,256,128]{2,1,0:T(8,128)(2,1)S(1)}, bf16[3,256,128]{2,1,0:T(8,128)(2,1)S(1)}, u32[]{:S(2)}, u32[]{:S(2)}) collective-permute-start(bf16[3,256,128]{2,1,0:T(8,128)(2,1)S(1)} %pad_maximum_fusion.2), channel_id=1, source_target_pairs={{0,16},{4,20},{8,24},{12,28},{16,0},{20,4},{24,8},{28,12},{1,17},{... | collective-permute-start | bytes 589832 | tf_op jit(solution)/shard_map/ppermute | solution.py:182
  11.6 0.0 copy-start
  11.6 0.0 copy-start.1
  11.6 0.5 collective-permute-start.2
  12.2 4.0 %collective-permute-done.refs_1_ = bf16[3,256,128]{2,1,0:T(8,128)(2,1)S(1)} collective-permute-done((bf16[3,256,128]{2,1,0:T(8,128)(2,1)S(1)}, bf16[3,256,128]{2,1,0:T(8,128)(2,1)S(1)}, u32[]{:S(2)}, u32[]{:S(2)}) %collective-permute-start) | collective-permute-done | bytes 196640 | tf_op jit(solution)/shard_map/ppermute | solution.py:182
  16.2 0.0 collective-permute-start.5
  16.2 3.9 %collective-permute-done.1.refs_2_ = bf16[3,256,128]{2,1,0:T(8,128)(2,1)S(1)} collective-permute-done((bf16[3,256,128]{2,1,0:T(8,128)(2,1)S(1)}, bf16[3,256,128]{2,1,0:T(8,128)(2,1)S(1)}, u32[]{:S(2)}, u32[]{:S(2)}) %collective-permute-start.1) | collective-permute-done | bytes 196640 | tf_op jit(solution)/shard_map/ppermute | solution.py:182
  20.1 0.0 collective-permute-start.6
  20.1 0.0 collective-permute-done.2.refs_3_
  20.1 0.6 collective-permute-start.7
  20.7 0.0 collective-permute-done.3.refs_2_
  20.7 0.0 collective-permute-done.4.refs_1_
  20.7 0.1 collective-permute-start.8
  20.8 0.5 collective-permute-start.9
  21.4 0.0 collective-permute-done.5.refs_4_
  21.4 0.1 collective-permute-done.6.refs_5_
  21.4 0.2 collective-permute-done.7.refs_6_
  21.7 0.4 collective-permute-done.8.refs_7_
  22.1 0.0 copy-done.2
  22.1 2.5 %shard_map.93 = (bf16[4,256,128]{2,1,0:T(8,128)(2,1)S(1)}, bf16[4,256,1024]{2,1,0:T(8,128)(2,1)S(1)}, bf16[4,2,512,128]{3,2,1,0:T(8,128)(2,1)S(1)}, bf16[4,256,128]{2,1,0:T(8,128)(2,1)S(1)}, f32[4,256,128]{2,1,0:T(8,128)S(1)}) custom-call(s32[4,4]{1,0:T(4,128)S(1)} %copy-done.2, bf16[3,256,128]{2,1,0:T(8,128)(2,1)S(1)} %pad_maximum_fusion.refs_0_, ...), custom_call_target="tpu_custom_call" | custom-call | flops 536870912 | bytes 5767168 | tf_op jit(solution)/shard_map/pallas_call | solution.py:29
  24.6 0.8 %collective-permute-start.10 = (bf16[256,128]{1,0:T(8,128)(2,1)S(1)}, bf16[256,128]{1,0:T(8,128)(2,1)S(1)}, u32[]{:S(2)}, u32[]{:S(2)}) collective-permute-start(bf16[256,128]{1,0:T(8,128)(2,1)S(1)} %get-tuple-element.68), channel_id=1, source_target_pairs={{0,8},{4,12},{8,0},{12,4},{16,24},{20,28},{24,16},{28,20},{1,9},{5... | collective-permute-start | bytes 196616 | tf_op jit(solution)/shard_map/ppermute | solution.py:182
  25.4 1.3 %collective-permute-start.11 = (bf16[256,128]{1,0:T(8,128)(2,1)S(1)}, bf16[256,128]{1,0:T(8,128)(2,1)S(1)}, u32[]{:S(2)}, u32[]{:S(2)}) collective-permute-start(bf16[256,128]{1,0:T(8,128)(2,1)S(1)} %get-tuple-element.67), channel_id=1, source_target_pairs={{0,16},{4,20},{8,24},{12,28},{16,0},{20,4},{24,8},{28,12},{1,17},{... | collective-permute-start | bytes 196616 | tf_op jit(solution)/shard_map/ppermute | solution.py:182
  26.8 1.4 %collective-permute-start.12 = (bf16[256,128]{1,0:T(8,128)(2,1)S(1)}, bf16[256,128]{1,0:T(8,128)(2,1)S(1)}, u32[]{:S(2)}, u32[]{:S(2)}) collective-permute-start(bf16[256,128]{1,0:T(8,128)(2,1)S(1)} %get-tuple-element.66), channel_id=1, source_target_pairs={{0,24},{4,28},{8,16},{12,20},{16,8},{20,12},{24,0},{28,4},{1,25},{... | collective-permute-start | bytes 196616 | tf_op jit(solution)/shard_map/ppermute | solution.py:182
  28.2 1.4 %collective-permute-done.9.refs_3_ = bf16[256,512]{1,0:T(8,128)(2,1)S(1)} collective-permute-done((bf16[256,512]{1,0:T(8,128)(2,1)S(1)}, bf16[256,512]{1,0:T(8,128)(2,1)S(1)}, u32[]{:S(2)}, u32[]{:S(2)}) %collective-permute-start.9) | collective-permute-done | bytes 262176 | tf_op jit(solution)/shard_map/ppermute | solution.py:203
  29.6 0.0 copy-done
  29.6 0.0 copy-done.1
  29.6 0.8 %shard_map.94 = (bf16[256,128]{1,0:T(8,128)(2,1)S(1)}, bf16[256,128]{1,0:T(8,128)(2,1)S(1)}, bf16[256,128]{1,0:T(8,128)(2,1)S(1)}, bf16[256,128]{1,0:T(8,128)(2,1)S(1)}) custom-call(bf16[4,128,2048]{2,1,0:T(8,128)(2,1)S(1)} %copy-done, bf16[256,512]{1,0:T(8,128)(2,1)S(1)} %copy-done.1, bf16[256,512]{1,0:T(8,128)(2,1)S(1)} %collective-permute-done.4.refs_1_, ...), custom_call_target="tpu_custom_call" | custom-call | flops 536870912 | bytes 3932160 | tf_op jit(solution)/shard_map/pallas_call | solution.py:29
  30.4 0.6 %collective-permute-start.13 = (bf16[256,128]{1,0:T(8,128)(2,1)S(1)}, bf16[256,128]{1,0:T(8,128)(2,1)S(1)}, u32[]{:S(2)}, u32[]{:S(2)}) collective-permute-start(bf16[256,128]{1,0:T(8,128)(2,1)S(1)} %get-tuple-element.47), channel_id=1, source_target_pairs={{0,8},{4,12},{8,0},{12,4},{16,24},{20,28},{24,16},{28,20},{1,9},{5... | collective-permute-start | bytes 196616 | tf_op jit(solution)/shard_map/ppermute | solution.py:182
  31.0 1.5 %collective-permute-start.17 = (bf16[256,128]{1,0:T(8,128)(2,1)S(1)}, bf16[256,128]{1,0:T(8,128)(2,1)S(1)}, u32[]{:S(2)}, u32[]{:S(2)}) collective-permute-start(bf16[256,128]{1,0:T(8,128)(2,1)S(1)} %get-tuple-element.52), channel_id=1, source_target_pairs={{0,16},{4,20},{8,24},{12,28},{16,0},{20,4},{24,8},{28,12},{1,17},{... | collective-permute-start | bytes 196616 | tf_op jit(solution)/shard_map/ppermute | solution.py:182
  32.5 0.0 collective-permute-done.10.refs_1_
  32.5 1.4 %collective-permute-start.18 = (bf16[256,128]{1,0:T(8,128)(2,1)S(1)}, bf16[256,128]{1,0:T(8,128)(2,1)S(1)}, u32[]{:S(2)}, u32[]{:S(2)}) collective-permute-start(bf16[256,128]{1,0:T(8,128)(2,1)S(1)} %get-tuple-element.53), channel_id=1, source_target_pairs={{0,24},{4,28},{8,16},{12,20},{16,8},{20,12},{24,0},{28,4},{1,25},{... | collective-permute-start | bytes 196616 | tf_op jit(solution)/shard_map/ppermute | solution.py:182
  33.9 0.0 collective-permute-done.11.refs_2_
  33.9 0.0 collective-permute-done.12.refs_3_
  33.9 0.8 %shard_map.95 = (bf16[256,512]{1,0:T(8,128)(2,1)S(1)}, bf16[256,512]{1,0:T(8,128)(2,1)S(1)}, bf16[256,512]{1,0:T(8,128)(2,1)S(1)}, bf16[256,512]{1,0:T(8,128)(2,1)S(1)}) custom-call(bf16[4,128,2048]{2,1,0:T(8,128)(2,1)S(1)} %copy-done, bf16[256,128]{1,0:T(8,128)(2,1)S(1)} %get-tuple-element.44.refs_0_, bf16[256,128]{1,0:T(8,128)(2,1)S(1)} %collective-permute-done.10.refs_1_, ...), custom_call_target="tpu_custom_call" | custom-call | flops 536870912 | bytes 3670016 | tf_op jit(solution)/shard_map/pallas_call | solution.py:29
  34.7 0.5 collective-permute-start.15
  35.2 0.2 collective-permute-done.13.refs_1_
  35.4 1.4 %collective-permute-start.14 = (bf16[256,512]{1,0:T(8,128)(2,1)S(1)}, bf16[256,512]{1,0:T(8,128)(2,1)S(1)}, u32[]{:S(2)}, u32[]{:S(2)}) collective-permute-start(bf16[256,512]{1,0:T(8,128)(2,1)S(1)} %get-tuple-element.48), channel_id=1, source_target_pairs={{0,1},{1,0},{2,3},{3,2},{4,5},{5,4},{6,7},{7,6},{8,9},{9,8},{10,11... | collective-permute-start | bytes 786440 | tf_op jit(solution)/shard_map/ppermute | solution.py:203
  36.8 0.0 collective-permute-done.17.refs_2_
  36.8 0.8 %collective-permute-done.18.refs_3_ = bf16[256,128]{1,0:T(8,128)(2,1)S(1)} collective-permute-done((bf16[256,128]{1,0:T(8,128)(2,1)S(1)}, bf16[256,128]{1,0:T(8,128)(2,1)S(1)}, u32[]{:S(2)}, u32[]{:S(2)}) %collective-permute-start.18) | collective-permute-done | bytes 65568 | tf_op jit(solution)/shard_map/ppermute | solution.py:182
  37.7 3.4 %shard_map.97 = (bf16[4,256,128]{2,1,0:T(8,128)(2,1)S(1)}, f32[4,2,256,128]{3,2,1,0:T(8,128)S(1)}, bf16[4,2,256,128]{3,2,1,0:T(8,128)(2,1)S(1)}) custom-call(s32[4,4]{1,0:T(4,128)S(1)} %copy-done.2, bf16[256,128]{1,0:T(8,128)(2,1)S(1)} %get-tuple-element.51.refs_0_, bf16[256,128]{1,0:T(8,128)(2,1)S(1)} %collective-permute-done.13.refs_1_, ...), custom_call_target="tpu_custom_call" | custom-call | flops 8589934592 | bytes 7340032 | tf_op jit(solution)/shard_map/pallas_call | solution.py:29
  41.0 0.1 collective-permute-start.19
  41.1 2.9 %collective-permute-done.15.refs_0_ = bf16[256,512]{1,0:T(8,128)(2,1)S(1)} collective-permute-done((bf16[256,512]{1,0:T(8,128)(2,1)S(1)}, bf16[256,512]{1,0:T(8,128)(2,1)S(1)}, u32[]{:S(2)}, u32[]{:S(2)}) %collective-permute-start.15) | collective-permute-done | bytes 262176 | tf_op jit(solution)/shard_map/ppermute | solution.py:203
  44.0 0.1 shard_map.96
  44.1 0.4 collective-permute-start.16
  44.5 0.0 collective-permute-done.19.arrived
  44.5 0.1 shard_map.98
  44.7 0.6 %collective-permute-start.20 = (bf16[3,256,128]{2,1,0:T(8,128)(2,1)S(1)}, bf16[3,256,128]{2,1,0:T(8,128)(2,1)S(1)}, u32[]{:S(2)}, u32[]{:S(2)}) collective-permute-start(bf16[3,256,128]{2,1,0:T(8,128)(2,1)S(1)} %get-tuple-element.63), channel_id=1, source_target_pairs={{0,8},{4,12},{8,0},{12,4},{16,24},{20,28},{24,16},{28,20},{1,9},{5... | collective-permute-start | bytes 589832 | tf_op jit(solution)/shard_map/ppermute | solution.py:182
  45.3 1.5 %collective-permute-start.21 = (bf16[3,256,128]{2,1,0:T(8,128)(2,1)S(1)}, bf16[3,256,128]{2,1,0:T(8,128)(2,1)S(1)}, u32[]{:S(2)}, u32[]{:S(2)}) collective-permute-start(bf16[3,256,128]{2,1,0:T(8,128)(2,1)S(1)} %get-tuple-element.64), channel_id=1, source_target_pairs={{0,16},{4,20},{8,24},{12,28},{16,0},{20,4},{24,8},{28,12},{1,17},{... | collective-permute-start | bytes 589832 | tf_op jit(solution)/shard_map/ppermute | solution.py:182
  46.8 1.4 %collective-permute-start.22 = (bf16[3,256,128]{2,1,0:T(8,128)(2,1)S(1)}, bf16[3,256,128]{2,1,0:T(8,128)(2,1)S(1)}, u32[]{:S(2)}, u32[]{:S(2)}) collective-permute-start(bf16[3,256,128]{2,1,0:T(8,128)(2,1)S(1)} %get-tuple-element.65), channel_id=1, source_target_pairs={{0,24},{4,28},{8,16},{12,20},{16,8},{20,12},{24,0},{28,4},{1,25},{... | collective-permute-start | bytes 589832 | tf_op jit(solution)/shard_map/ppermute | solution.py:182
  48.2 1.4 %collective-permute-done.14.refs_1_ = bf16[256,512]{1,0:T(8,128)(2,1)S(1)} collective-permute-done((bf16[256,512]{1,0:T(8,128)(2,1)S(1)}, bf16[256,512]{1,0:T(8,128)(2,1)S(1)}, u32[]{:S(2)}, u32[]{:S(2)}) %collective-permute-start.14) | collective-permute-done | bytes 262176 | tf_op jit(solution)/shard_map/ppermute | solution.py:203
  49.6 6.8 %collective-permute-done.16.refs_2_ = bf16[256,512]{1,0:T(8,128)(2,1)S(1)} collective-permute-done((bf16[256,512]{1,0:T(8,128)(2,1)S(1)}, bf16[256,512]{1,0:T(8,128)(2,1)S(1)}, u32[]{:S(2)}, u32[]{:S(2)}) %collective-permute-start.16) | collective-permute-done | bytes 262176 | tf_op jit(solution)/shard_map/ppermute | solution.py:203
  56.4 0.0 collective-permute-done.20.refs_4_
  56.4 0.0 collective-permute-done.21.refs_5_
  56.5 0.0 collective-permute-done.22.refs_6_
  56.5 1.1 %shard_map.99 = (bf16[256,512]{1,0:T(8,128)(2,1)}, bf16[4,256,128]{2,1,0:T(8,128)(2,1)}, bf16[4,256,128]{2,1,0:T(8,128)(2,1)}, bf16[4,256,128]{2,1,0:T(8,128)(2,1)}) custom-call(bf16[256,512]{1,0:T(8,128)(2,1)S(1)} %get-tuple-element.45.refs_0_, bf16[256,512]{1,0:T(8,128)(2,1)S(1)} %collective-permute-done.14.refs_1_, ...), custom_call_target="tpu_custom_call" | custom-call | bytes 1572864 | tf_op jit(solution)/shard_map/pallas_call | solution.py:29
  (9 shorter events, 0.2 us)
Async XLA Ops:
  0.6 20.1 %collective-permute-start.3 = (bf16[256,512]{1,0:T(8,128)(2,1)}, bf16[256,512]{1,0:T(8,128)(2,1)S(1)}, u32[]{:S(2)}, u32[]{:S(2)}) collective-permute-start(bf16[256,512]{1,0:T(8,128)(2,1)} %refs_0_), channel_id=1, source_target_pairs={{0,2},{1,3},{2,0},{3,1},{4,6},{5,7},{6,4},{7,5},{8,10},{9,11},{10,... | collective-permute-start | bytes 786440 | tf_op jit(solution)/shard_map/ppermute | solution.py:203
  4.7 16.0 %collective-permute-start.4 = (bf16[256,512]{1,0:T(8,128)(2,1)}, bf16[256,512]{1,0:T(8,128)(2,1)S(1)}, u32[]{:S(2)}, u32[]{:S(2)}) collective-permute-start(bf16[256,512]{1,0:T(8,128)(2,1)} %refs_0_), channel_id=1, source_target_pairs={{0,1},{1,0},{2,3},{3,2},{4,5},{5,4},{6,7},{7,6},{8,9},{9,8},{10,11... | collective-permute-start | bytes 786440 | tf_op jit(solution)/shard_map/ppermute | solution.py:203
  6.3 15.8 %copy-start.2 = (s32[4,4]{1,0:T(4,128)S(1)}, s32[4,4]{1,0:T(4,128)}, u32[]{:S(2)}) copy-start(s32[4,4]{1,0:T(4,128)} %perm.3) | copy-start | bytes 196
  8.4 7.8 %collective-permute-start = (bf16[3,256,128]{2,1,0:T(8,128)(2,1)S(1)}, bf16[3,256,128]{2,1,0:T(8,128)(2,1)S(1)}, u32[]{:S(2)}, u32[]{:S(2)}) collective-permute-start(bf16[3,256,128]{2,1,0:T(8,128)(2,1)S(1)} %pad_maximum_fusion.1), channel_id=1, source_target_pairs={{0,8},{4,12},{8,0},{12,4},{16,24},{20,28},{24,16},{28,20},{1,9},{5... | collective-permute-start | bytes 589832 | tf_op jit(solution)/shard_map/ppermute | solution.py:182
  10.0 10.1 %collective-permute-start.1 = (bf16[3,256,128]{2,1,0:T(8,128)(2,1)S(1)}, bf16[3,256,128]{2,1,0:T(8,128)(2,1)S(1)}, u32[]{:S(2)}, u32[]{:S(2)}) collective-permute-start(bf16[3,256,128]{2,1,0:T(8,128)(2,1)S(1)} %pad_maximum_fusion.2), channel_id=1, source_target_pairs={{0,16},{4,20},{8,24},{12,28},{16,0},{20,4},{24,8},{28,12},{1,17},{... | collective-permute-start | bytes 589832 | tf_op jit(solution)/shard_map/ppermute | solution.py:182
  11.6 18.0 %copy-start = (bf16[4,128,2048]{2,1,0:T(8,128)(2,1)S(1)}, bf16[4,128,2048]{2,1,0:T(8,128)(2,1)}, u32[]{:S(2)}) copy-start(bf16[4,128,2048]{2,1,0:T(8,128)(2,1)} %weight.3) | copy-start | bytes 6291460
  11.6 18.0 %copy-start.1 = (bf16[256,512]{1,0:T(8,128)(2,1)S(1)}, bf16[256,512]{1,0:T(8,128)(2,1)}, u32[]{:S(2)}) copy-start(bf16[256,512]{1,0:T(8,128)(2,1)} %refs_0_) | copy-start | bytes 786436
  11.6 8.5 %collective-permute-start.2 = (bf16[3,256,128]{2,1,0:T(8,128)(2,1)S(1)}, bf16[3,256,128]{2,1,0:T(8,128)(2,1)S(1)}, u32[]{:S(2)}, u32[]{:S(2)}) collective-permute-start(bf16[3,256,128]{2,1,0:T(8,128)(2,1)S(1)} %pad_maximum_fusion.3), channel_id=1, source_target_pairs={{0,24},{4,28},{8,16},{12,20},{16,8},{20,12},{24,0},{28,4},{1,25},{... | collective-permute-start | bytes 589832 | tf_op jit(solution)/shard_map/ppermute | solution.py:182
  16.2 5.1 %collective-permute-start.5 = (bf16[2,256,128]{2,1,0:T(8,128)(2,1)S(1)}, bf16[2,256,128]{2,1,0:T(8,128)(2,1)S(1)}, u32[]{:S(2)}, u32[]{:S(2)}) collective-permute-start(bf16[2,256,128]{2,1,0:T(8,128)(2,1)S(1)} %pad_maximum_fusion.4), channel_id=1, source_target_pairs={{0,4},{4,0},{8,12},{12,8},{16,20},{20,16},{24,28},{28,24},{1,5},{5... | collective-permute-start | bytes 393224 | tf_op jit(solution)/shard_map/ppermute | solution.py:185
  20.1 1.3 %collective-permute-start.6 = (bf16[2,256,128]{2,1,0:T(8,128)(2,1)S(1)}, bf16[2,256,128]{2,1,0:T(8,128)(2,1)S(1)}, u32[]{:S(2)}, u32[]{:S(2)}) collective-permute-start(bf16[2,256,128]{2,1,0:T(8,128)(2,1)S(1)} %slice.30), channel_id=1, source_target_pairs={{0,4},{4,0},{8,12},{12,8},{16,20},{20,16},{24,28},{28,24},{1,5},{5... | collective-permute-start | bytes 393224 | tf_op jit(solution)/shard_map/ppermute | solution.py:185
  20.1 1.6 %collective-permute-start.7 = (bf16[2,256,128]{2,1,0:T(8,128)(2,1)S(1)}, bf16[2,256,128]{2,1,0:T(8,128)(2,1)S(1)}, u32[]{:S(2)}, u32[]{:S(2)}) collective-permute-start(bf16[2,256,128]{2,1,0:T(8,128)(2,1)S(1)} %slice.31), channel_id=1, source_target_pairs={{0,4},{4,0},{8,12},{12,8},{16,20},{20,16},{24,28},{28,24},{1,5},{5... | collective-permute-start | bytes 393224 | tf_op jit(solution)/shard_map/ppermute | solution.py:185
  20.7 1.4 %collective-permute-start.8 = (bf16[2,256,128]{2,1,0:T(8,128)(2,1)S(1)}, bf16[2,256,128]{2,1,0:T(8,128)(2,1)S(1)}, u32[]{:S(2)}, u32[]{:S(2)}) collective-permute-start(bf16[2,256,128]{2,1,0:T(8,128)(2,1)S(1)} %slice.25), channel_id=1, source_target_pairs={{0,4},{4,0},{8,12},{12,8},{16,20},{20,16},{24,28},{28,24},{1,5},{5... | collective-permute-start | bytes 393224 | tf_op jit(solution)/shard_map/ppermute | solution.py:185
  20.8 8.8 %collective-permute-start.9 = (bf16[256,512]{1,0:T(8,128)(2,1)S(1)}, bf16[256,512]{1,0:T(8,128)(2,1)S(1)}, u32[]{:S(2)}, u32[]{:S(2)}) collective-permute-start(bf16[256,512]{1,0:T(8,128)(2,1)S(1)} %collective-permute-done.3.refs_2_), channel_id=1, source_target_pairs={{0,1},{1,0},{2,3},{3,2},{4,5},{5,4},{6,7},{7,6},{8,9},{9,8},{10,11... | collective-permute-start | bytes 786440 | tf_op jit(solution)/shard_map/ppermute | solution.py:203
  24.6 7.9 %collective-permute-start.10 = (bf16[256,128]{1,0:T(8,128)(2,1)S(1)}, bf16[256,128]{1,0:T(8,128)(2,1)S(1)}, u32[]{:S(2)}, u32[]{:S(2)}) collective-permute-start(bf16[256,128]{1,0:T(8,128)(2,1)S(1)} %get-tuple-element.68), channel_id=1, source_target_pairs={{0,8},{4,12},{8,0},{12,4},{16,24},{20,28},{24,16},{28,20},{1,9},{5... | collective-permute-start | bytes 196616 | tf_op jit(solution)/shard_map/ppermute | solution.py:182
  25.4 8.5 %collective-permute-start.11 = (bf16[256,128]{1,0:T(8,128)(2,1)S(1)}, bf16[256,128]{1,0:T(8,128)(2,1)S(1)}, u32[]{:S(2)}, u32[]{:S(2)}) collective-permute-start(bf16[256,128]{1,0:T(8,128)(2,1)S(1)} %get-tuple-element.67), channel_id=1, source_target_pairs={{0,16},{4,20},{8,24},{12,28},{16,0},{20,4},{24,8},{28,12},{1,17},{... | collective-permute-start | bytes 196616 | tf_op jit(solution)/shard_map/ppermute | solution.py:182
  26.8 7.2 %collective-permute-start.12 = (bf16[256,128]{1,0:T(8,128)(2,1)S(1)}, bf16[256,128]{1,0:T(8,128)(2,1)S(1)}, u32[]{:S(2)}, u32[]{:S(2)}) collective-permute-start(bf16[256,128]{1,0:T(8,128)(2,1)S(1)} %get-tuple-element.66), channel_id=1, source_target_pairs={{0,24},{4,28},{8,16},{12,20},{16,8},{20,12},{24,0},{28,4},{1,25},{... | collective-permute-start | bytes 196616 | tf_op jit(solution)/shard_map/ppermute | solution.py:182
  30.4 5.0 %collective-permute-start.13 = (bf16[256,128]{1,0:T(8,128)(2,1)S(1)}, bf16[256,128]{1,0:T(8,128)(2,1)S(1)}, u32[]{:S(2)}, u32[]{:S(2)}) collective-permute-start(bf16[256,128]{1,0:T(8,128)(2,1)S(1)} %get-tuple-element.47), channel_id=1, source_target_pairs={{0,8},{4,12},{8,0},{12,4},{16,24},{20,28},{24,16},{28,20},{1,9},{5... | collective-permute-start | bytes 196616 | tf_op jit(solution)/shard_map/ppermute | solution.py:182
  31.0 5.8 %collective-permute-start.17 = (bf16[256,128]{1,0:T(8,128)(2,1)S(1)}, bf16[256,128]{1,0:T(8,128)(2,1)S(1)}, u32[]{:S(2)}, u32[]{:S(2)}) collective-permute-start(bf16[256,128]{1,0:T(8,128)(2,1)S(1)} %get-tuple-element.52), channel_id=1, source_target_pairs={{0,16},{4,20},{8,24},{12,28},{16,0},{20,4},{24,8},{28,12},{1,17},{... | collective-permute-start | bytes 196616 | tf_op jit(solution)/shard_map/ppermute | solution.py:182
  32.5 5.2 %collective-permute-start.18 = (bf16[256,128]{1,0:T(8,128)(2,1)S(1)}, bf16[256,128]{1,0:T(8,128)(2,1)S(1)}, u32[]{:S(2)}, u32[]{:S(2)}) collective-permute-start(bf16[256,128]{1,0:T(8,128)(2,1)S(1)} %get-tuple-element.53), channel_id=1, source_target_pairs={{0,24},{4,28},{8,16},{12,20},{16,8},{20,12},{24,0},{28,4},{1,25},{... | collective-permute-start | bytes 196616 | tf_op jit(solution)/shard_map/ppermute | solution.py:182
  34.7 9.3 %collective-permute-start.15 = (bf16[256,512]{1,0:T(8,128)(2,1)S(1)}, bf16[256,512]{1,0:T(8,128)(2,1)S(1)}, u32[]{:S(2)}, u32[]{:S(2)}) collective-permute-start(bf16[256,512]{1,0:T(8,128)(2,1)S(1)} %get-tuple-element.49), channel_id=1, source_target_pairs={{0,1},{1,0},{2,3},{3,2},{4,5},{5,4},{6,7},{7,6},{8,9},{9,8},{10,11... | collective-permute-start | bytes 786440 | tf_op jit(solution)/shard_map/ppermute | solution.py:203
  35.4 14.2 %collective-permute-start.14 = (bf16[256,512]{1,0:T(8,128)(2,1)S(1)}, bf16[256,512]{1,0:T(8,128)(2,1)S(1)}, u32[]{:S(2)}, u32[]{:S(2)}) collective-permute-start(bf16[256,512]{1,0:T(8,128)(2,1)S(1)} %get-tuple-element.48), channel_id=1, source_target_pairs={{0,1},{1,0},{2,3},{3,2},{4,5},{5,4},{6,7},{7,6},{8,9},{9,8},{10,11... | collective-permute-start | bytes 786440 | tf_op jit(solution)/shard_map/ppermute | solution.py:203
  41.0 3.5 %collective-permute-start.19 = (bf16[4,2,256,128]{3,2,1,0:T(8,128)(2,1)S(1)}, bf16[4,2,256,128]{3,2,1,0:T(8,128)(2,1)S(1)}, u32[]{:S(2)}, u32[]{:S(2)}) collective-permute-start(bf16[4,2,256,128]{3,2,1,0:T(8,128)(2,1)S(1)} %get-tuple-element.61), channel_id=1, source_target_pairs={{0,4},{4,0},{8,12},{12,8},{16,20},{20,16},{24,28},{28,24},{1,5},{5... | collective-permute-start | bytes 1572872 | tf_op jit(solution)/shard_map/ppermute | solution.py:185
  44.1 12.4 %collective-permute-start.16 = (bf16[256,512]{1,0:T(8,128)(2,1)S(1)}, bf16[256,512]{1,0:T(8,128)(2,1)S(1)}, u32[]{:S(2)}, u32[]{:S(2)}) collective-permute-start(bf16[256,512]{1,0:T(8,128)(2,1)S(1)} %shard_map.96), channel_id=1, source_target_pairs={{0,2},{1,3},{2,0},{3,1},{4,6},{5,7},{6,4},{7,5},{8,10},{9,11},{10,... | collective-permute-start | bytes 786440 | tf_op jit(solution)/shard_map/ppermute | solution.py:203
  44.7 11.8 %collective-permute-start.20 = (bf16[3,256,128]{2,1,0:T(8,128)(2,1)S(1)}, bf16[3,256,128]{2,1,0:T(8,128)(2,1)S(1)}, u32[]{:S(2)}, u32[]{:S(2)}) collective-permute-start(bf16[3,256,128]{2,1,0:T(8,128)(2,1)S(1)} %get-tuple-element.63), channel_id=1, source_target_pairs={{0,8},{4,12},{8,0},{12,4},{16,24},{20,28},{24,16},{28,20},{1,9},{5... | collective-permute-start | bytes 589832 | tf_op jit(solution)/shard_map/ppermute | solution.py:182
  45.3 11.2 %collective-permute-start.21 = (bf16[3,256,128]{2,1,0:T(8,128)(2,1)S(1)}, bf16[3,256,128]{2,1,0:T(8,128)(2,1)S(1)}, u32[]{:S(2)}, u32[]{:S(2)}) collective-permute-start(bf16[3,256,128]{2,1,0:T(8,128)(2,1)S(1)} %get-tuple-element.64), channel_id=1, source_target_pairs={{0,16},{4,20},{8,24},{12,28},{16,0},{20,4},{24,8},{28,12},{1,17},{... | collective-permute-start | bytes 589832 | tf_op jit(solution)/shard_map/ppermute | solution.py:182
  46.8 9.7 %collective-permute-start.22 = (bf16[3,256,128]{2,1,0:T(8,128)(2,1)S(1)}, bf16[3,256,128]{2,1,0:T(8,128)(2,1)S(1)}, u32[]{:S(2)}, u32[]{:S(2)}) collective-permute-start(bf16[3,256,128]{2,1,0:T(8,128)(2,1)S(1)} %get-tuple-element.65), channel_id=1, source_target_pairs={{0,24},{4,28},{8,16},{12,20},{16,8},{20,12},{24,0},{28,4},{1,25},{... | collective-permute-start | bytes 589832 | tf_op jit(solution)/shard_map/ppermute | solution.py:182

commit v5 on v4

--- a/solution.py
+++ b/solution.py
@@ -105,20 +105,26 @@
             out[d, 1] = value_part.astype(out.dtype)
 
 
-def project_body(chips, groups, weight, *refs):
-    incoming, outs, joined = refs[:chips], refs[chips : chips + groups], refs[chips + groups]
-    chip = chip_index()
-    level = lax.axis_index("head")
+def join_body(chips, groups, weight, *refs):
+    incoming, joined, out = refs[:chips], refs[chips], refs[chips + 1]
+    chip = chip_index()
     width = incoming[0].shape[1]
     for d in range(chips):
         lanes = pl.ds(pl.multiple_of((chip ^ d) * width, width), width)
         joined[:, lanes] = incoming[d][...]
-    rows = joined[...]
-    for j in range(groups):
-        columns = outs[j].shape[1]
-        lanes = pl.ds(pl.multiple_of((level ^ j) * columns, columns), columns)
-        term = weight[:, :, lanes].reshape(chips * width, columns)
-        outs[j][...] = dot(rows, term).astype(LOW)
+    project_part(weight, joined[...], out, lax.axis_index("head") ^ (groups - 1))
+
+
+def project_part(weight, rows, out, index):
+    columns = out.shape[1]
+    lanes = pl.ds(pl.multiple_of(index * columns, columns), columns)
+    out[...] = dot(rows, weight[:, :, lanes].reshape(rows.shape[1], columns)).astype(LOW)
+
+
+def project_body(weight, joined, *outs):
+    level = lax.axis_index("head")
+    for j, out in enumerate(outs):
+        project_part(weight, joined[...], out, level ^ j)
 
 
 def grad_body(chips, groups, weight, *refs):
@@ -159,9 +165,8 @@
 
 
 def place_body(chips, *refs):
-    summands, pieces, projected, outs = refs[:3], refs[3 : 3 + chips], refs[3 + chips], refs[4 + chips :]
-    chip = chip_index()
-    sum_body(*summands, projected)
+    pieces, outs = refs[:chips], refs[chips:]
+    chip = chip_index()
     for d in range(chips):
         for kind in range(3):
             outs[kind][chip ^ d] = pieces[d][kind]
@@ -246,17 +251,25 @@
     )
     incoming = exchange(grad_att)
     own_attended[0] = together(own_attended[0], grad_att[0])[0]
-    parts = call(
-        functools.partial(project_body, chips, groups),
-        tuple(shape((rows, columns), LOW) for _ in range(groups)),
+    block = shape((rows, columns), LOW)
+    joined, *parts = call(
+        functools.partial(join_body, chips, groups),
+        (shape((rows, heads * width), LOW), block),
         out_weight,
         *own_attended,
-        flops=2 * rows * heads * width * features,
-        moved=weight_bytes + 2 * rows * features + 4 * chips * tile,
-        scratch=[pltpu.VMEM((rows, heads * width), LOW)],
-    )
-    halfway = across(parts[3], 1)
-    neighbour = across(together(parts[1], incoming[1])[0], 1)
+        flops=2 * rows * heads * width * columns,
+        moved=weight_bytes // groups + 4 * chips * tile,
+    )
+    halfway = across(parts[0], 1)
+    parts = call(
+        project_body,
+        (block,) * (groups - 1),
+        out_weight,
+        joined,
+        flops=2 * rows * heads * width * (features - columns),
+        moved=weight_bytes + 2 * rows * features,
+    )
+    neighbour = across(together(parts[1], *incoming[2:])[0], 1)
     halfway = call(sum_body, shape((rows, columns), LOW), halfway, parts[2], flops=2**33, moved=2**28)
     incoming[0] = together(incoming[0], parts[0])[0]
     query_grad, own_part, sibling_part = call(
@@ -291,15 +304,16 @@
             moved=2 * 14 * chips * tile,
         )
     )
-    return call(
+    summands = [parts[0], neighbour, across(halfway, 2)]
+    gradients = call(
         functools.partial(place_body, chips),
-        (shape((rows, columns), LOW),) + (shape((heads, rows, width), LOW),) * 3,
-        parts[0],
-        neighbour,
-        across(halfway, 2),
+        (shape((heads, rows, width), LOW),) * 3,
         *returned,
         moved=2 * 6 * chips * tile,
     )
+    summands[0], *gradients = together(summands[0], *gradients)
+    projected = call(sum_body, block, *summands)
+    return (projected, *gradients)
 
 
 def partner(shard, axis, bit):
@@ -412,7 +426,7 @@
 
 def per_device(*arrays):
     chips = lax.axis_size("seq") // 2
-    square = chips == arrays[0].shape[0]
+    square = chips == arrays[0].shape[0] == lax.axis_size("head") == 4
     return (by_heads if square else by_routing)(*arrays)
 
 

time: 57.8 us -> 56.9 us (0.984)
  starting transfers between devices: 23.6 us -> 22.6 us
  Pallas kernels: 8.63 us -> 9.46 us
    ppermute x6, waiting for transfers between devices: 12.6 us -> 3.76 us  [along(): return lax.ppermute(array, 'head', pairs)]
    ppermute x12, waiting for transfers between devices: 8.92 us -> 17.5 us  [to_chip(): return lax.ppermute(array, 'seq', [(i, i ^ 2 * d) for i in range(devices)])]
    ppermute x6, starting transfers between devices: 8.56 us -> 7.57 us  [along(): return lax.ppermute(array, 'head', pairs)]
    pallas_call x7 -> x9, Pallas kernels: 8.63 us -> 9.46 us  [call(): pl.pallas_call(body, out_shape=outs, in_specs=[scalar if i in smem else v...]
  transfers between devices with their start and end apart: 23 -> 23, of which waited for: 11 -> 11; matrix products, arithmetic and copies ran while one was open for 4% -> 4% of each run, Pallas kernels for 13% -> 15%
where the time goes in v5:
time: 56.9 us; the launch traced here: 56.7 us
  starting transfers between devices  22.6 us (40%)
  waiting for transfers between devices  21.7 us (38%)
  Pallas kernels  9.46 us (17%)
  local copies, waits for them, and re-layouts  2.14 us (4%)
  between operations  0.76 us (1%)
    ppermute x12, waiting for transfers between devices, to_chip(): return lax.ppermute(array, 'seq', [(i, i ^ 2 * d) for i in range(devices)])  17.5 us
    ppermute x12, starting transfers between devices, to_chip(): return lax.ppermute(array, 'seq', [(i, i ^ 2 * d) for i in range(devices)])  14.4 us
    pallas_call x9, Pallas kernels, call(): pl.pallas_call(body, out_shape=outs, in_specs=[scalar if i in smem else v...  9.46 us
    ppermute x6, starting transfers between devices, along(): return lax.ppermute(array, 'head', pairs)  7.57 us
    ppermute x6, waiting for transfers between devices, along(): return lax.ppermute(array, 'head', pairs)  3.76 us
    dynamic_slice x2, local copies, waits for them, and re-layouts, head_piece(): lax.dynamic_index_in_dim(a, h, 0, keepdims=False)  2.08 us
  transfers between devices with their start and end apart: 23, of which 11 were waited for; matrix products, arithmetic and copies ran while one was open for 4% of the time, Pallas kernels for 15%

profile of v5, /device:TPU:0, one launch (start us, length us, event | category | flops | bytes accessed | tf_op | source)
XLA Modules:
  0.0 56.7 jit_solution(3981702687635723588)
XLA Ops:
  0.6 4.1 %collective-permute-start.3 = (bf16[256,512]{1,0:T(8,128)(2,1)}, bf16[256,512]{1,0:T(8,128)(2,1)S(1)}, u32[]{:S(2)}, u32[]{:S(2)}) collective-permute-start(bf16[256,512]{1,0:T(8,128)(2,1)} %refs_0_), channel_id=1, source_target_pairs={{0,2},{1,3},{2,0},{3,1},{4,6},{5,7},{6,4},{7,5},{8,10},{9,11},{10,... | collective-permute-start | bytes 786440 | tf_op jit(solution)/shard_map/ppermute | solution.py:208
  4.7 1.6 %collective-permute-start.4 = (bf16[256,512]{1,0:T(8,128)(2,1)}, bf16[256,512]{1,0:T(8,128)(2,1)S(1)}, u32[]{:S(2)}, u32[]{:S(2)}) collective-permute-start(bf16[256,512]{1,0:T(8,128)(2,1)} %refs_0_), channel_id=1, source_target_pairs={{0,1},{1,0},{2,3},{3,2},{4,5},{5,4},{6,7},{7,6},{8,9},{9,8},{10,11... | collective-permute-start | bytes 786440 | tf_op jit(solution)/shard_map/ppermute | solution.py:208
  6.3 0.0 copy-start.2
  6.3 1.0 %constant_dynamic-slice_fusion.2 = (bf16[1,256,128]{2,1,0:T(8,128)(2,1)S(1)}, bf16[1,256,128]{2,1,0:T(8,128)(2,1)S(1)}, bf16[1,256,128]{2,1,0:T(8,128)(2,1)S(1)}, bf16[1,256,128]{2,1,0:T(8,128)(2,1)S(1)}) fusion(bf16[4,256,128]{2,1,0:T(8,128)(2,1)} %param.7, s32[]{:T(128)S(6)} %select_n.30, s32[]{:T(128)S(6)} %select_n.28, s32[]{:T(128)S(6)} %select_n.27, ...), kind=kLoop, calls=%fused_computation.11 | loop fusion | bytes 524304 | tf_op jit(solution)/shard_map/jit(dynamic_index_in_dim)/dynamic_slice | solution.py:202
  7.3 1.1 %constant_dynamic-slice_fusion = (bf16[1,256,128]{2,1,0:T(8,128)(2,1)S(1)}, bf16[1,256,128]{2,1,0:T(8,128)(2,1)S(1)}, bf16[1,256,128]{2,1,0:T(8,128)(2,1)S(1)}, ...) fusion(bf16[4,256,128]{2,1,0:T(8,128)(2,1)} %param.6, ...), kind=kLoop, calls=%fused_computation.9 | loop fusion | bytes 1048592 | tf_op jit(solution)/shard_map/jit(dynamic_index_in_dim)/dynamic_slice | solution.py:202
  8.4 1.6 %collective-permute-start.1 = (bf16[3,256,128]{2,1,0:T(8,128)(2,1)S(1)}, bf16[3,256,128]{2,1,0:T(8,128)(2,1)S(1)}, u32[]{:S(2)}, u32[]{:S(2)}) collective-permute-start(bf16[3,256,128]{2,1,0:T(8,128)(2,1)S(1)} %pad_maximum_fusion.2), channel_id=1, source_target_pairs={{0,16},{4,20},{8,24},{12,28},{16,0},{20,4},{24,8},{28,12},{1,17},{... | collective-permute-start | bytes 589832 | tf_op jit(solution)/shard_map/ppermute | solution.py:187
  10.0 1.6 %collective-permute-start = (bf16[3,256,128]{2,1,0:T(8,128)(2,1)S(1)}, bf16[3,256,128]{2,1,0:T(8,128)(2,1)S(1)}, u32[]{:S(2)}, u32[]{:S(2)}) collective-permute-start(bf16[3,256,128]{2,1,0:T(8,128)(2,1)S(1)} %pad_maximum_fusion.1), channel_id=1, source_target_pairs={{0,8},{4,12},{8,0},{12,4},{16,24},{20,28},{24,16},{28,20},{1,9},{5... | collective-permute-start | bytes 589832 | tf_op jit(solution)/shard_map/ppermute | solution.py:187
  11.6 0.0 copy-start
  11.6 0.0 copy-start.1
  11.6 0.5 collective-permute-start.2
  12.2 3.1 %collective-permute-done.1.refs_2_ = bf16[3,256,128]{2,1,0:T(8,128)(2,1)S(1)} collective-permute-done((bf16[3,256,128]{2,1,0:T(8,128)(2,1)S(1)}, bf16[3,256,128]{2,1,0:T(8,128)(2,1)S(1)}, u32[]{:S(2)}, u32[]{:S(2)}) %collective-permute-start.1) | collective-permute-done | bytes 196640 | tf_op jit(solution)/shard_map/ppermute | solution.py:187
  15.2 0.0 collective-permute-start.5
  15.3 2.7 %collective-permute-done.refs_1_ = bf16[3,256,128]{2,1,0:T(8,128)(2,1)S(1)} collective-permute-done((bf16[3,256,128]{2,1,0:T(8,128)(2,1)S(1)}, bf16[3,256,128]{2,1,0:T(8,128)(2,1)S(1)}, u32[]{:S(2)}, u32[]{:S(2)}) %collective-permute-start) | collective-permute-done | bytes 196640 | tf_op jit(solution)/shard_map/ppermute | solution.py:187
  17.9 0.0 collective-permute-start.7
  18.0 2.1 %collective-permute-done.2.refs_3_ = bf16[3,256,128]{2,1,0:T(8,128)(2,1)S(1)} collective-permute-done((bf16[3,256,128]{2,1,0:T(8,128)(2,1)S(1)}, bf16[3,256,128]{2,1,0:T(8,128)(2,1)S(1)}, u32[]{:S(2)}, u32[]{:S(2)}) %collective-permute-start.2) | collective-permute-done | bytes 196640 | tf_op jit(solution)/shard_map/ppermute | solution.py:187
  20.1 0.0 collective-permute-start.6
  20.1 0.0 collective-permute-done.3.refs_2_
  20.1 0.0 collective-permute-done.4.refs_1_
  20.1 0.6 collective-permute-start.8
  20.7 0.5 collective-permute-start.9
  21.2 0.0 collective-permute-done.5.refs_4_
  21.2 0.0 collective-permute-done.7.refs_6_
  21.2 0.2 collective-permute-done.6.refs_5_
  21.4 0.2 collective-permute-done.8.refs_7_
  21.6 0.0 copy-done.2
  21.7 2.5 %shard_map.93 = (bf16[4,256,128]{2,1,0:T(8,128)(2,1)S(1)}, bf16[4,256,1024]{2,1,0:T(8,128)(2,1)S(1)}, bf16[4,2,512,128]{3,2,1,0:T(8,128)(2,1)S(1)}, bf16[4,256,128]{2,1,0:T(8,128)(2,1)S(1)}, f32[4,256,128]{2,1,0:T(8,128)S(1)}) custom-call(s32[4,4]{1,0:T(4,128)S(1)} %copy-done.2, bf16[3,256,128]{2,1,0:T(8,128)(2,1)S(1)} %pad_maximum_fusion.refs_0_, ...), custom_call_target="tpu_custom_call" | custom-call | flops 536870912 | bytes 5767168 | tf_op jit(solution)/shard_map/pallas_call | solution.py:29
  24.2 2.5 %collective-permute-start.12 = (bf16[256,128]{1,0:T(8,128)(2,1)S(1)}, bf16[256,128]{1,0:T(8,128)(2,1)S(1)}, u32[]{:S(2)}, u32[]{:S(2)}) collective-permute-start(bf16[256,128]{1,0:T(8,128)(2,1)S(1)} %get-tuple-element.82), channel_id=1, source_target_pairs={{0,24},{4,28},{8,16},{12,20},{16,8},{20,12},{24,0},{28,4},{1,25},{... | collective-permute-start | bytes 196616 | tf_op jit(solution)/shard_map/ppermute | solution.py:187
  26.7 0.5 collective-permute-start.11
  27.2 0.5 collective-permute-start.10
  27.7 1.3 %collective-permute-done.9.refs_3_ = bf16[256,512]{1,0:T(8,128)(2,1)S(1)} collective-permute-done((bf16[256,512]{1,0:T(8,128)(2,1)S(1)}, bf16[256,512]{1,0:T(8,128)(2,1)S(1)}, u32[]{:S(2)}, u32[]{:S(2)}) %collective-permute-start.9) | collective-permute-done | bytes 262176 | tf_op jit(solution)/shard_map/ppermute | solution.py:208
  29.0 0.0 copy-done
  29.0 0.0 copy-done.1
  29.0 0.8 %shard_map.94 = (bf16[256,128]{1,0:T(8,128)(2,1)S(1)}, bf16[256,128]{1,0:T(8,128)(2,1)S(1)}, bf16[256,128]{1,0:T(8,128)(2,1)S(1)}, bf16[256,128]{1,0:T(8,128)(2,1)S(1)}) custom-call(bf16[4,128,2048]{2,1,0:T(8,128)(2,1)S(1)} %copy-done, bf16[256,512]{1,0:T(8,128)(2,1)S(1)} %copy-done.1, bf16[256,512]{1,0:T(8,128)(2,1)S(1)} %collective-permute-done.4.refs_1_, ...), custom_call_target="tpu_custom_call" | custom-call | flops 536870912 | bytes 3932160 | tf_op jit(solution)/shard_map/pallas_call | solution.py:29
  29.8 1.6 %collective-permute-start.14 = (bf16[256,128]{1,0:T(8,128)(2,1)S(1)}, bf16[256,128]{1,0:T(8,128)(2,1)S(1)}, u32[]{:S(2)}, u32[]{:S(2)}) collective-permute-start(bf16[256,128]{1,0:T(8,128)(2,1)S(1)} %get-tuple-element.57), channel_id=1, source_target_pairs={{0,16},{4,20},{8,24},{12,28},{16,0},{20,4},{24,8},{28,12},{1,17},{... | collective-permute-start | bytes 196616 | tf_op jit(solution)/shard_map/ppermute | solution.py:187
  31.4 1.4 %collective-permute-start.15 = (bf16[256,128]{1,0:T(8,128)(2,1)S(1)}, bf16[256,128]{1,0:T(8,128)(2,1)S(1)}, u32[]{:S(2)}, u32[]{:S(2)}) collective-permute-start(bf16[256,128]{1,0:T(8,128)(2,1)S(1)} %get-tuple-element.58), channel_id=1, source_target_pairs={{0,24},{4,28},{8,16},{12,20},{16,8},{20,12},{24,0},{28,4},{1,25},{... | collective-permute-start | bytes 196616 | tf_op jit(solution)/shard_map/ppermute | solution.py:187
  32.8 0.0 collective-permute-done.12.refs_3_
  32.8 0.5 collective-permute-start.13
  33.3 0.0 collective-permute-done.11.refs_2_
  33.3 0.0 collective-permute-done.10.refs_1_
  33.3 0.3 shard_map.95
  33.7 0.5 collective-permute-start.21
  34.2 0.6 %shard_map.96 = (bf16[256,512]{1,0:T(8,128)(2,1)S(1)}, bf16[256,512]{1,0:T(8,128)(2,1)S(1)}, bf16[256,512]{1,0:T(8,128)(2,1)S(1)}) custom-call(bf16[4,128,2048]{2,1,0:T(8,128)(2,1)S(1)} %copy-done, bf16[256,512]{1,0:T(8,128)(2,1)S(1)} %get-tuple-element.53.joined), custom_call_target="tpu_custom_call" | custom-call | flops 402653184 | bytes 3145728 | tf_op jit(solution)/shard_map/pallas_call | solution.py:29
  34.8 0.0 collective-permute-done.14.refs_2_
  34.8 1.7 %collective-permute-done.15.refs_3_ = bf16[256,128]{1,0:T(8,128)(2,1)S(1)} collective-permute-done((bf16[256,128]{1,0:T(8,128)(2,1)S(1)}, bf16[256,128]{1,0:T(8,128)(2,1)S(1)}, u32[]{:S(2)}, u32[]{:S(2)}) %collective-permute-start.15) | collective-permute-done | bytes 65568 | tf_op jit(solution)/shard_map/ppermute | solution.py:187
  36.5 0.4 collective-permute-start.20
  37.0 0.1 collective-permute-done.13.refs_1_
  37.1 3.4 %shard_map.97 = (bf16[4,256,128]{2,1,0:T(8,128)(2,1)S(1)}, f32[4,2,256,128]{3,2,1,0:T(8,128)S(1)}, bf16[4,2,256,128]{3,2,1,0:T(8,128)(2,1)S(1)}) custom-call(s32[4,4]{1,0:T(4,128)S(1)} %copy-done.2, bf16[256,128]{1,0:T(8,128)(2,1)S(1)} %get-tuple-element.55.refs_0_, bf16[256,128]{1,0:T(8,128)(2,1)S(1)} %collective-permute-done.13.refs_1_, ...), custom_call_target="tpu_custom_call" | custom-call | flops 8589934592 | bytes 7340032 | tf_op jit(solution)/shard_map/pallas_call | solution.py:29
  40.4 0.1 collective-permute-start.16
  40.5 2.5 %collective-permute-done.21.refs_0_ = bf16[256,512]{1,0:T(8,128)(2,1)S(1)} collective-permute-done((bf16[256,512]{1,0:T(8,128)(2,1)S(1)}, bf16[256,512]{1,0:T(8,128)(2,1)S(1)}, u32[]{:S(2)}, u32[]{:S(2)}) %collective-permute-start.21) | collective-permute-done | bytes 262176 | tf_op jit(solution)/shard_map/ppermute | solution.py:208
  43.0 0.1 shard_map.100
  43.1 0.4 collective-permute-start.22
  43.5 0.0 collective-permute-done.16.arrived
  43.5 0.1 shard_map.98
  43.6 1.6 %collective-permute-start.17 = (bf16[3,256,128]{2,1,0:T(8,128)(2,1)S(1)}, bf16[3,256,128]{2,1,0:T(8,128)(2,1)S(1)}, u32[]{:S(2)}, u32[]{:S(2)}) collective-permute-start(bf16[3,256,128]{2,1,0:T(8,128)(2,1)S(1)} %get-tuple-element.68), channel_id=1, source_target_pairs={{0,8},{4,12},{8,0},{12,4},{16,24},{20,28},{24,16},{28,20},{1,9},{5... | collective-permute-start | bytes 589832 | tf_op jit(solution)/shard_map/ppermute | solution.py:187
  45.2 1.5 %collective-permute-start.18 = (bf16[3,256,128]{2,1,0:T(8,128)(2,1)S(1)}, bf16[3,256,128]{2,1,0:T(8,128)(2,1)S(1)}, u32[]{:S(2)}, u32[]{:S(2)}) collective-permute-start(bf16[3,256,128]{2,1,0:T(8,128)(2,1)S(1)} %get-tuple-element.69), channel_id=1, source_target_pairs={{0,16},{4,20},{8,24},{12,28},{16,0},{20,4},{24,8},{28,12},{1,17},{... | collective-permute-start | bytes 589832 | tf_op jit(solution)/shard_map/ppermute | solution.py:187
  46.7 0.5 collective-permute-start.19
  47.2 4.3 %collective-permute-done.17.refs_1_ = bf16[3,256,128]{2,1,0:T(8,128)(2,1)S(1)} collective-permute-done((bf16[3,256,128]{2,1,0:T(8,128)(2,1)S(1)}, bf16[3,256,128]{2,1,0:T(8,128)(2,1)S(1)}, u32[]{:S(2)}, u32[]{:S(2)}) %collective-permute-start.17) | collective-permute-done | bytes 196640 | tf_op jit(solution)/shard_map/ppermute | solution.py:187
  51.5 3.5 %collective-permute-done.18.refs_2_ = bf16[3,256,128]{2,1,0:T(8,128)(2,1)S(1)} collective-permute-done((bf16[3,256,128]{2,1,0:T(8,128)(2,1)S(1)}, bf16[3,256,128]{2,1,0:T(8,128)(2,1)S(1)}, u32[]{:S(2)}, u32[]{:S(2)}) %collective-permute-start.18) | collective-permute-done | bytes 196640 | tf_op jit(solution)/shard_map/ppermute | solution.py:187
  55.0 0.0 collective-permute-done.19.refs_3_
  55.0 0.9 %shard_map.99 = (bf16[4,256,128]{2,1,0:T(8,128)(2,1)}, bf16[4,256,128]{2,1,0:T(8,128)(2,1)}, bf16[4,256,128]{2,1,0:T(8,128)(2,1)}) custom-call(bf16[3,256,128]{2,1,0:T(8,128)(2,1)S(1)} %get-tuple-element.67.refs_0_, bf16[3,256,128]{2,1,0:T(8,128)(2,1)S(1)} %collective-permute-done.17.refs_1_, bf16[3,256,128]{2,1,0:T(8,128)(2,1)S(1)} %collective-permute-done.18.refs_2_, ...), custom_call_target="tpu_custom_call" | custom-call | bytes 1572864 | tf_op jit(solution)/shard_map/pallas_call | solution.py:29
  55.9 0.0 collective-permute-done.20.refs_1_
  55.9 0.0 collective-permute-done.22.refs_2_
  55.9 0.8 %shard_map.101 = bf16[256,512]{1,0:T(8,128)(2,1)} custom-call(bf16[256,512]{1,0:T(8,128)(2,1)S(1)} %get-tuple-element.74.refs_0_, bf16[256,512]{1,0:T(8,128)(2,1)S(1)} %collective-permute-done.20.refs_1_, bf16[256,512]{1,0:T(8,128)(2,1)S(1)} %collective-permute-done.22.refs_2_), custom_call_target="tpu_custom_call" | custom-call | tf_op jit(solution)/shard_map/pallas_call | solution.py:29
  (9 shorter events, 0.2 us)
Async XLA Ops:
  0.6 19.4 %collective-permute-start.3 = (bf16[256,512]{1,0:T(8,128)(2,1)}, bf16[256,512]{1,0:T(8,128)(2,1)S(1)}, u32[]{:S(2)}, u32[]{:S(2)}) collective-permute-start(bf16[256,512]{1,0:T(8,128)(2,1)} %refs_0_), channel_id=1, source_target_pairs={{0,2},{1,3},{2,0},{3,1},{4,6},{5,7},{6,4},{7,5},{8,10},{9,11},{10,... | collective-permute-start | bytes 786440 | tf_op jit(solution)/shard_map/ppermute | solution.py:208
  4.7 15.3 %collective-permute-start.4 = (bf16[256,512]{1,0:T(8,128)(2,1)}, bf16[256,512]{1,0:T(8,128)(2,1)S(1)}, u32[]{:S(2)}, u32[]{:S(2)}) collective-permute-start(bf16[256,512]{1,0:T(8,128)(2,1)} %refs_0_), channel_id=1, source_target_pairs={{0,1},{1,0},{2,3},{3,2},{4,5},{5,4},{6,7},{7,6},{8,9},{9,8},{10,11... | collective-permute-start | bytes 786440 | tf_op jit(solution)/shard_map/ppermute | solution.py:208
  6.3 15.3 %copy-start.2 = (s32[4,4]{1,0:T(4,128)S(1)}, s32[4,4]{1,0:T(4,128)}, u32[]{:S(2)}) copy-start(s32[4,4]{1,0:T(4,128)} %perm.3) | copy-start | bytes 196
  8.4 6.8 %collective-permute-start.1 = (bf16[3,256,128]{2,1,0:T(8,128)(2,1)S(1)}, bf16[3,256,128]{2,1,0:T(8,128)(2,1)S(1)}, u32[]{:S(2)}, u32[]{:S(2)}) collective-permute-start(bf16[3,256,128]{2,1,0:T(8,128)(2,1)S(1)} %pad_maximum_fusion.2), channel_id=1, source_target_pairs={{0,16},{4,20},{8,24},{12,28},{16,0},{20,4},{24,8},{28,12},{1,17},{... | collective-permute-start | bytes 589832 | tf_op jit(solution)/shard_map/ppermute | solution.py:187
  10.0 7.9 %collective-permute-start = (bf16[3,256,128]{2,1,0:T(8,128)(2,1)S(1)}, bf16[3,256,128]{2,1,0:T(8,128)(2,1)S(1)}, u32[]{:S(2)}, u32[]{:S(2)}) collective-permute-start(bf16[3,256,128]{2,1,0:T(8,128)(2,1)S(1)} %pad_maximum_fusion.1), channel_id=1, source_target_pairs={{0,8},{4,12},{8,0},{12,4},{16,24},{20,28},{24,16},{28,20},{1,9},{5... | collective-permute-start | bytes 589832 | tf_op jit(solution)/shard_map/ppermute | solution.py:187
  11.6 17.4 %copy-start = (bf16[4,128,2048]{2,1,0:T(8,128)(2,1)S(1)}, bf16[4,128,2048]{2,1,0:T(8,128)(2,1)}, u32[]{:S(2)}) copy-start(bf16[4,128,2048]{2,1,0:T(8,128)(2,1)} %weight.5) | copy-start | bytes 6291460
  11.6 17.4 %copy-start.1 = (bf16[256,512]{1,0:T(8,128)(2,1)S(1)}, bf16[256,512]{1,0:T(8,128)(2,1)}, u32[]{:S(2)}) copy-start(bf16[256,512]{1,0:T(8,128)(2,1)} %refs_0_) | copy-start | bytes 786436
  11.6 8.4 %collective-permute-start.2 = (bf16[3,256,128]{2,1,0:T(8,128)(2,1)S(1)}, bf16[3,256,128]{2,1,0:T(8,128)(2,1)S(1)}, u32[]{:S(2)}, u32[]{:S(2)}) collective-permute-start(bf16[3,256,128]{2,1,0:T(8,128)(2,1)S(1)} %pad_maximum_fusion.3), channel_id=1, source_target_pairs={{0,24},{4,28},{8,16},{12,20},{16,8},{20,12},{24,0},{28,4},{1,25},{... | collective-permute-start | bytes 589832 | tf_op jit(solution)/shard_map/ppermute | solution.py:187
  15.2 6.0 %collective-permute-start.5 = (bf16[2,256,128]{2,1,0:T(8,128)(2,1)S(1)}, bf16[2,256,128]{2,1,0:T(8,128)(2,1)S(1)}, u32[]{:S(2)}, u32[]{:S(2)}) collective-permute-start(bf16[2,256,128]{2,1,0:T(8,128)(2,1)S(1)} %pad_maximum_fusion.4), channel_id=1, source_target_pairs={{0,4},{4,0},{8,12},{12,8},{16,20},{20,16},{24,28},{28,24},{1,5},{5... | collective-permute-start | bytes 393224 | tf_op jit(solution)/shard_map/ppermute | solution.py:190
  17.9 3.3 %collective-permute-start.7 = (bf16[2,256,128]{2,1,0:T(8,128)(2,1)S(1)}, bf16[2,256,128]{2,1,0:T(8,128)(2,1)S(1)}, u32[]{:S(2)}, u32[]{:S(2)}) collective-permute-start(bf16[2,256,128]{2,1,0:T(8,128)(2,1)S(1)} %slice.31), channel_id=1, source_target_pairs={{0,4},{4,0},{8,12},{12,8},{16,20},{20,16},{24,28},{28,24},{1,5},{5... | collective-permute-start | bytes 393224 | tf_op jit(solution)/shard_map/ppermute | solution.py:190
  20.1 1.3 %collective-permute-start.6 = (bf16[2,256,128]{2,1,0:T(8,128)(2,1)S(1)}, bf16[2,256,128]{2,1,0:T(8,128)(2,1)S(1)}, u32[]{:S(2)}, u32[]{:S(2)}) collective-permute-start(bf16[2,256,128]{2,1,0:T(8,128)(2,1)S(1)} %slice.30), channel_id=1, source_target_pairs={{0,4},{4,0},{8,12},{12,8},{16,20},{20,16},{24,28},{28,24},{1,5},{5... | collective-permute-start | bytes 393224 | tf_op jit(solution)/shard_map/ppermute | solution.py:190
  20.1 1.6 %collective-permute-start.8 = (bf16[2,256,128]{2,1,0:T(8,128)(2,1)S(1)}, bf16[2,256,128]{2,1,0:T(8,128)(2,1)S(1)}, u32[]{:S(2)}, u32[]{:S(2)}) collective-permute-start(bf16[2,256,128]{2,1,0:T(8,128)(2,1)S(1)} %slice.25), channel_id=1, source_target_pairs={{0,4},{4,0},{8,12},{12,8},{16,20},{20,16},{24,28},{28,24},{1,5},{5... | collective-permute-start | bytes 393224 | tf_op jit(solution)/shard_map/ppermute | solution.py:190
  20.7 8.3 %collective-permute-start.9 = (bf16[256,512]{1,0:T(8,128)(2,1)S(1)}, bf16[256,512]{1,0:T(8,128)(2,1)S(1)}, u32[]{:S(2)}, u32[]{:S(2)}) collective-permute-start(bf16[256,512]{1,0:T(8,128)(2,1)S(1)} %collective-permute-done.3.refs_2_), channel_id=1, source_target_pairs={{0,1},{1,0},{2,3},{3,2},{4,5},{5,4},{6,7},{7,6},{8,9},{9,8},{10,11... | collective-permute-start | bytes 786440 | tf_op jit(solution)/shard_map/ppermute | solution.py:208
  24.2 8.6 %collective-permute-start.12 = (bf16[256,128]{1,0:T(8,128)(2,1)S(1)}, bf16[256,128]{1,0:T(8,128)(2,1)S(1)}, u32[]{:S(2)}, u32[]{:S(2)}) collective-permute-start(bf16[256,128]{1,0:T(8,128)(2,1)S(1)} %get-tuple-element.82), channel_id=1, source_target_pairs={{0,24},{4,28},{8,16},{12,20},{16,8},{20,12},{24,0},{28,4},{1,25},{... | collective-permute-start | bytes 196616 | tf_op jit(solution)/shard_map/ppermute | solution.py:187
  26.7 6.7 %collective-permute-start.11 = (bf16[256,128]{1,0:T(8,128)(2,1)S(1)}, bf16[256,128]{1,0:T(8,128)(2,1)S(1)}, u32[]{:S(2)}, u32[]{:S(2)}) collective-permute-start(bf16[256,128]{1,0:T(8,128)(2,1)S(1)} %get-tuple-element.83), channel_id=1, source_target_pairs={{0,16},{4,20},{8,24},{12,28},{16,0},{20,4},{24,8},{28,12},{1,17},{... | collective-permute-start | bytes 196616 | tf_op jit(solution)/shard_map/ppermute | solution.py:187
  27.2 6.2 %collective-permute-start.10 = (bf16[256,128]{1,0:T(8,128)(2,1)S(1)}, bf16[256,128]{1,0:T(8,128)(2,1)S(1)}, u32[]{:S(2)}, u32[]{:S(2)}) collective-permute-start(bf16[256,128]{1,0:T(8,128)(2,1)S(1)} %get-tuple-element.84), channel_id=1, source_target_pairs={{0,8},{4,12},{8,0},{12,4},{16,24},{20,28},{24,16},{28,20},{1,9},{5... | collective-permute-start | bytes 196616 | tf_op jit(solution)/shard_map/ppermute | solution.py:187
  29.8 5.0 %collective-permute-start.14 = (bf16[256,128]{1,0:T(8,128)(2,1)S(1)}, bf16[256,128]{1,0:T(8,128)(2,1)S(1)}, u32[]{:S(2)}, u32[]{:S(2)}) collective-permute-start(bf16[256,128]{1,0:T(8,128)(2,1)S(1)} %get-tuple-element.57), channel_id=1, source_target_pairs={{0,16},{4,20},{8,24},{12,28},{16,0},{20,4},{24,8},{28,12},{1,17},{... | collective-permute-start | bytes 196616 | tf_op jit(solution)/shard_map/ppermute | solution.py:187
  31.4 5.2 %collective-permute-start.15 = (bf16[256,128]{1,0:T(8,128)(2,1)S(1)}, bf16[256,128]{1,0:T(8,128)(2,1)S(1)}, u32[]{:S(2)}, u32[]{:S(2)}) collective-permute-start(bf16[256,128]{1,0:T(8,128)(2,1)S(1)} %get-tuple-element.58), channel_id=1, source_target_pairs={{0,24},{4,28},{8,16},{12,20},{16,8},{20,12},{24,0},{28,4},{1,25},{... | collective-permute-start | bytes 196616 | tf_op jit(solution)/shard_map/ppermute | solution.py:187
  32.8 4.3 %collective-permute-start.13 = (bf16[256,128]{1,0:T(8,128)(2,1)S(1)}, bf16[256,128]{1,0:T(8,128)(2,1)S(1)}, u32[]{:S(2)}, u32[]{:S(2)}) collective-permute-start(bf16[256,128]{1,0:T(8,128)(2,1)S(1)} %get-tuple-element.56), channel_id=1, source_target_pairs={{0,8},{4,12},{8,0},{12,4},{16,24},{20,28},{24,16},{28,20},{1,9},{5... | collective-permute-start | bytes 196616 | tf_op jit(solution)/shard_map/ppermute | solution.py:187
  33.7 9.3 %collective-permute-start.21 = (bf16[256,512]{1,0:T(8,128)(2,1)S(1)}, bf16[256,512]{1,0:T(8,128)(2,1)S(1)}, u32[]{:S(2)}, u32[]{:S(2)}) collective-permute-start(bf16[256,512]{1,0:T(8,128)(2,1)S(1)} %get-tuple-element.77), channel_id=1, source_target_pairs={{0,1},{1,0},{2,3},{3,2},{4,5},{5,4},{6,7},{7,6},{8,9},{9,8},{10,11... | collective-permute-start | bytes 786440 | tf_op jit(solution)/shard_map/ppermute | solution.py:208
  36.5 19.4 %collective-permute-start.20 = (bf16[256,512]{1,0:T(8,128)(2,1)S(1)}, bf16[256,512]{1,0:T(8,128)(2,1)S(1)}, u32[]{:S(2)}, u32[]{:S(2)}) collective-permute-start(bf16[256,512]{1,0:T(8,128)(2,1)S(1)} %get-tuple-element.76), channel_id=1, source_target_pairs={{0,1},{1,0},{2,3},{3,2},{4,5},{5,4},{6,7},{7,6},{8,9},{9,8},{10,11... | collective-permute-start | bytes 786440 | tf_op jit(solution)/shard_map/ppermute | solution.py:208
  40.4 3.0 %collective-permute-start.16 = (bf16[4,2,256,128]{3,2,1,0:T(8,128)(2,1)S(1)}, bf16[4,2,256,128]{3,2,1,0:T(8,128)(2,1)S(1)}, u32[]{:S(2)}, u32[]{:S(2)}) collective-permute-start(bf16[4,2,256,128]{3,2,1,0:T(8,128)(2,1)S(1)} %get-tuple-element.66), channel_id=1, source_target_pairs={{0,4},{4,0},{8,12},{12,8},{16,20},{20,16},{24,28},{28,24},{1,5},{5... | collective-permute-start | bytes 1572872 | tf_op jit(solution)/shard_map/ppermute | solution.py:190
  43.1 12.9 %collective-permute-start.22 = (bf16[256,512]{1,0:T(8,128)(2,1)S(1)}, bf16[256,512]{1,0:T(8,128)(2,1)S(1)}, u32[]{:S(2)}, u32[]{:S(2)}) collective-permute-start(bf16[256,512]{1,0:T(8,128)(2,1)S(1)} %shard_map.100), channel_id=1, source_target_pairs={{0,2},{1,3},{2,0},{3,1},{4,6},{5,7},{6,4},{7,5},{8,10},{9,11},{10,... | collective-permute-start | bytes 786440 | tf_op jit(solution)/shard_map/ppermute | solution.py:208
  43.6 7.8 %collective-permute-start.17 = (bf16[3,256,128]{2,1,0:T(8,128)(2,1)S(1)}, bf16[3,256,128]{2,1,0:T(8,128)(2,1)S(1)}, u32[]{:S(2)}, u32[]{:S(2)}) collective-permute-start(bf16[3,256,128]{2,1,0:T(8,128)(2,1)S(1)} %get-tuple-element.68), channel_id=1, source_target_pairs={{0,8},{4,12},{8,0},{12,4},{16,24},{20,28},{24,16},{28,20},{1,9},{5... | collective-permute-start | bytes 589832 | tf_op jit(solution)/shard_map/ppermute | solution.py:187
  45.2 9.8 %collective-permute-start.18 = (bf16[3,256,128]{2,1,0:T(8,128)(2,1)S(1)}, bf16[3,256,128]{2,1,0:T(8,128)(2,1)S(1)}, u32[]{:S(2)}, u32[]{:S(2)}) collective-permute-start(bf16[3,256,128]{2,1,0:T(8,128)(2,1)S(1)} %get-tuple-element.69), channel_id=1, source_target_pairs={{0,16},{4,20},{8,24},{12,28},{16,0},{20,4},{24,8},{28,12},{1,17},{... | collective-permute-start | bytes 589832 | tf_op jit(solution)/shard_map/ppermute | solution.py:187
  46.7 8.3 %collective-permute-start.19 = (bf16[3,256,128]{2,1,0:T(8,128)(2,1)S(1)}, bf16[3,256,128]{2,1,0:T(8,128)(2,1)S(1)}, u32[]{:S(2)}, u32[]{:S(2)}) collective-permute-start(bf16[3,256,128]{2,1,0:T(8,128)(2,1)S(1)} %get-tuple-element.70), channel_id=1, source_target_pairs={{0,24},{4,28},{8,16},{12,20},{16,8},{20,12},{24,0},{28,4},{1,25},{... | collective-permute-start | bytes 589832 | tf_op jit(solution)/shard_map/ppermute | solution.py:187

commit v6 on v5

--- a/solution.py
+++ b/solution.py
@@ -127,18 +127,24 @@
         project_part(weight, joined[...], out, level ^ j)
 
 
-def grad_body(chips, groups, weight, *refs):
-    slices, outs = refs[:groups], refs[groups:]
-    chip = chip_index()
+def slice_product(weight, block, index):
+    rows, columns = weight.shape[0] * weight.shape[1], block.shape[1]
+    lanes = pl.ds(pl.multiple_of(index * columns, columns), columns)
+    return dot(block[...], weight[:, :, lanes].reshape(rows, columns), NT)
+
+
+def partial_body(weight, *refs):
     level = lax.axis_index("head")
+    total = slice_product(weight, refs[0], level)
+    for j in range(1, len(refs) - 1):
+        total = total + slice_product(weight, refs[j], level ^ j)
+    refs[-1][...] = total
+
+
+def grad_body(chips, groups, weight, partial_grad, block, *outs):
+    chip = chip_index()
     width = outs[0].shape[1]
-    total = None
-    for j in range(groups):
-        block = slices[j][...]
-        columns = block.shape[1]
-        lanes = pl.ds(pl.multiple_of((level ^ j) * columns, columns), columns)
-        term = dot(block, weight[:, :, lanes].reshape(chips * width, columns), NT)
-        total = term if total is None else total + term
+    total = partial_grad[...] + slice_product(weight, block, lax.axis_index("head") ^ (groups - 1))
     total = total.astype(LOW)
     for c in range(chips):
 
@@ -240,14 +246,23 @@
     )
     weight_bytes = 2 * heads * width * features
     own_attended = exchange([attended[d] for d in range(chips)])
-    attended, *slices = together(attended, *slices)
+    attended, *slices[:-1] = together(attended, *slices[:-1])
+    partial_grad = call(
+        partial_body,
+        shape((rows, heads * width), F32),
+        out_weight,
+        *slices[:-1],
+        flops=2 * rows * heads * width * (features - columns),
+        moved=weight_bytes + 4 * rows * features,
+    )
     grad_att = call(
         functools.partial(grad_body, chips, groups),
         (piece,) * chips,
         out_weight,
-        *slices,
-        flops=2 * rows * heads * width * features,
-        moved=weight_bytes + 2 * rows * features + 6 * chips * tile,
+        partial_grad,
+        slices[-1],
+        flops=2 * rows * heads * width * columns,
+        moved=weight_bytes // groups + 4 * rows * features,
     )
     incoming = exchange(grad_att)
     own_attended[0] = together(own_attended[0], grad_att[0])[0]

time: 56.9 us -> 56.5 us (level)
  waiting for transfers between devices: 21.7 us -> 20.9 us
    ppermute x6, waiting for transfers between devices: 3.76 us -> 3.14 us  [along(): return lax.ppermute(array, 'head', pairs)]
    pallas_call x9 -> x10, Pallas kernels: 9.46 us -> 9.65 us  [call(): pl.pallas_call(body, out_shape=outs, in_specs=[scalar if i in smem else v...]
  transfers between devices with their start and end apart: 23 -> 23, of which waited for: 11 -> 10; matrix products, arithmetic and copies ran while one was open for 4% -> 4% of each run, Pallas kernels for 15% -> 16%
where the time goes in v6:
time: 56.5 us; the launch traced here: 56.3 us
  starting transfers between devices  22.7 us (40%)
  waiting for transfers between devices  20.9 us (37%)
  Pallas kernels  9.65 us (17%)
  local copies, waits for them, and re-layouts  2.14 us (4%)
  between operations  0.78 us (1%)
    ppermute x12, waiting for transfers between devices, to_chip(): return lax.ppermute(array, 'seq', [(i, i ^ 2 * d) for i in range(devices)])  17.3 us
    ppermute x12, starting transfers between devices, to_chip(): return lax.ppermute(array, 'seq', [(i, i ^ 2 * d) for i in range(devices)])  14.4 us
    pallas_call x10, Pallas kernels, call(): pl.pallas_call(body, out_shape=outs, in_specs=[scalar if i in smem else v...  9.65 us
    ppermute x6, starting transfers between devices, along(): return lax.ppermute(array, 'head', pairs)  7.73 us
    ppermute x6, waiting for transfers between devices, along(): return lax.ppermute(array, 'head', pairs)  3.14 us
    dynamic_slice x2, local copies, waits for them, and re-layouts, head_piece(): lax.dynamic_index_in_dim(a, h, 0, keepdims=False)  2.08 us
  transfers between devices with their start and end apart: 23, of which 10 were waited for; matrix products, arithmetic and copies ran while one was open for 4% of the time, Pallas kernels for 16%

profile of v6, /device:TPU:0, one launch (start us, length us, event | category | flops | bytes accessed | tf_op | source)
XLA Modules:
  0.0 56.3 jit_solution(16104019775325907016)
XLA Ops:
  0.6 4.1 %collective-permute-start.3 = (bf16[256,512]{1,0:T(8,128)(2,1)}, bf16[256,512]{1,0:T(8,128)(2,1)S(1)}, u32[]{:S(2)}, u32[]{:S(2)}) collective-permute-start(bf16[256,512]{1,0:T(8,128)(2,1)} %refs_0_), channel_id=1, source_target_pairs={{0,2},{1,3},{2,0},{3,1},{4,6},{5,7},{6,4},{7,5},{8,10},{9,11},{10,... | collective-permute-start | bytes 786440 | tf_op jit(solution)/shard_map/ppermute | solution.py:214
  4.7 1.6 %collective-permute-start.4 = (bf16[256,512]{1,0:T(8,128)(2,1)}, bf16[256,512]{1,0:T(8,128)(2,1)S(1)}, u32[]{:S(2)}, u32[]{:S(2)}) collective-permute-start(bf16[256,512]{1,0:T(8,128)(2,1)} %refs_0_), channel_id=1, source_target_pairs={{0,1},{1,0},{2,3},{3,2},{4,5},{5,4},{6,7},{7,6},{8,9},{9,8},{10,11... | collective-permute-start | bytes 786440 | tf_op jit(solution)/shard_map/ppermute | solution.py:214
  6.3 0.0 copy-start.2
  6.3 1.0 %constant_dynamic-slice_fusion.2 = (bf16[1,256,128]{2,1,0:T(8,128)(2,1)S(1)}, bf16[1,256,128]{2,1,0:T(8,128)(2,1)S(1)}, bf16[1,256,128]{2,1,0:T(8,128)(2,1)S(1)}, bf16[1,256,128]{2,1,0:T(8,128)(2,1)S(1)}) fusion(bf16[4,256,128]{2,1,0:T(8,128)(2,1)} %param.7, s32[]{:T(128)S(6)} %select_n.30, s32[]{:T(128)S(6)} %select_n.28, s32[]{:T(128)S(6)} %select_n.27, ...), kind=kLoop, calls=%fused_computation.11 | loop fusion | bytes 524304 | tf_op jit(solution)/shard_map/jit(dynamic_index_in_dim)/dynamic_slice | solution.py:208
  7.3 1.1 %constant_dynamic-slice_fusion = (bf16[1,256,128]{2,1,0:T(8,128)(2,1)S(1)}, bf16[1,256,128]{2,1,0:T(8,128)(2,1)S(1)}, bf16[1,256,128]{2,1,0:T(8,128)(2,1)S(1)}, ...) fusion(bf16[4,256,128]{2,1,0:T(8,128)(2,1)} %param.6, ...), kind=kLoop, calls=%fused_computation.9 | loop fusion | bytes 1048592 | tf_op jit(solution)/shard_map/jit(dynamic_index_in_dim)/dynamic_slice | solution.py:208
  8.4 1.6 %collective-permute-start.1 = (bf16[3,256,128]{2,1,0:T(8,128)(2,1)S(1)}, bf16[3,256,128]{2,1,0:T(8,128)(2,1)S(1)}, u32[]{:S(2)}, u32[]{:S(2)}) collective-permute-start(bf16[3,256,128]{2,1,0:T(8,128)(2,1)S(1)} %pad_maximum_fusion.2), channel_id=1, source_target_pairs={{0,16},{4,20},{8,24},{12,28},{16,0},{20,4},{24,8},{28,12},{1,17},{... | collective-permute-start | bytes 589832 | tf_op jit(solution)/shard_map/ppermute | solution.py:193
  10.0 1.6 %collective-permute-start = (bf16[3,256,128]{2,1,0:T(8,128)(2,1)S(1)}, bf16[3,256,128]{2,1,0:T(8,128)(2,1)S(1)}, u32[]{:S(2)}, u32[]{:S(2)}) collective-permute-start(bf16[3,256,128]{2,1,0:T(8,128)(2,1)S(1)} %pad_maximum_fusion.1), channel_id=1, source_target_pairs={{0,8},{4,12},{8,0},{12,4},{16,24},{20,28},{24,16},{28,20},{1,9},{5... | collective-permute-start | bytes 589832 | tf_op jit(solution)/shard_map/ppermute | solution.py:193
  11.6 0.0 copy-start
  11.6 0.0 copy-start.1
  11.6 0.5 collective-permute-start.2
  12.2 3.1 %collective-permute-done.1.refs_2_ = bf16[3,256,128]{2,1,0:T(8,128)(2,1)S(1)} collective-permute-done((bf16[3,256,128]{2,1,0:T(8,128)(2,1)S(1)}, bf16[3,256,128]{2,1,0:T(8,128)(2,1)S(1)}, u32[]{:S(2)}, u32[]{:S(2)}) %collective-permute-start.1) | collective-permute-done | bytes 196640 | tf_op jit(solution)/shard_map/ppermute | solution.py:193
  15.2 0.0 collective-permute-start.5
  15.3 2.7 %collective-permute-done.refs_1_ = bf16[3,256,128]{2,1,0:T(8,128)(2,1)S(1)} collective-permute-done((bf16[3,256,128]{2,1,0:T(8,128)(2,1)S(1)}, bf16[3,256,128]{2,1,0:T(8,128)(2,1)S(1)}, u32[]{:S(2)}, u32[]{:S(2)}) %collective-permute-start) | collective-permute-done | bytes 196640 | tf_op jit(solution)/shard_map/ppermute | solution.py:193
  17.9 0.0 collective-permute-start.7
  18.0 2.1 %collective-permute-done.2.refs_3_ = bf16[3,256,128]{2,1,0:T(8,128)(2,1)S(1)} collective-permute-done((bf16[3,256,128]{2,1,0:T(8,128)(2,1)S(1)}, bf16[3,256,128]{2,1,0:T(8,128)(2,1)S(1)}, u32[]{:S(2)}, u32[]{:S(2)}) %collective-permute-start.2) | collective-permute-done | bytes 196640 | tf_op jit(solution)/shard_map/ppermute | solution.py:193
  20.1 0.0 collective-permute-start.6
  20.1 0.0 collective-permute-done.3.refs_2_
  20.1 0.0 collective-permute-done.4.refs_1_
  20.1 0.6 %collective-permute-start.8 = (bf16[2,256,128]{2,1,0:T(8,128)(2,1)S(1)}, bf16[2,256,128]{2,1,0:T(8,128)(2,1)S(1)}, u32[]{:S(2)}, u32[]{:S(2)}) collective-permute-start(bf16[2,256,128]{2,1,0:T(8,128)(2,1)S(1)} %slice.25), channel_id=1, source_target_pairs={{0,4},{4,0},{8,12},{12,8},{16,20},{20,16},{24,28},{28,24},{1,5},{5... | collective-permute-start | bytes 393224 | tf_op jit(solution)/shard_map/ppermute | solution.py:196
  20.7 0.5 collective-permute-start.9
  21.2 0.0 collective-permute-done.5.refs_4_
  21.2 0.0 collective-permute-done.7.refs_6_
  21.2 0.2 collective-permute-done.6.refs_5_
  21.4 0.2 collective-permute-done.8.refs_7_
  21.6 0.0 copy-done.2
  21.7 2.5 %shard_map.93 = (bf16[4,256,128]{2,1,0:T(8,128)(2,1)S(1)}, bf16[4,256,1024]{2,1,0:T(8,128)(2,1)S(1)}, bf16[4,2,512,128]{3,2,1,0:T(8,128)(2,1)S(1)}, bf16[4,256,128]{2,1,0:T(8,128)(2,1)S(1)}, f32[4,256,128]{2,1,0:T(8,128)S(1)}) custom-call(s32[4,4]{1,0:T(4,128)S(1)} %copy-done.2, bf16[3,256,128]{2,1,0:T(8,128)(2,1)S(1)} %pad_maximum_fusion.refs_0_, ...), custom_call_target="tpu_custom_call" | custom-call | flops 536870912 | bytes 5767168 | tf_op jit(solution)/shard_map/pallas_call | solution.py:29
  24.2 2.5 %collective-permute-start.12 = (bf16[256,128]{1,0:T(8,128)(2,1)S(1)}, bf16[256,128]{1,0:T(8,128)(2,1)S(1)}, u32[]{:S(2)}, u32[]{:S(2)}) collective-permute-start(bf16[256,128]{1,0:T(8,128)(2,1)S(1)} %get-tuple-element.80), channel_id=1, source_target_pairs={{0,24},{4,28},{8,16},{12,20},{16,8},{20,12},{24,0},{28,4},{1,25},{... | collective-permute-start | bytes 196616 | tf_op jit(solution)/shard_map/ppermute | solution.py:193
  26.7 0.5 collective-permute-start.11
  27.2 0.5 collective-permute-start.10
  27.7 0.0 copy-done
  27.7 0.0 copy-done.1
  27.7 0.6 %shard_map.94.partial_grad = f32[256,512]{1,0:T(8,128)S(1)} custom-call(bf16[4,128,2048]{2,1,0:T(8,128)(2,1)S(1)} %copy-done, bf16[256,512]{1,0:T(8,128)(2,1)S(1)} %copy-done.1, bf16[256,512]{1,0:T(8,128)(2,1)S(1)} %collective-permute-done.4.refs_1_, bf16[256,512]{1,0:T(8,128)(2,1)S(1)} %collective-permute-done.3.refs_2_), custom_call_target="tpu_custom_call" | custom-call | flops 402653184 | bytes 4194304 | tf_op jit(solution)/shard_map/pallas_call | solution.py:29
  28.3 0.6 %collective-permute-done.9.block = bf16[256,512]{1,0:T(8,128)(2,1)S(1)} collective-permute-done((bf16[256,512]{1,0:T(8,128)(2,1)S(1)}, bf16[256,512]{1,0:T(8,128)(2,1)S(1)}, u32[]{:S(2)}, u32[]{:S(2)}) %collective-permute-start.9) | collective-permute-done | bytes 262176 | tf_op jit(solution)/shard_map/ppermute | solution.py:214
  29.0 0.4 shard_map.95
  29.4 1.6 %collective-permute-start.14 = (bf16[256,128]{1,0:T(8,128)(2,1)S(1)}, bf16[256,128]{1,0:T(8,128)(2,1)S(1)}, u32[]{:S(2)}, u32[]{:S(2)}) collective-permute-start(bf16[256,128]{1,0:T(8,128)(2,1)S(1)} %get-tuple-element.55), channel_id=1, source_target_pairs={{0,16},{4,20},{8,24},{12,28},{16,0},{20,4},{24,8},{28,12},{1,17},{... | collective-permute-start | bytes 196616 | tf_op jit(solution)/shard_map/ppermute | solution.py:193
  30.9 1.4 %collective-permute-start.15 = (bf16[256,128]{1,0:T(8,128)(2,1)S(1)}, bf16[256,128]{1,0:T(8,128)(2,1)S(1)}, u32[]{:S(2)}, u32[]{:S(2)}) collective-permute-start(bf16[256,128]{1,0:T(8,128)(2,1)S(1)} %get-tuple-element.56), channel_id=1, source_target_pairs={{0,24},{4,28},{8,16},{12,20},{16,8},{20,12},{24,0},{28,4},{1,25},{... | collective-permute-start | bytes 196616 | tf_op jit(solution)/shard_map/ppermute | solution.py:193
  32.4 0.0 collective-permute-done.12.refs_3_
  32.4 0.5 collective-permute-start.13
  32.9 0.0 collective-permute-done.11.refs_2_
  32.9 0.0 collective-permute-done.10.refs_1_
  32.9 0.3 shard_map.96
  33.3 0.6 %collective-permute-start.21 = (bf16[256,512]{1,0:T(8,128)(2,1)S(1)}, bf16[256,512]{1,0:T(8,128)(2,1)S(1)}, u32[]{:S(2)}, u32[]{:S(2)}) collective-permute-start(bf16[256,512]{1,0:T(8,128)(2,1)S(1)} %get-tuple-element.75), channel_id=1, source_target_pairs={{0,1},{1,0},{2,3},{3,2},{4,5},{5,4},{6,7},{7,6},{8,9},{9,8},{10,11... | collective-permute-start | bytes 786440 | tf_op jit(solution)/shard_map/ppermute | solution.py:214
  33.9 0.6 %shard_map.97 = (bf16[256,512]{1,0:T(8,128)(2,1)S(1)}, bf16[256,512]{1,0:T(8,128)(2,1)S(1)}, bf16[256,512]{1,0:T(8,128)(2,1)S(1)}) custom-call(bf16[4,128,2048]{2,1,0:T(8,128)(2,1)S(1)} %copy-done, bf16[256,512]{1,0:T(8,128)(2,1)S(1)} %get-tuple-element.51.joined), custom_call_target="tpu_custom_call" | custom-call | flops 402653184 | bytes 3145728 | tf_op jit(solution)/shard_map/pallas_call | solution.py:29
  34.4 0.0 collective-permute-done.14.refs_2_
  34.5 1.6 %collective-permute-done.15.refs_3_ = bf16[256,128]{1,0:T(8,128)(2,1)S(1)} collective-permute-done((bf16[256,128]{1,0:T(8,128)(2,1)S(1)}, bf16[256,128]{1,0:T(8,128)(2,1)S(1)}, u32[]{:S(2)}, u32[]{:S(2)}) %collective-permute-start.15) | collective-permute-done | bytes 65568 | tf_op jit(solution)/shard_map/ppermute | solution.py:193
  36.1 0.5 collective-permute-start.20
  36.6 0.0 collective-permute-done.13.refs_1_
  36.6 3.4 %shard_map.98 = (bf16[4,256,128]{2,1,0:T(8,128)(2,1)S(1)}, f32[4,2,256,128]{3,2,1,0:T(8,128)S(1)}, bf16[4,2,256,128]{3,2,1,0:T(8,128)(2,1)S(1)}) custom-call(s32[4,4]{1,0:T(4,128)S(1)} %copy-done.2, bf16[256,128]{1,0:T(8,128)(2,1)S(1)} %get-tuple-element.53.refs_0_, bf16[256,128]{1,0:T(8,128)(2,1)S(1)} %collective-permute-done.13.refs_1_, ...), custom_call_target="tpu_custom_call" | custom-call | flops 8589934592 | bytes 7340032 | tf_op jit(solution)/shard_map/pallas_call | solution.py:29
  40.0 0.1 collective-permute-start.16
  40.1 2.5 %collective-permute-done.21.refs_0_ = bf16[256,512]{1,0:T(8,128)(2,1)S(1)} collective-permute-done((bf16[256,512]{1,0:T(8,128)(2,1)S(1)}, bf16[256,512]{1,0:T(8,128)(2,1)S(1)}, u32[]{:S(2)}, u32[]{:S(2)}) %collective-permute-start.21) | collective-permute-done | bytes 262176 | tf_op jit(solution)/shard_map/ppermute | solution.py:214
  42.6 0.1 shard_map.101
  42.6 0.4 collective-permute-start.22
  43.1 0.0 collective-permute-done.16.arrived
  43.1 0.1 shard_map.99
  43.2 1.6 %collective-permute-start.17 = (bf16[3,256,128]{2,1,0:T(8,128)(2,1)S(1)}, bf16[3,256,128]{2,1,0:T(8,128)(2,1)S(1)}, u32[]{:S(2)}, u32[]{:S(2)}) collective-permute-start(bf16[3,256,128]{2,1,0:T(8,128)(2,1)S(1)} %get-tuple-element.66), channel_id=1, source_target_pairs={{0,8},{4,12},{8,0},{12,4},{16,24},{20,28},{24,16},{28,20},{1,9},{5... | collective-permute-start | bytes 589832 | tf_op jit(solution)/shard_map/ppermute | solution.py:193
  44.8 1.5 %collective-permute-start.18 = (bf16[3,256,128]{2,1,0:T(8,128)(2,1)S(1)}, bf16[3,256,128]{2,1,0:T(8,128)(2,1)S(1)}, u32[]{:S(2)}, u32[]{:S(2)}) collective-permute-start(bf16[3,256,128]{2,1,0:T(8,128)(2,1)S(1)} %get-tuple-element.67), channel_id=1, source_target_pairs={{0,16},{4,20},{8,24},{12,28},{16,0},{20,4},{24,8},{28,12},{1,17},{... | collective-permute-start | bytes 589832 | tf_op jit(solution)/shard_map/ppermute | solution.py:193
  46.3 0.5 collective-permute-start.19
  46.8 4.2 %collective-permute-done.17.refs_1_ = bf16[3,256,128]{2,1,0:T(8,128)(2,1)S(1)} collective-permute-done((bf16[3,256,128]{2,1,0:T(8,128)(2,1)S(1)}, bf16[3,256,128]{2,1,0:T(8,128)(2,1)S(1)}, u32[]{:S(2)}, u32[]{:S(2)}) %collective-permute-start.17) | collective-permute-done | bytes 196640 | tf_op jit(solution)/shard_map/ppermute | solution.py:193
  51.0 3.6 %collective-permute-done.18.refs_2_ = bf16[3,256,128]{2,1,0:T(8,128)(2,1)S(1)} collective-permute-done((bf16[3,256,128]{2,1,0:T(8,128)(2,1)S(1)}, bf16[3,256,128]{2,1,0:T(8,128)(2,1)S(1)}, u32[]{:S(2)}, u32[]{:S(2)}) %collective-permute-start.18) | collective-permute-done | bytes 196640 | tf_op jit(solution)/shard_map/ppermute | solution.py:193
  54.6 0.0 collective-permute-done.19.refs_3_
  54.6 0.9 %shard_map.100 = (bf16[4,256,128]{2,1,0:T(8,128)(2,1)}, bf16[4,256,128]{2,1,0:T(8,128)(2,1)}, bf16[4,256,128]{2,1,0:T(8,128)(2,1)}) custom-call(bf16[3,256,128]{2,1,0:T(8,128)(2,1)S(1)} %get-tuple-element.65.refs_0_, bf16[3,256,128]{2,1,0:T(8,128)(2,1)S(1)} %collective-permute-done.17.refs_1_, bf16[3,256,128]{2,1,0:T(8,128)(2,1)S(1)} %collective-permute-done.18.refs_2_, ...), custom_call_target="tpu_custom_call" | custom-call | bytes 1572864 | tf_op jit(solution)/shard_map/pallas_call | solution.py:29
  55.5 0.0 collective-permute-done.20.refs_1_
  55.5 0.0 collective-permute-done.22.refs_2_
  55.5 0.8 %shard_map.102 = bf16[256,512]{1,0:T(8,128)(2,1)} custom-call(bf16[256,512]{1,0:T(8,128)(2,1)S(1)} %get-tuple-element.72.refs_0_, bf16[256,512]{1,0:T(8,128)(2,1)S(1)} %collective-permute-done.20.refs_1_, bf16[256,512]{1,0:T(8,128)(2,1)S(1)} %collective-permute-done.22.refs_2_), custom_call_target="tpu_custom_call" | custom-call | tf_op jit(solution)/shard_map/pallas_call | solution.py:29
  (9 shorter events, 0.2 us)
Async XLA Ops:
  0.6 19.4 %collective-permute-start.3 = (bf16[256,512]{1,0:T(8,128)(2,1)}, bf16[256,512]{1,0:T(8,128)(2,1)S(1)}, u32[]{:S(2)}, u32[]{:S(2)}) collective-permute-start(bf16[256,512]{1,0:T(8,128)(2,1)} %refs_0_), channel_id=1, source_target_pairs={{0,2},{1,3},{2,0},{3,1},{4,6},{5,7},{6,4},{7,5},{8,10},{9,11},{10,... | collective-permute-start | bytes 786440 | tf_op jit(solution)/shard_map/ppermute | solution.py:214
  4.7 15.3 %collective-permute-start.4 = (bf16[256,512]{1,0:T(8,128)(2,1)}, bf16[256,512]{1,0:T(8,128)(2,1)S(1)}, u32[]{:S(2)}, u32[]{:S(2)}) collective-permute-start(bf16[256,512]{1,0:T(8,128)(2,1)} %refs_0_), channel_id=1, source_target_pairs={{0,1},{1,0},{2,3},{3,2},{4,5},{5,4},{6,7},{7,6},{8,9},{9,8},{10,11... | collective-permute-start | bytes 786440 | tf_op jit(solution)/shard_map/ppermute | solution.py:214
  6.3 15.3 %copy-start.2 = (s32[4,4]{1,0:T(4,128)S(1)}, s32[4,4]{1,0:T(4,128)}, u32[]{:S(2)}) copy-start(s32[4,4]{1,0:T(4,128)} %perm.3) | copy-start | bytes 196
  8.4 6.8 %collective-permute-start.1 = (bf16[3,256,128]{2,1,0:T(8,128)(2,1)S(1)}, bf16[3,256,128]{2,1,0:T(8,128)(2,1)S(1)}, u32[]{:S(2)}, u32[]{:S(2)}) collective-permute-start(bf16[3,256,128]{2,1,0:T(8,128)(2,1)S(1)} %pad_maximum_fusion.2), channel_id=1, source_target_pairs={{0,16},{4,20},{8,24},{12,28},{16,0},{20,4},{24,8},{28,12},{1,17},{... | collective-permute-start | bytes 589832 | tf_op jit(solution)/shard_map/ppermute | solution.py:193
  10.0 7.9 %collective-permute-start = (bf16[3,256,128]{2,1,0:T(8,128)(2,1)S(1)}, bf16[3,256,128]{2,1,0:T(8,128)(2,1)S(1)}, u32[]{:S(2)}, u32[]{:S(2)}) collective-permute-start(bf16[3,256,128]{2,1,0:T(8,128)(2,1)S(1)} %pad_maximum_fusion.1), channel_id=1, source_target_pairs={{0,8},{4,12},{8,0},{12,4},{16,24},{20,28},{24,16},{28,20},{1,9},{5... | collective-permute-start | bytes 589832 | tf_op jit(solution)/shard_map/ppermute | solution.py:193
  11.6 16.1 %copy-start = (bf16[4,128,2048]{2,1,0:T(8,128)(2,1)S(1)}, bf16[4,128,2048]{2,1,0:T(8,128)(2,1)}, u32[]{:S(2)}) copy-start(bf16[4,128,2048]{2,1,0:T(8,128)(2,1)} %weight.7) | copy-start | bytes 6291460
  11.6 16.1 %copy-start.1 = (bf16[256,512]{1,0:T(8,128)(2,1)S(1)}, bf16[256,512]{1,0:T(8,128)(2,1)}, u32[]{:S(2)}) copy-start(bf16[256,512]{1,0:T(8,128)(2,1)} %refs_0_) | copy-start | bytes 786436
  11.6 8.4 %collective-permute-start.2 = (bf16[3,256,128]{2,1,0:T(8,128)(2,1)S(1)}, bf16[3,256,128]{2,1,0:T(8,128)(2,1)S(1)}, u32[]{:S(2)}, u32[]{:S(2)}) collective-permute-start(bf16[3,256,128]{2,1,0:T(8,128)(2,1)S(1)} %pad_maximum_fusion.3), channel_id=1, source_target_pairs={{0,24},{4,28},{8,16},{12,20},{16,8},{20,12},{24,0},{28,4},{1,25},{... | collective-permute-start | bytes 589832 | tf_op jit(solution)/shard_map/ppermute | solution.py:193
  15.2 6.0 %collective-permute-start.5 = (bf16[2,256,128]{2,1,0:T(8,128)(2,1)S(1)}, bf16[2,256,128]{2,1,0:T(8,128)(2,1)S(1)}, u32[]{:S(2)}, u32[]{:S(2)}) collective-permute-start(bf16[2,256,128]{2,1,0:T(8,128)(2,1)S(1)} %pad_maximum_fusion.4), channel_id=1, source_target_pairs={{0,4},{4,0},{8,12},{12,8},{16,20},{20,16},{24,28},{28,24},{1,5},{5... | collective-permute-start | bytes 393224 | tf_op jit(solution)/shard_map/ppermute | solution.py:196
  17.9 3.3 %collective-permute-start.7 = (bf16[2,256,128]{2,1,0:T(8,128)(2,1)S(1)}, bf16[2,256,128]{2,1,0:T(8,128)(2,1)S(1)}, u32[]{:S(2)}, u32[]{:S(2)}) collective-permute-start(bf16[2,256,128]{2,1,0:T(8,128)(2,1)S(1)} %slice.31), channel_id=1, source_target_pairs={{0,4},{4,0},{8,12},{12,8},{16,20},{20,16},{24,28},{28,24},{1,5},{5... | collective-permute-start | bytes 393224 | tf_op jit(solution)/shard_map/ppermute | solution.py:196
  20.1 1.3 %collective-permute-start.6 = (bf16[2,256,128]{2,1,0:T(8,128)(2,1)S(1)}, bf16[2,256,128]{2,1,0:T(8,128)(2,1)S(1)}, u32[]{:S(2)}, u32[]{:S(2)}) collective-permute-start(bf16[2,256,128]{2,1,0:T(8,128)(2,1)S(1)} %slice.30), channel_id=1, source_target_pairs={{0,4},{4,0},{8,12},{12,8},{16,20},{20,16},{24,28},{28,24},{1,5},{5... | collective-permute-start | bytes 393224 | tf_op jit(solution)/shard_map/ppermute | solution.py:196
  20.1 1.6 %collective-permute-start.8 = (bf16[2,256,128]{2,1,0:T(8,128)(2,1)S(1)}, bf16[2,256,128]{2,1,0:T(8,128)(2,1)S(1)}, u32[]{:S(2)}, u32[]{:S(2)}) collective-permute-start(bf16[2,256,128]{2,1,0:T(8,128)(2,1)S(1)} %slice.25), channel_id=1, source_target_pairs={{0,4},{4,0},{8,12},{12,8},{16,20},{20,16},{24,28},{28,24},{1,5},{5... | collective-permute-start | bytes 393224 | tf_op jit(solution)/shard_map/ppermute | solution.py:196
  20.7 8.3 %collective-permute-start.9 = (bf16[256,512]{1,0:T(8,128)(2,1)S(1)}, bf16[256,512]{1,0:T(8,128)(2,1)S(1)}, u32[]{:S(2)}, u32[]{:S(2)}) collective-permute-start(bf16[256,512]{1,0:T(8,128)(2,1)S(1)} %collective-permute-done.3.refs_2_), channel_id=1, source_target_pairs={{0,1},{1,0},{2,3},{3,2},{4,5},{5,4},{6,7},{7,6},{8,9},{9,8},{10,11... | collective-permute-start | bytes 786440 | tf_op jit(solution)/shard_map/ppermute | solution.py:214
  24.2 8.2 %collective-permute-start.12 = (bf16[256,128]{1,0:T(8,128)(2,1)S(1)}, bf16[256,128]{1,0:T(8,128)(2,1)S(1)}, u32[]{:S(2)}, u32[]{:S(2)}) collective-permute-start(bf16[256,128]{1,0:T(8,128)(2,1)S(1)} %get-tuple-element.80), channel_id=1, source_target_pairs={{0,24},{4,28},{8,16},{12,20},{16,8},{20,12},{24,0},{28,4},{1,25},{... | collective-permute-start | bytes 196616 | tf_op jit(solution)/shard_map/ppermute | solution.py:193
  26.7 6.2 %collective-permute-start.11 = (bf16[256,128]{1,0:T(8,128)(2,1)S(1)}, bf16[256,128]{1,0:T(8,128)(2,1)S(1)}, u32[]{:S(2)}, u32[]{:S(2)}) collective-permute-start(bf16[256,128]{1,0:T(8,128)(2,1)S(1)} %get-tuple-element.81), channel_id=1, source_target_pairs={{0,16},{4,20},{8,24},{12,28},{16,0},{20,4},{24,8},{28,12},{1,17},{... | collective-permute-start | bytes 196616 | tf_op jit(solution)/shard_map/ppermute | solution.py:193
  27.2 5.7 %collective-permute-start.10 = (bf16[256,128]{1,0:T(8,128)(2,1)S(1)}, bf16[256,128]{1,0:T(8,128)(2,1)S(1)}, u32[]{:S(2)}, u32[]{:S(2)}) collective-permute-start(bf16[256,128]{1,0:T(8,128)(2,1)S(1)} %get-tuple-element.82), channel_id=1, source_target_pairs={{0,8},{4,12},{8,0},{12,4},{16,24},{20,28},{24,16},{28,20},{1,9},{5... | collective-permute-start | bytes 196616 | tf_op jit(solution)/shard_map/ppermute | solution.py:193
  29.4 5.1 %collective-permute-start.14 = (bf16[256,128]{1,0:T(8,128)(2,1)S(1)}, bf16[256,128]{1,0:T(8,128)(2,1)S(1)}, u32[]{:S(2)}, u32[]{:S(2)}) collective-permute-start(bf16[256,128]{1,0:T(8,128)(2,1)S(1)} %get-tuple-element.55), channel_id=1, source_target_pairs={{0,16},{4,20},{8,24},{12,28},{16,0},{20,4},{24,8},{28,12},{1,17},{... | collective-permute-start | bytes 196616 | tf_op jit(solution)/shard_map/ppermute | solution.py:193
  30.9 5.2 %collective-permute-start.15 = (bf16[256,128]{1,0:T(8,128)(2,1)S(1)}, bf16[256,128]{1,0:T(8,128)(2,1)S(1)}, u32[]{:S(2)}, u32[]{:S(2)}) collective-permute-start(bf16[256,128]{1,0:T(8,128)(2,1)S(1)} %get-tuple-element.56), channel_id=1, source_target_pairs={{0,24},{4,28},{8,16},{12,20},{16,8},{20,12},{24,0},{28,4},{1,25},{... | collective-permute-start | bytes 196616 | tf_op jit(solution)/shard_map/ppermute | solution.py:193
  32.4 4.3 %collective-permute-start.13 = (bf16[256,128]{1,0:T(8,128)(2,1)S(1)}, bf16[256,128]{1,0:T(8,128)(2,1)S(1)}, u32[]{:S(2)}, u32[]{:S(2)}) collective-permute-start(bf16[256,128]{1,0:T(8,128)(2,1)S(1)} %get-tuple-element.54), channel_id=1, source_target_pairs={{0,8},{4,12},{8,0},{12,4},{16,24},{20,28},{24,16},{28,20},{1,9},{5... | collective-permute-start | bytes 196616 | tf_op jit(solution)/shard_map/ppermute | solution.py:193
  33.3 9.3 %collective-permute-start.21 = (bf16[256,512]{1,0:T(8,128)(2,1)S(1)}, bf16[256,512]{1,0:T(8,128)(2,1)S(1)}, u32[]{:S(2)}, u32[]{:S(2)}) collective-permute-start(bf16[256,512]{1,0:T(8,128)(2,1)S(1)} %get-tuple-element.75), channel_id=1, source_target_pairs={{0,1},{1,0},{2,3},{3,2},{4,5},{5,4},{6,7},{7,6},{8,9},{9,8},{10,11... | collective-permute-start | bytes 786440 | tf_op jit(solution)/shard_map/ppermute | solution.py:214
  36.1 19.4 %collective-permute-start.20 = (bf16[256,512]{1,0:T(8,128)(2,1)S(1)}, bf16[256,512]{1,0:T(8,128)(2,1)S(1)}, u32[]{:S(2)}, u32[]{:S(2)}) collective-permute-start(bf16[256,512]{1,0:T(8,128)(2,1)S(1)} %get-tuple-element.74), channel_id=1, source_target_pairs={{0,1},{1,0},{2,3},{3,2},{4,5},{5,4},{6,7},{7,6},{8,9},{9,8},{10,11... | collective-permute-start | bytes 786440 | tf_op jit(solution)/shard_map/ppermute | solution.py:214
  40.0 3.1 %collective-permute-start.16 = (bf16[4,2,256,128]{3,2,1,0:T(8,128)(2,1)S(1)}, bf16[4,2,256,128]{3,2,1,0:T(8,128)(2,1)S(1)}, u32[]{:S(2)}, u32[]{:S(2)}) collective-permute-start(bf16[4,2,256,128]{3,2,1,0:T(8,128)(2,1)S(1)} %get-tuple-element.64), channel_id=1, source_target_pairs={{0,4},{4,0},{8,12},{12,8},{16,20},{20,16},{24,28},{28,24},{1,5},{5... | collective-permute-start | bytes 1572872 | tf_op jit(solution)/shard_map/ppermute | solution.py:196
  42.6 12.9 %collective-permute-start.22 = (bf16[256,512]{1,0:T(8,128)(2,1)S(1)}, bf16[256,512]{1,0:T(8,128)(2,1)S(1)}, u32[]{:S(2)}, u32[]{:S(2)}) collective-permute-start(bf16[256,512]{1,0:T(8,128)(2,1)S(1)} %shard_map.101), channel_id=1, source_target_pairs={{0,2},{1,3},{2,0},{3,1},{4,6},{5,7},{6,4},{7,5},{8,10},{9,11},{10,... | collective-permute-start | bytes 786440 | tf_op jit(solution)/shard_map/ppermute | solution.py:214
  43.2 7.7 %collective-permute-start.17 = (bf16[3,256,128]{2,1,0:T(8,128)(2,1)S(1)}, bf16[3,256,128]{2,1,0:T(8,128)(2,1)S(1)}, u32[]{:S(2)}, u32[]{:S(2)}) collective-permute-start(bf16[3,256,128]{2,1,0:T(8,128)(2,1)S(1)} %get-tuple-element.66), channel_id=1, source_target_pairs={{0,8},{4,12},{8,0},{12,4},{16,24},{20,28},{24,16},{28,20},{1,9},{5... | collective-permute-start | bytes 589832 | tf_op jit(solution)/shard_map/ppermute | solution.py:193
  44.8 9.8 %collective-permute-start.18 = (bf16[3,256,128]{2,1,0:T(8,128)(2,1)S(1)}, bf16[3,256,128]{2,1,0:T(8,128)(2,1)S(1)}, u32[]{:S(2)}, u32[]{:S(2)}) collective-permute-start(bf16[3,256,128]{2,1,0:T(8,128)(2,1)S(1)} %get-tuple-element.67), channel_id=1, source_target_pairs={{0,16},{4,20},{8,24},{12,28},{16,0},{20,4},{24,8},{28,12},{1,17},{... | collective-permute-start | bytes 589832 | tf_op jit(solution)/shard_map/ppermute | solution.py:193
  46.3 8.3 %collective-permute-start.19 = (bf16[3,256,128]{2,1,0:T(8,128)(2,1)S(1)}, bf16[3,256,128]{2,1,0:T(8,128)(2,1)S(1)}, u32[]{:S(2)}, u32[]{:S(2)}) collective-permute-start(bf16[3,256,128]{2,1,0:T(8,128)(2,1)S(1)} %get-tuple-element.68), channel_id=1, source_target_pairs={{0,24},{4,28},{8,16},{12,20},{16,8},{20,12},{24,0},{28,4},{1,25},{... | collective-permute-start | bytes 589832 | tf_op jit(solution)/shard_map/ppermute | solution.py:193

commit v7 on v6

--- a/solution.py
+++ b/solution.py
@@ -94,15 +94,15 @@
         for i in range(chips):
             asker = jnp.where(perm[chip, i] == chip ^ d, i, asker)
         asker = asker ^ chip
-        for half, out in ((0, own_part), (1, sibling_part)):
-            near = slice(half * rows, (half + 1) * rows)
-            far = slice((half + 2) * rows, (half + 3) * rows)
-            key_part = dot(score_grad[0, d, :, near], scaled[0, d], TN)
-            key_part += dot(score_grad[1, asker, :, near], scaled[0, asker], TN)
-            value_part = dot(probs[d, :, near], scaled[1, d], TN)
-            value_part += dot(probs[asker, :, far], scaled[1, asker], TN)
-            out[d, 0] = key_part.astype(out.dtype)
-            out[d, 1] = value_part.astype(out.dtype)
+        local = slice(0, 2 * rows)
+        remote = slice(2 * rows, 4 * rows)
+        key_part = dot(scaled[0, d], score_grad[0, d], TN)
+        key_part += dot(scaled[0, asker], score_grad[1, asker], TN)
+        value_part = dot(scaled[1, d], probs[d, :, local], TN)
+        value_part += dot(scaled[1, asker], probs[asker, :, remote], TN)
+        for kind, part in enumerate((key_part, value_part)):
+            own_part[d, kind] = part[:, :rows].T
+            sibling_part[d, kind] = part[:, rows:].astype(LOW).T
 
 
 def join_body(chips, groups, weight, *refs):

time: 56.5 us -> 56 us (level)
  transfers between devices with their start and end apart: 23 -> 23, of which waited for: 10 -> 10; matrix products, arithmetic and copies ran while one was open for 4% -> 4% of each run, Pallas kernels for 16% -> 15%
where the time goes in v7:
time: 56 us; the launch traced here: 55.8 us
  starting transfers between devices  22.7 us (41%)
  waiting for transfers between devices  20.9 us (37%)
  Pallas kernels  9.15 us (16%)
  local copies, waits for them, and re-layouts  2.14 us (4%)
  between operations  0.78 us (1%)
    ppermute x12, waiting for transfers between devices, to_chip(): return lax.ppermute(array, 'seq', [(i, i ^ 2 * d) for i in range(devices)])  16.8 us
    ppermute x12, starting transfers between devices, to_chip(): return lax.ppermute(array, 'seq', [(i, i ^ 2 * d) for i in range(devices)])  14.4 us
    pallas_call x10, Pallas kernels, call(): pl.pallas_call(body, out_shape=outs, in_specs=[scalar if i in smem else v...  9.15 us
    ppermute x6, starting transfers between devices, along(): return lax.ppermute(array, 'head', pairs)  7.73 us
    ppermute x6, waiting for transfers between devices, along(): return lax.ppermute(array, 'head', pairs)  3.64 us
    dynamic_slice x2, local copies, waits for them, and re-layouts, head_piece(): lax.dynamic_index_in_dim(a, h, 0, keepdims=False)  2.08 us
  transfers between devices with their start and end apart: 23, of which 10 were waited for; matrix products, arithmetic and copies ran while one was open for 4% of the time, Pallas kernels for 15%

profile of v7, /device:TPU:0, one launch (start us, length us, event | category | flops | bytes accessed | tf_op | source)
XLA Modules:
  0.0 55.8 jit_solution(14876988508218559115)
XLA Ops:
  0.6 4.1 %collective-permute-start.3 = (bf16[256,512]{1,0:T(8,128)(2,1)}, bf16[256,512]{1,0:T(8,128)(2,1)S(1)}, u32[]{:S(2)}, u32[]{:S(2)}) collective-permute-start(bf16[256,512]{1,0:T(8,128)(2,1)} %refs_0_), channel_id=1, source_target_pairs={{0,2},{1,3},{2,0},{3,1},{4,6},{5,7},{6,4},{7,5},{8,10},{9,11},{10,... | collective-permute-start | bytes 786440 | tf_op jit(solution)/shard_map/ppermute | solution.py:214
  4.7 1.6 %collective-permute-start.4 = (bf16[256,512]{1,0:T(8,128)(2,1)}, bf16[256,512]{1,0:T(8,128)(2,1)S(1)}, u32[]{:S(2)}, u32[]{:S(2)}) collective-permute-start(bf16[256,512]{1,0:T(8,128)(2,1)} %refs_0_), channel_id=1, source_target_pairs={{0,1},{1,0},{2,3},{3,2},{4,5},{5,4},{6,7},{7,6},{8,9},{9,8},{10,11... | collective-permute-start | bytes 786440 | tf_op jit(solution)/shard_map/ppermute | solution.py:214
  6.3 0.0 copy-start.2
  6.3 1.0 %constant_dynamic-slice_fusion.2 = (bf16[1,256,128]{2,1,0:T(8,128)(2,1)S(1)}, bf16[1,256,128]{2,1,0:T(8,128)(2,1)S(1)}, bf16[1,256,128]{2,1,0:T(8,128)(2,1)S(1)}, bf16[1,256,128]{2,1,0:T(8,128)(2,1)S(1)}) fusion(bf16[4,256,128]{2,1,0:T(8,128)(2,1)} %param.7, s32[]{:T(128)S(6)} %select_n.30, s32[]{:T(128)S(6)} %select_n.28, s32[]{:T(128)S(6)} %select_n.27, ...), kind=kLoop, calls=%fused_computation.11 | loop fusion | bytes 524304 | tf_op jit(solution)/shard_map/jit(dynamic_index_in_dim)/dynamic_slice | solution.py:208
  7.3 1.1 %constant_dynamic-slice_fusion = (bf16[1,256,128]{2,1,0:T(8,128)(2,1)S(1)}, bf16[1,256,128]{2,1,0:T(8,128)(2,1)S(1)}, bf16[1,256,128]{2,1,0:T(8,128)(2,1)S(1)}, ...) fusion(bf16[4,256,128]{2,1,0:T(8,128)(2,1)} %param.6, ...), kind=kLoop, calls=%fused_computation.9 | loop fusion | bytes 1048592 | tf_op jit(solution)/shard_map/jit(dynamic_index_in_dim)/dynamic_slice | solution.py:208
  8.4 1.6 %collective-permute-start.1 = (bf16[3,256,128]{2,1,0:T(8,128)(2,1)S(1)}, bf16[3,256,128]{2,1,0:T(8,128)(2,1)S(1)}, u32[]{:S(2)}, u32[]{:S(2)}) collective-permute-start(bf16[3,256,128]{2,1,0:T(8,128)(2,1)S(1)} %pad_maximum_fusion.2), channel_id=1, source_target_pairs={{0,16},{4,20},{8,24},{12,28},{16,0},{20,4},{24,8},{28,12},{1,17},{... | collective-permute-start | bytes 589832 | tf_op jit(solution)/shard_map/ppermute | solution.py:193
  10.0 1.6 %collective-permute-start = (bf16[3,256,128]{2,1,0:T(8,128)(2,1)S(1)}, bf16[3,256,128]{2,1,0:T(8,128)(2,1)S(1)}, u32[]{:S(2)}, u32[]{:S(2)}) collective-permute-start(bf16[3,256,128]{2,1,0:T(8,128)(2,1)S(1)} %pad_maximum_fusion.1), channel_id=1, source_target_pairs={{0,8},{4,12},{8,0},{12,4},{16,24},{20,28},{24,16},{28,20},{1,9},{5... | collective-permute-start | bytes 589832 | tf_op jit(solution)/shard_map/ppermute | solution.py:193
  11.6 0.0 copy-start
  11.6 0.0 copy-start.1
  11.6 0.5 collective-permute-start.2
  12.2 3.1 %collective-permute-done.1.refs_2_ = bf16[3,256,128]{2,1,0:T(8,128)(2,1)S(1)} collective-permute-done((bf16[3,256,128]{2,1,0:T(8,128)(2,1)S(1)}, bf16[3,256,128]{2,1,0:T(8,128)(2,1)S(1)}, u32[]{:S(2)}, u32[]{:S(2)}) %collective-permute-start.1) | collective-permute-done | bytes 196640 | tf_op jit(solution)/shard_map/ppermute | solution.py:193
  15.2 0.0 collective-permute-start.5
  15.3 2.7 %collective-permute-done.refs_1_ = bf16[3,256,128]{2,1,0:T(8,128)(2,1)S(1)} collective-permute-done((bf16[3,256,128]{2,1,0:T(8,128)(2,1)S(1)}, bf16[3,256,128]{2,1,0:T(8,128)(2,1)S(1)}, u32[]{:S(2)}, u32[]{:S(2)}) %collective-permute-start) | collective-permute-done | bytes 196640 | tf_op jit(solution)/shard_map/ppermute | solution.py:193
  17.9 0.0 collective-permute-start.7
  18.0 2.1 %collective-permute-done.2.refs_3_ = bf16[3,256,128]{2,1,0:T(8,128)(2,1)S(1)} collective-permute-done((bf16[3,256,128]{2,1,0:T(8,128)(2,1)S(1)}, bf16[3,256,128]{2,1,0:T(8,128)(2,1)S(1)}, u32[]{:S(2)}, u32[]{:S(2)}) %collective-permute-start.2) | collective-permute-done | bytes 196640 | tf_op jit(solution)/shard_map/ppermute | solution.py:193
  20.1 0.0 collective-permute-start.6
  20.1 0.0 collective-permute-done.3.refs_2_
  20.1 0.0 collective-permute-done.4.refs_1_
  20.1 0.6 %collective-permute-start.8 = (bf16[2,256,128]{2,1,0:T(8,128)(2,1)S(1)}, bf16[2,256,128]{2,1,0:T(8,128)(2,1)S(1)}, u32[]{:S(2)}, u32[]{:S(2)}) collective-permute-start(bf16[2,256,128]{2,1,0:T(8,128)(2,1)S(1)} %slice.25), channel_id=1, source_target_pairs={{0,4},{4,0},{8,12},{12,8},{16,20},{20,16},{24,28},{28,24},{1,5},{5... | collective-permute-start | bytes 393224 | tf_op jit(solution)/shard_map/ppermute | solution.py:196
  20.7 0.5 collective-permute-start.9
  21.2 0.0 collective-permute-done.5.refs_4_
  21.2 0.0 collective-permute-done.7.refs_6_
  21.2 0.2 collective-permute-done.6.refs_5_
  21.4 0.2 collective-permute-done.8.refs_7_
  21.6 0.0 copy-done.2
  21.7 2.5 %shard_map.93 = (bf16[4,256,128]{2,1,0:T(8,128)(2,1)S(1)}, bf16[4,256,1024]{2,1,0:T(8,128)(2,1)S(1)}, bf16[4,2,512,128]{3,2,1,0:T(8,128)(2,1)S(1)}, bf16[4,256,128]{2,1,0:T(8,128)(2,1)S(1)}, f32[4,256,128]{2,1,0:T(8,128)S(1)}) custom-call(s32[4,4]{1,0:T(4,128)S(1)} %copy-done.2, bf16[3,256,128]{2,1,0:T(8,128)(2,1)S(1)} %pad_maximum_fusion.refs_0_, ...), custom_call_target="tpu_custom_call" | custom-call | flops 536870912 | bytes 5767168 | tf_op jit(solution)/shard_map/pallas_call | solution.py:29
  24.2 2.5 %collective-permute-start.12 = (bf16[256,128]{1,0:T(8,128)(2,1)S(1)}, bf16[256,128]{1,0:T(8,128)(2,1)S(1)}, u32[]{:S(2)}, u32[]{:S(2)}) collective-permute-start(bf16[256,128]{1,0:T(8,128)(2,1)S(1)} %get-tuple-element.80), channel_id=1, source_target_pairs={{0,24},{4,28},{8,16},{12,20},{16,8},{20,12},{24,0},{28,4},{1,25},{... | collective-permute-start | bytes 196616 | tf_op jit(solution)/shard_map/ppermute | solution.py:193
  26.7 0.5 collective-permute-start.11
  27.2 0.5 collective-permute-start.10
  27.7 0.0 copy-done
  27.7 0.0 copy-done.1
  27.7 0.6 %shard_map.94.partial_grad = f32[256,512]{1,0:T(8,128)S(1)} custom-call(bf16[4,128,2048]{2,1,0:T(8,128)(2,1)S(1)} %copy-done, bf16[256,512]{1,0:T(8,128)(2,1)S(1)} %copy-done.1, bf16[256,512]{1,0:T(8,128)(2,1)S(1)} %collective-permute-done.4.refs_1_, bf16[256,512]{1,0:T(8,128)(2,1)S(1)} %collective-permute-done.3.refs_2_), custom_call_target="tpu_custom_call" | custom-call | flops 402653184 | bytes 4194304 | tf_op jit(solution)/shard_map/pallas_call | solution.py:29
  28.3 0.6 %collective-permute-done.9.block = bf16[256,512]{1,0:T(8,128)(2,1)S(1)} collective-permute-done((bf16[256,512]{1,0:T(8,128)(2,1)S(1)}, bf16[256,512]{1,0:T(8,128)(2,1)S(1)}, u32[]{:S(2)}, u32[]{:S(2)}) %collective-permute-start.9) | collective-permute-done | bytes 262176 | tf_op jit(solution)/shard_map/ppermute | solution.py:214
  29.0 0.4 shard_map.95
  29.4 1.6 %collective-permute-start.14 = (bf16[256,128]{1,0:T(8,128)(2,1)S(1)}, bf16[256,128]{1,0:T(8,128)(2,1)S(1)}, u32[]{:S(2)}, u32[]{:S(2)}) collective-permute-start(bf16[256,128]{1,0:T(8,128)(2,1)S(1)} %get-tuple-element.55), channel_id=1, source_target_pairs={{0,16},{4,20},{8,24},{12,28},{16,0},{20,4},{24,8},{28,12},{1,17},{... | collective-permute-start | bytes 196616 | tf_op jit(solution)/shard_map/ppermute | solution.py:193
  30.9 1.4 %collective-permute-start.15 = (bf16[256,128]{1,0:T(8,128)(2,1)S(1)}, bf16[256,128]{1,0:T(8,128)(2,1)S(1)}, u32[]{:S(2)}, u32[]{:S(2)}) collective-permute-start(bf16[256,128]{1,0:T(8,128)(2,1)S(1)} %get-tuple-element.56), channel_id=1, source_target_pairs={{0,24},{4,28},{8,16},{12,20},{16,8},{20,12},{24,0},{28,4},{1,25},{... | collective-permute-start | bytes 196616 | tf_op jit(solution)/shard_map/ppermute | solution.py:193
  32.4 0.0 collective-permute-done.12.refs_3_
  32.4 0.5 collective-permute-start.13
  32.9 0.0 collective-permute-done.11.refs_2_
  32.9 0.0 collective-permute-done.10.refs_1_
  32.9 0.3 shard_map.96
  33.3 0.6 %collective-permute-start.21 = (bf16[256,512]{1,0:T(8,128)(2,1)S(1)}, bf16[256,512]{1,0:T(8,128)(2,1)S(1)}, u32[]{:S(2)}, u32[]{:S(2)}) collective-permute-start(bf16[256,512]{1,0:T(8,128)(2,1)S(1)} %get-tuple-element.75), channel_id=1, source_target_pairs={{0,1},{1,0},{2,3},{3,2},{4,5},{5,4},{6,7},{7,6},{8,9},{9,8},{10,11... | collective-permute-start | bytes 786440 | tf_op jit(solution)/shard_map/ppermute | solution.py:214
  33.9 0.6 %shard_map.97 = (bf16[256,512]{1,0:T(8,128)(2,1)S(1)}, bf16[256,512]{1,0:T(8,128)(2,1)S(1)}, bf16[256,512]{1,0:T(8,128)(2,1)S(1)}) custom-call(bf16[4,128,2048]{2,1,0:T(8,128)(2,1)S(1)} %copy-done, bf16[256,512]{1,0:T(8,128)(2,1)S(1)} %get-tuple-element.51.joined), custom_call_target="tpu_custom_call" | custom-call | flops 402653184 | bytes 3145728 | tf_op jit(solution)/shard_map/pallas_call | solution.py:29
  34.4 0.0 collective-permute-done.14.refs_2_
  34.5 1.6 %collective-permute-done.15.refs_3_ = bf16[256,128]{1,0:T(8,128)(2,1)S(1)} collective-permute-done((bf16[256,128]{1,0:T(8,128)(2,1)S(1)}, bf16[256,128]{1,0:T(8,128)(2,1)S(1)}, u32[]{:S(2)}, u32[]{:S(2)}) %collective-permute-start.15) | collective-permute-done | bytes 65568 | tf_op jit(solution)/shard_map/ppermute | solution.py:193
  36.1 0.5 collective-permute-start.20
  36.6 0.0 collective-permute-done.13.refs_1_
  36.6 2.9 %shard_map.98 = (bf16[4,256,128]{2,1,0:T(8,128)(2,1)S(1)}, f32[4,2,256,128]{3,2,1,0:T(8,128)S(1)}, bf16[4,2,256,128]{3,2,1,0:T(8,128)(2,1)S(1)}) custom-call(s32[4,4]{1,0:T(4,128)S(1)} %copy-done.2, bf16[256,128]{1,0:T(8,128)(2,1)S(1)} %get-tuple-element.53.refs_0_, bf16[256,128]{1,0:T(8,128)(2,1)S(1)} %collective-permute-done.13.refs_1_, ...), custom_call_target="tpu_custom_call" | custom-call | flops 8589934592 | bytes 7340032 | tf_op jit(solution)/shard_map/pallas_call | solution.py:29
  39.5 0.1 collective-permute-start.16
  39.6 3.0 %collective-permute-done.21.refs_0_ = bf16[256,512]{1,0:T(8,128)(2,1)S(1)} collective-permute-done((bf16[256,512]{1,0:T(8,128)(2,1)S(1)}, bf16[256,512]{1,0:T(8,128)(2,1)S(1)}, u32[]{:S(2)}, u32[]{:S(2)}) %collective-permute-start.21) | collective-permute-done | bytes 262176 | tf_op jit(solution)/shard_map/ppermute | solution.py:214
  42.6 0.1 shard_map.101
  42.6 0.4 collective-permute-start.22
  43.1 0.0 collective-permute-done.16.arrived
  43.1 0.1 shard_map.99
  43.2 1.6 %collective-permute-start.17 = (bf16[3,256,128]{2,1,0:T(8,128)(2,1)S(1)}, bf16[3,256,128]{2,1,0:T(8,128)(2,1)S(1)}, u32[]{:S(2)}, u32[]{:S(2)}) collective-permute-start(bf16[3,256,128]{2,1,0:T(8,128)(2,1)S(1)} %get-tuple-element.66), channel_id=1, source_target_pairs={{0,8},{4,12},{8,0},{12,4},{16,24},{20,28},{24,16},{28,20},{1,9},{5... | collective-permute-start | bytes 589832 | tf_op jit(solution)/shard_map/ppermute | solution.py:193
  44.8 1.5 %collective-permute-start.18 = (bf16[3,256,128]{2,1,0:T(8,128)(2,1)S(1)}, bf16[3,256,128]{2,1,0:T(8,128)(2,1)S(1)}, u32[]{:S(2)}, u32[]{:S(2)}) collective-permute-start(bf16[3,256,128]{2,1,0:T(8,128)(2,1)S(1)} %get-tuple-element.67), channel_id=1, source_target_pairs={{0,16},{4,20},{8,24},{12,28},{16,0},{20,4},{24,8},{28,12},{1,17},{... | collective-permute-start | bytes 589832 | tf_op jit(solution)/shard_map/ppermute | solution.py:193
  46.3 0.5 collective-permute-start.19
  46.8 4.3 %collective-permute-done.17.refs_1_ = bf16[3,256,128]{2,1,0:T(8,128)(2,1)S(1)} collective-permute-done((bf16[3,256,128]{2,1,0:T(8,128)(2,1)S(1)}, bf16[3,256,128]{2,1,0:T(8,128)(2,1)S(1)}, u32[]{:S(2)}, u32[]{:S(2)}) %collective-permute-start.17) | collective-permute-done | bytes 196640 | tf_op jit(solution)/shard_map/ppermute | solution.py:193
  51.0 3.0 %collective-permute-done.18.refs_2_ = bf16[3,256,128]{2,1,0:T(8,128)(2,1)S(1)} collective-permute-done((bf16[3,256,128]{2,1,0:T(8,128)(2,1)S(1)}, bf16[3,256,128]{2,1,0:T(8,128)(2,1)S(1)}, u32[]{:S(2)}, u32[]{:S(2)}) %collective-permute-start.18) | collective-permute-done | bytes 196640 | tf_op jit(solution)/shard_map/ppermute | solution.py:193
  54.1 0.0 collective-permute-done.19.refs_3_
  54.1 0.9 %shard_map.100 = (bf16[4,256,128]{2,1,0:T(8,128)(2,1)}, bf16[4,256,128]{2,1,0:T(8,128)(2,1)}, bf16[4,256,128]{2,1,0:T(8,128)(2,1)}) custom-call(bf16[3,256,128]{2,1,0:T(8,128)(2,1)S(1)} %get-tuple-element.65.refs_0_, bf16[3,256,128]{2,1,0:T(8,128)(2,1)S(1)} %collective-permute-done.17.refs_1_, bf16[3,256,128]{2,1,0:T(8,128)(2,1)S(1)} %collective-permute-done.18.refs_2_, ...), custom_call_target="tpu_custom_call" | custom-call | bytes 1572864 | tf_op jit(solution)/shard_map/pallas_call | solution.py:29
  55.0 0.0 collective-permute-done.20.refs_1_
  55.0 0.0 collective-permute-done.22.refs_2_
  55.0 0.8 %shard_map.102 = bf16[256,512]{1,0:T(8,128)(2,1)} custom-call(bf16[256,512]{1,0:T(8,128)(2,1)S(1)} %get-tuple-element.72.refs_0_, bf16[256,512]{1,0:T(8,128)(2,1)S(1)} %collective-permute-done.20.refs_1_, bf16[256,512]{1,0:T(8,128)(2,1)S(1)} %collective-permute-done.22.refs_2_), custom_call_target="tpu_custom_call" | custom-call | tf_op jit(solution)/shard_map/pallas_call | solution.py:29
  (9 shorter events, 0.2 us)
Async XLA Ops:
  0.6 19.4 %collective-permute-start.3 = (bf16[256,512]{1,0:T(8,128)(2,1)}, bf16[256,512]{1,0:T(8,128)(2,1)S(1)}, u32[]{:S(2)}, u32[]{:S(2)}) collective-permute-start(bf16[256,512]{1,0:T(8,128)(2,1)} %refs_0_), channel_id=1, source_target_pairs={{0,2},{1,3},{2,0},{3,1},{4,6},{5,7},{6,4},{7,5},{8,10},{9,11},{10,... | collective-permute-start | bytes 786440 | tf_op jit(solution)/shard_map/ppermute | solution.py:214
  4.7 15.3 %collective-permute-start.4 = (bf16[256,512]{1,0:T(8,128)(2,1)}, bf16[256,512]{1,0:T(8,128)(2,1)S(1)}, u32[]{:S(2)}, u32[]{:S(2)}) collective-permute-start(bf16[256,512]{1,0:T(8,128)(2,1)} %refs_0_), channel_id=1, source_target_pairs={{0,1},{1,0},{2,3},{3,2},{4,5},{5,4},{6,7},{7,6},{8,9},{9,8},{10,11... | collective-permute-start | bytes 786440 | tf_op jit(solution)/shard_map/ppermute | solution.py:214
  6.3 15.3 %copy-start.2 = (s32[4,4]{1,0:T(4,128)S(1)}, s32[4,4]{1,0:T(4,128)}, u32[]{:S(2)}) copy-start(s32[4,4]{1,0:T(4,128)} %perm.3) | copy-start | bytes 196
  8.4 6.8 %collective-permute-start.1 = (bf16[3,256,128]{2,1,0:T(8,128)(2,1)S(1)}, bf16[3,256,128]{2,1,0:T(8,128)(2,1)S(1)}, u32[]{:S(2)}, u32[]{:S(2)}) collective-permute-start(bf16[3,256,128]{2,1,0:T(8,128)(2,1)S(1)} %pad_maximum_fusion.2), channel_id=1, source_target_pairs={{0,16},{4,20},{8,24},{12,28},{16,0},{20,4},{24,8},{28,12},{1,17},{... | collective-permute-start | bytes 589832 | tf_op jit(solution)/shard_map/ppermute | solution.py:193
  10.0 7.9 %collective-permute-start = (bf16[3,256,128]{2,1,0:T(8,128)(2,1)S(1)}, bf16[3,256,128]{2,1,0:T(8,128)(2,1)S(1)}, u32[]{:S(2)}, u32[]{:S(2)}) collective-permute-start(bf16[3,256,128]{2,1,0:T(8,128)(2,1)S(1)} %pad_maximum_fusion.1), channel_id=1, source_target_pairs={{0,8},{4,12},{8,0},{12,4},{16,24},{20,28},{24,16},{28,20},{1,9},{5... | collective-permute-start | bytes 589832 | tf_op jit(solution)/shard_map/ppermute | solution.py:193
  11.6 16.1 %copy-start = (bf16[4,128,2048]{2,1,0:T(8,128)(2,1)S(1)}, bf16[4,128,2048]{2,1,0:T(8,128)(2,1)}, u32[]{:S(2)}) copy-start(bf16[4,128,2048]{2,1,0:T(8,128)(2,1)} %weight.7) | copy-start | bytes 6291460
  11.6 16.1 %copy-start.1 = (bf16[256,512]{1,0:T(8,128)(2,1)S(1)}, bf16[256,512]{1,0:T(8,128)(2,1)}, u32[]{:S(2)}) copy-start(bf16[256,512]{1,0:T(8,128)(2,1)} %refs_0_) | copy-start | bytes 786436
  11.6 8.4 %collective-permute-start.2 = (bf16[3,256,128]{2,1,0:T(8,128)(2,1)S(1)}, bf16[3,256,128]{2,1,0:T(8,128)(2,1)S(1)}, u32[]{:S(2)}, u32[]{:S(2)}) collective-permute-start(bf16[3,256,128]{2,1,0:T(8,128)(2,1)S(1)} %pad_maximum_fusion.3), channel_id=1, source_target_pairs={{0,24},{4,28},{8,16},{12,20},{16,8},{20,12},{24,0},{28,4},{1,25},{... | collective-permute-start | bytes 589832 | tf_op jit(solution)/shard_map/ppermute | solution.py:193
  15.2 6.0 %collective-permute-start.5 = (bf16[2,256,128]{2,1,0:T(8,128)(2,1)S(1)}, bf16[2,256,128]{2,1,0:T(8,128)(2,1)S(1)}, u32[]{:S(2)}, u32[]{:S(2)}) collective-permute-start(bf16[2,256,128]{2,1,0:T(8,128)(2,1)S(1)} %pad_maximum_fusion.4), channel_id=1, source_target_pairs={{0,4},{4,0},{8,12},{12,8},{16,20},{20,16},{24,28},{28,24},{1,5},{5... | collective-permute-start | bytes 393224 | tf_op jit(solution)/shard_map/ppermute | solution.py:196
  17.9 3.3 %collective-permute-start.7 = (bf16[2,256,128]{2,1,0:T(8,128)(2,1)S(1)}, bf16[2,256,128]{2,1,0:T(8,128)(2,1)S(1)}, u32[]{:S(2)}, u32[]{:S(2)}) collective-permute-start(bf16[2,256,128]{2,1,0:T(8,128)(2,1)S(1)} %slice.31), channel_id=1, source_target_pairs={{0,4},{4,0},{8,12},{12,8},{16,20},{20,16},{24,28},{28,24},{1,5},{5... | collective-permute-start | bytes 393224 | tf_op jit(solution)/shard_map/ppermute | solution.py:196
  20.1 1.3 %collective-permute-start.6 = (bf16[2,256,128]{2,1,0:T(8,128)(2,1)S(1)}, bf16[2,256,128]{2,1,0:T(8,128)(2,1)S(1)}, u32[]{:S(2)}, u32[]{:S(2)}) collective-permute-start(bf16[2,256,128]{2,1,0:T(8,128)(2,1)S(1)} %slice.30), channel_id=1, source_target_pairs={{0,4},{4,0},{8,12},{12,8},{16,20},{20,16},{24,28},{28,24},{1,5},{5... | collective-permute-start | bytes 393224 | tf_op jit(solution)/shard_map/ppermute | solution.py:196
  20.1 1.6 %collective-permute-start.8 = (bf16[2,256,128]{2,1,0:T(8,128)(2,1)S(1)}, bf16[2,256,128]{2,1,0:T(8,128)(2,1)S(1)}, u32[]{:S(2)}, u32[]{:S(2)}) collective-permute-start(bf16[2,256,128]{2,1,0:T(8,128)(2,1)S(1)} %slice.25), channel_id=1, source_target_pairs={{0,4},{4,0},{8,12},{12,8},{16,20},{20,16},{24,28},{28,24},{1,5},{5... | collective-permute-start | bytes 393224 | tf_op jit(solution)/shard_map/ppermute | solution.py:196
  20.7 8.3 %collective-permute-start.9 = (bf16[256,512]{1,0:T(8,128)(2,1)S(1)}, bf16[256,512]{1,0:T(8,128)(2,1)S(1)}, u32[]{:S(2)}, u32[]{:S(2)}) collective-permute-start(bf16[256,512]{1,0:T(8,128)(2,1)S(1)} %collective-permute-done.3.refs_2_), channel_id=1, source_target_pairs={{0,1},{1,0},{2,3},{3,2},{4,5},{5,4},{6,7},{7,6},{8,9},{9,8},{10,11... | collective-permute-start | bytes 786440 | tf_op jit(solution)/shard_map/ppermute | solution.py:214
  24.2 8.2 %collective-permute-start.12 = (bf16[256,128]{1,0:T(8,128)(2,1)S(1)}, bf16[256,128]{1,0:T(8,128)(2,1)S(1)}, u32[]{:S(2)}, u32[]{:S(2)}) collective-permute-start(bf16[256,128]{1,0:T(8,128)(2,1)S(1)} %get-tuple-element.80), channel_id=1, source_target_pairs={{0,24},{4,28},{8,16},{12,20},{16,8},{20,12},{24,0},{28,4},{1,25},{... | collective-permute-start | bytes 196616 | tf_op jit(solution)/shard_map/ppermute | solution.py:193
  26.7 6.2 %collective-permute-start.11 = (bf16[256,128]{1,0:T(8,128)(2,1)S(1)}, bf16[256,128]{1,0:T(8,128)(2,1)S(1)}, u32[]{:S(2)}, u32[]{:S(2)}) collective-permute-start(bf16[256,128]{1,0:T(8,128)(2,1)S(1)} %get-tuple-element.81), channel_id=1, source_target_pairs={{0,16},{4,20},{8,24},{12,28},{16,0},{20,4},{24,8},{28,12},{1,17},{... | collective-permute-start | bytes 196616 | tf_op jit(solution)/shard_map/ppermute | solution.py:193
  27.2 5.7 %collective-permute-start.10 = (bf16[256,128]{1,0:T(8,128)(2,1)S(1)}, bf16[256,128]{1,0:T(8,128)(2,1)S(1)}, u32[]{:S(2)}, u32[]{:S(2)}) collective-permute-start(bf16[256,128]{1,0:T(8,128)(2,1)S(1)} %get-tuple-element.82), channel_id=1, source_target_pairs={{0,8},{4,12},{8,0},{12,4},{16,24},{20,28},{24,16},{28,20},{1,9},{5... | collective-permute-start | bytes 196616 | tf_op jit(solution)/shard_map/ppermute | solution.py:193
  29.4 5.1 %collective-permute-start.14 = (bf16[256,128]{1,0:T(8,128)(2,1)S(1)}, bf16[256,128]{1,0:T(8,128)(2,1)S(1)}, u32[]{:S(2)}, u32[]{:S(2)}) collective-permute-start(bf16[256,128]{1,0:T(8,128)(2,1)S(1)} %get-tuple-element.55), channel_id=1, source_target_pairs={{0,16},{4,20},{8,24},{12,28},{16,0},{20,4},{24,8},{28,12},{1,17},{... | collective-permute-start | bytes 196616 | tf_op jit(solution)/shard_map/ppermute | solution.py:193
  30.9 5.2 %collective-permute-start.15 = (bf16[256,128]{1,0:T(8,128)(2,1)S(1)}, bf16[256,128]{1,0:T(8,128)(2,1)S(1)}, u32[]{:S(2)}, u32[]{:S(2)}) collective-permute-start(bf16[256,128]{1,0:T(8,128)(2,1)S(1)} %get-tuple-element.56), channel_id=1, source_target_pairs={{0,24},{4,28},{8,16},{12,20},{16,8},{20,12},{24,0},{28,4},{1,25},{... | collective-permute-start | bytes 196616 | tf_op jit(solution)/shard_map/ppermute | solution.py:193
  32.4 4.3 %collective-permute-start.13 = (bf16[256,128]{1,0:T(8,128)(2,1)S(1)}, bf16[256,128]{1,0:T(8,128)(2,1)S(1)}, u32[]{:S(2)}, u32[]{:S(2)}) collective-permute-start(bf16[256,128]{1,0:T(8,128)(2,1)S(1)} %get-tuple-element.54), channel_id=1, source_target_pairs={{0,8},{4,12},{8,0},{12,4},{16,24},{20,28},{24,16},{28,20},{1,9},{5... | collective-permute-start | bytes 196616 | tf_op jit(solution)/shard_map/ppermute | solution.py:193
  33.3 9.3 %collective-permute-start.21 = (bf16[256,512]{1,0:T(8,128)(2,1)S(1)}, bf16[256,512]{1,0:T(8,128)(2,1)S(1)}, u32[]{:S(2)}, u32[]{:S(2)}) collective-permute-start(bf16[256,512]{1,0:T(8,128)(2,1)S(1)} %get-tuple-element.75), channel_id=1, source_target_pairs={{0,1},{1,0},{2,3},{3,2},{4,5},{5,4},{6,7},{7,6},{8,9},{9,8},{10,11... | collective-permute-start | bytes 786440 | tf_op jit(solution)/shard_map/ppermute | solution.py:214
  36.1 18.9 %collective-permute-start.20 = (bf16[256,512]{1,0:T(8,128)(2,1)S(1)}, bf16[256,512]{1,0:T(8,128)(2,1)S(1)}, u32[]{:S(2)}, u32[]{:S(2)}) collective-permute-start(bf16[256,512]{1,0:T(8,128)(2,1)S(1)} %get-tuple-element.74), channel_id=1, source_target_pairs={{0,1},{1,0},{2,3},{3,2},{4,5},{5,4},{6,7},{7,6},{8,9},{9,8},{10,11... | collective-permute-start | bytes 786440 | tf_op jit(solution)/shard_map/ppermute | solution.py:214
  39.5 3.6 %collective-permute-start.16 = (bf16[4,2,256,128]{3,2,1,0:T(8,128)(2,1)S(1)}, bf16[4,2,256,128]{3,2,1,0:T(8,128)(2,1)S(1)}, u32[]{:S(2)}, u32[]{:S(2)}) collective-permute-start(bf16[4,2,256,128]{3,2,1,0:T(8,128)(2,1)S(1)} %get-tuple-element.64), channel_id=1, source_target_pairs={{0,4},{4,0},{8,12},{12,8},{16,20},{20,16},{24,28},{28,24},{1,5},{5... | collective-permute-start | bytes 1572872 | tf_op jit(solution)/shard_map/ppermute | solution.py:196
  42.6 12.4 %collective-permute-start.22 = (bf16[256,512]{1,0:T(8,128)(2,1)S(1)}, bf16[256,512]{1,0:T(8,128)(2,1)S(1)}, u32[]{:S(2)}, u32[]{:S(2)}) collective-permute-start(bf16[256,512]{1,0:T(8,128)(2,1)S(1)} %shard_map.101), channel_id=1, source_target_pairs={{0,2},{1,3},{2,0},{3,1},{4,6},{5,7},{6,4},{7,5},{8,10},{9,11},{10,... | collective-permute-start | bytes 786440 | tf_op jit(solution)/shard_map/ppermute | solution.py:214
  43.2 7.8 %collective-permute-start.17 = (bf16[3,256,128]{2,1,0:T(8,128)(2,1)S(1)}, bf16[3,256,128]{2,1,0:T(8,128)(2,1)S(1)}, u32[]{:S(2)}, u32[]{:S(2)}) collective-permute-start(bf16[3,256,128]{2,1,0:T(8,128)(2,1)S(1)} %get-tuple-element.66), channel_id=1, source_target_pairs={{0,8},{4,12},{8,0},{12,4},{16,24},{20,28},{24,16},{28,20},{1,9},{5... | collective-permute-start | bytes 589832 | tf_op jit(solution)/shard_map/ppermute | solution.py:193
  44.8 9.3 %collective-permute-start.18 = (bf16[3,256,128]{2,1,0:T(8,128)(2,1)S(1)}, bf16[3,256,128]{2,1,0:T(8,128)(2,1)S(1)}, u32[]{:S(2)}, u32[]{:S(2)}) collective-permute-start(bf16[3,256,128]{2,1,0:T(8,128)(2,1)S(1)} %get-tuple-element.67), channel_id=1, source_target_pairs={{0,16},{4,20},{8,24},{12,28},{16,0},{20,4},{24,8},{28,12},{1,17},{... | collective-permute-start | bytes 589832 | tf_op jit(solution)/shard_map/ppermute | solution.py:193
  46.3 7.8 %collective-permute-start.19 = (bf16[3,256,128]{2,1,0:T(8,128)(2,1)S(1)}, bf16[3,256,128]{2,1,0:T(8,128)(2,1)S(1)}, u32[]{:S(2)}, u32[]{:S(2)}) collective-permute-start(bf16[3,256,128]{2,1,0:T(8,128)(2,1)S(1)} %get-tuple-element.68), channel_id=1, source_target_pairs={{0,24},{4,28},{8,16},{12,20},{16,8},{20,12},{24,0},{28,4},{1,25},{... | collective-permute-start | bytes 589832 | tf_op jit(solution)/shard_map/ppermute | solution.py:193

commit v8 on v7

--- a/solution.py
+++ b/solution.py
@@ -284,7 +284,6 @@
         flops=2 * rows * heads * width * (features - columns),
         moved=weight_bytes + 2 * rows * features,
     )
-    neighbour = across(together(parts[1], *incoming[2:])[0], 1)
     halfway = call(sum_body, shape((rows, columns), LOW), halfway, parts[2], flops=2**33, moved=2**28)
     incoming[0] = together(incoming[0], parts[0])[0]
     query_grad, own_part, sibling_part = call(
@@ -309,6 +308,7 @@
         ],
         smem=(0,),
     )
+    neighbour = across(together(parts[1], sibling_part)[0], 1)
     returned = exchange(
         call(
             functools.partial(merge_body, chips),

time: 56 us -> 57.2 us (1.021)
  waiting for transfers between devices: 20.9 us -> 22 us
    ppermute x12, waiting for transfers between devices: 16.8 us -> 18.9 us  [to_chip(): return lax.ppermute(array, 'seq', [(i, i ^ 2 * d) for i in range(devices)])]
    ppermute x6, waiting for transfers between devices: 3.64 us -> 1.87 us  [along(): return lax.ppermute(array, 'head', pairs)]
    ppermute x5, waiting for transfers between devices: 0.44 us -> 1.25 us  [to_sibling(): return lax.ppermute(array, 'seq', [(i, i ^ 1) for i in range(devices)])]
  transfers between devices with their start and end apart: 23 -> 23, of which waited for: 10 -> 12; matrix products, arithmetic and copies ran while one was open for 4% -> 4% of each run, Pallas kernels for 15% -> 15%
where the time goes in v8:
time: 57.2 us; the launch traced here: 57 us
  starting transfers between devices  22.8 us (40%)
  waiting for transfers between devices  22 us (38%)
  Pallas kernels  9.15 us (16%)
  local copies, waits for them, and re-layouts  2.14 us (4%)
  between operations  0.78 us (1%)
    ppermute x12, waiting for transfers between devices, to_chip(): return lax.ppermute(array, 'seq', [(i, i ^ 2 * d) for i in range(devices)])  18.9 us
    ppermute x12, starting transfers between devices, to_chip(): return lax.ppermute(array, 'seq', [(i, i ^ 2 * d) for i in range(devices)])  14.4 us
    pallas_call x10, Pallas kernels, call(): pl.pallas_call(body, out_shape=outs, in_specs=[scalar if i in smem else v...  9.15 us
    ppermute x6, starting transfers between devices, along(): return lax.ppermute(array, 'head', pairs)  7.8 us
    dynamic_slice x2, local copies, waits for them, and re-layouts, head_piece(): lax.dynamic_index_in_dim(a, h, 0, keepdims=False)  2.08 us
    ppermute x6, waiting for transfers between devices, along(): return lax.ppermute(array, 'head', pairs)  1.87 us
    ppermute x5, waiting for transfers between devices, to_sibling(): return lax.ppermute(array, 'seq', [(i, i ^ 1) for i in range(devices)])  1.25 us
  transfers between devices with their start and end apart: 23, of which 12 were waited for; matrix products, arithmetic and copies ran while one was open for 4% of the time, Pallas kernels for 15%

profile of v8, /device:TPU:0, one launch (start us, length us, event | category | flops | bytes accessed | tf_op | source)
XLA Modules:
  0.0 57.0 jit_solution(15792291265802539853)
XLA Ops:
  0.6 4.1 %collective-permute-start.3 = (bf16[256,512]{1,0:T(8,128)(2,1)}, bf16[256,512]{1,0:T(8,128)(2,1)S(1)}, u32[]{:S(2)}, u32[]{:S(2)}) collective-permute-start(bf16[256,512]{1,0:T(8,128)(2,1)} %refs_0_), channel_id=1, source_target_pairs={{0,2},{1,3},{2,0},{3,1},{4,6},{5,7},{6,4},{7,5},{8,10},{9,11},{10,... | collective-permute-start | bytes 786440 | tf_op jit(solution)/shard_map/ppermute | solution.py:214
  4.7 1.6 %collective-permute-start.4 = (bf16[256,512]{1,0:T(8,128)(2,1)}, bf16[256,512]{1,0:T(8,128)(2,1)S(1)}, u32[]{:S(2)}, u32[]{:S(2)}) collective-permute-start(bf16[256,512]{1,0:T(8,128)(2,1)} %refs_0_), channel_id=1, source_target_pairs={{0,1},{1,0},{2,3},{3,2},{4,5},{5,4},{6,7},{7,6},{8,9},{9,8},{10,11... | collective-permute-start | bytes 786440 | tf_op jit(solution)/shard_map/ppermute | solution.py:214
  6.3 0.0 copy-start.2
  6.3 1.0 %constant_dynamic-slice_fusion.2 = (bf16[1,256,128]{2,1,0:T(8,128)(2,1)S(1)}, bf16[1,256,128]{2,1,0:T(8,128)(2,1)S(1)}, bf16[1,256,128]{2,1,0:T(8,128)(2,1)S(1)}, bf16[1,256,128]{2,1,0:T(8,128)(2,1)S(1)}) fusion(bf16[4,256,128]{2,1,0:T(8,128)(2,1)} %param.7, s32[]{:T(128)S(6)} %select_n.30, s32[]{:T(128)S(6)} %select_n.28, s32[]{:T(128)S(6)} %select_n.27, ...), kind=kLoop, calls=%fused_computation.11 | loop fusion | bytes 524304 | tf_op jit(solution)/shard_map/jit(dynamic_index_in_dim)/dynamic_slice | solution.py:208
  7.3 1.1 %constant_dynamic-slice_fusion = (bf16[1,256,128]{2,1,0:T(8,128)(2,1)S(1)}, bf16[1,256,128]{2,1,0:T(8,128)(2,1)S(1)}, bf16[1,256,128]{2,1,0:T(8,128)(2,1)S(1)}, ...) fusion(bf16[4,256,128]{2,1,0:T(8,128)(2,1)} %param.6, ...), kind=kLoop, calls=%fused_computation.9 | loop fusion | bytes 1048592 | tf_op jit(solution)/shard_map/jit(dynamic_index_in_dim)/dynamic_slice | solution.py:208
  8.4 1.6 %collective-permute-start.1 = (bf16[3,256,128]{2,1,0:T(8,128)(2,1)S(1)}, bf16[3,256,128]{2,1,0:T(8,128)(2,1)S(1)}, u32[]{:S(2)}, u32[]{:S(2)}) collective-permute-start(bf16[3,256,128]{2,1,0:T(8,128)(2,1)S(1)} %pad_maximum_fusion.2), channel_id=1, source_target_pairs={{0,16},{4,20},{8,24},{12,28},{16,0},{20,4},{24,8},{28,12},{1,17},{... | collective-permute-start | bytes 589832 | tf_op jit(solution)/shard_map/ppermute | solution.py:193
  10.0 1.6 %collective-permute-start = (bf16[3,256,128]{2,1,0:T(8,128)(2,1)S(1)}, bf16[3,256,128]{2,1,0:T(8,128)(2,1)S(1)}, u32[]{:S(2)}, u32[]{:S(2)}) collective-permute-start(bf16[3,256,128]{2,1,0:T(8,128)(2,1)S(1)} %pad_maximum_fusion.1), channel_id=1, source_target_pairs={{0,8},{4,12},{8,0},{12,4},{16,24},{20,28},{24,16},{28,20},{1,9},{5... | collective-permute-start | bytes 589832 | tf_op jit(solution)/shard_map/ppermute | solution.py:193
  11.6 0.0 copy-start
  11.6 0.0 copy-start.1
  11.6 0.5 collective-permute-start.2
  12.2 3.1 %collective-permute-done.1.refs_2_ = bf16[3,256,128]{2,1,0:T(8,128)(2,1)S(1)} collective-permute-done((bf16[3,256,128]{2,1,0:T(8,128)(2,1)S(1)}, bf16[3,256,128]{2,1,0:T(8,128)(2,1)S(1)}, u32[]{:S(2)}, u32[]{:S(2)}) %collective-permute-start.1) | collective-permute-done | bytes 196640 | tf_op jit(solution)/shard_map/ppermute | solution.py:193
  15.2 0.0 collective-permute-start.5
  15.3 2.7 %collective-permute-done.refs_1_ = bf16[3,256,128]{2,1,0:T(8,128)(2,1)S(1)} collective-permute-done((bf16[3,256,128]{2,1,0:T(8,128)(2,1)S(1)}, bf16[3,256,128]{2,1,0:T(8,128)(2,1)S(1)}, u32[]{:S(2)}, u32[]{:S(2)}) %collective-permute-start) | collective-permute-done | bytes 196640 | tf_op jit(solution)/shard_map/ppermute | solution.py:193
  17.9 0.0 collective-permute-start.7
  18.0 2.1 %collective-permute-done.2.refs_3_ = bf16[3,256,128]{2,1,0:T(8,128)(2,1)S(1)} collective-permute-done((bf16[3,256,128]{2,1,0:T(8,128)(2,1)S(1)}, bf16[3,256,128]{2,1,0:T(8,128)(2,1)S(1)}, u32[]{:S(2)}, u32[]{:S(2)}) %collective-permute-start.2) | collective-permute-done | bytes 196640 | tf_op jit(solution)/shard_map/ppermute | solution.py:193
  20.1 0.0 collective-permute-start.6
  20.1 0.0 collective-permute-done.3.refs_2_
  20.1 0.0 collective-permute-done.4.refs_1_
  20.1 0.6 collective-permute-start.8
  20.7 0.5 collective-permute-start.9
  21.2 0.0 collective-permute-done.5.refs_4_
  21.2 0.0 collective-permute-done.7.refs_6_
  21.2 0.2 collective-permute-done.6.refs_5_
  21.4 0.2 collective-permute-done.8.refs_7_
  21.6 0.0 copy-done.2
  21.7 2.5 %shard_map.93 = (bf16[4,256,128]{2,1,0:T(8,128)(2,1)S(1)}, bf16[4,256,1024]{2,1,0:T(8,128)(2,1)S(1)}, bf16[4,2,512,128]{3,2,1,0:T(8,128)(2,1)S(1)}, bf16[4,256,128]{2,1,0:T(8,128)(2,1)S(1)}, f32[4,256,128]{2,1,0:T(8,128)S(1)}) custom-call(s32[4,4]{1,0:T(4,128)S(1)} %copy-done.2, bf16[3,256,128]{2,1,0:T(8,128)(2,1)S(1)} %pad_maximum_fusion.refs_0_, ...), custom_call_target="tpu_custom_call" | custom-call | flops 536870912 | bytes 5767168 | tf_op jit(solution)/shard_map/pallas_call | solution.py:29
  24.2 2.5 %collective-permute-start.12 = (bf16[256,128]{1,0:T(8,128)(2,1)S(1)}, bf16[256,128]{1,0:T(8,128)(2,1)S(1)}, u32[]{:S(2)}, u32[]{:S(2)}) collective-permute-start(bf16[256,128]{1,0:T(8,128)(2,1)S(1)} %get-tuple-element.80), channel_id=1, source_target_pairs={{0,24},{4,28},{8,16},{12,20},{16,8},{20,12},{24,0},{28,4},{1,25},{... | collective-permute-start | bytes 196616 | tf_op jit(solution)/shard_map/ppermute | solution.py:193
  26.7 0.5 collective-permute-start.11
  27.2 0.5 collective-permute-start.10
  27.7 0.0 copy-done
  27.7 0.0 copy-done.1
  27.7 0.6 %shard_map.94.partial_grad = f32[256,512]{1,0:T(8,128)S(1)} custom-call(bf16[4,128,2048]{2,1,0:T(8,128)(2,1)S(1)} %copy-done, bf16[256,512]{1,0:T(8,128)(2,1)S(1)} %copy-done.1, bf16[256,512]{1,0:T(8,128)(2,1)S(1)} %collective-permute-done.4.refs_1_, bf16[256,512]{1,0:T(8,128)(2,1)S(1)} %collective-permute-done.3.refs_2_), custom_call_target="tpu_custom_call" | custom-call | flops 402653184 | bytes 4194304 | tf_op jit(solution)/shard_map/pallas_call | solution.py:29
  28.3 0.6 %collective-permute-done.9.block = bf16[256,512]{1,0:T(8,128)(2,1)S(1)} collective-permute-done((bf16[256,512]{1,0:T(8,128)(2,1)S(1)}, bf16[256,512]{1,0:T(8,128)(2,1)S(1)}, u32[]{:S(2)}, u32[]{:S(2)}) %collective-permute-start.9) | collective-permute-done | bytes 262176 | tf_op jit(solution)/shard_map/ppermute | solution.py:214
  29.0 0.4 shard_map.95
  29.4 1.6 %collective-permute-start.13 = (bf16[256,128]{1,0:T(8,128)(2,1)S(1)}, bf16[256,128]{1,0:T(8,128)(2,1)S(1)}, u32[]{:S(2)}, u32[]{:S(2)}) collective-permute-start(bf16[256,128]{1,0:T(8,128)(2,1)S(1)} %get-tuple-element.54), channel_id=1, source_target_pairs={{0,8},{4,12},{8,0},{12,4},{16,24},{20,28},{24,16},{28,20},{1,9},{5... | collective-permute-start | bytes 196616 | tf_op jit(solution)/shard_map/ppermute | solution.py:193
  30.9 1.5 %collective-permute-start.14 = (bf16[256,128]{1,0:T(8,128)(2,1)S(1)}, bf16[256,128]{1,0:T(8,128)(2,1)S(1)}, u32[]{:S(2)}, u32[]{:S(2)}) collective-permute-start(bf16[256,128]{1,0:T(8,128)(2,1)S(1)} %get-tuple-element.55), channel_id=1, source_target_pairs={{0,16},{4,20},{8,24},{12,28},{16,0},{20,4},{24,8},{28,12},{1,17},{... | collective-permute-start | bytes 196616 | tf_op jit(solution)/shard_map/ppermute | solution.py:193
  32.4 0.0 collective-permute-done.12.refs_3_
  32.4 0.5 collective-permute-start.15
  32.9 0.0 collective-permute-done.11.refs_2_
  32.9 0.0 collective-permute-done.10.refs_1_
  32.9 0.3 shard_map.96
  33.3 0.6 %collective-permute-start.21 = (bf16[256,512]{1,0:T(8,128)(2,1)S(1)}, bf16[256,512]{1,0:T(8,128)(2,1)S(1)}, u32[]{:S(2)}, u32[]{:S(2)}) collective-permute-start(bf16[256,512]{1,0:T(8,128)(2,1)S(1)} %get-tuple-element.75), channel_id=1, source_target_pairs={{0,1},{1,0},{2,3},{3,2},{4,5},{5,4},{6,7},{7,6},{8,9},{9,8},{10,11... | collective-permute-start | bytes 786440 | tf_op jit(solution)/shard_map/ppermute | solution.py:214
  33.9 0.6 %shard_map.97 = (bf16[256,512]{1,0:T(8,128)(2,1)S(1)}, bf16[256,512]{1,0:T(8,128)(2,1)S(1)}, bf16[256,512]{1,0:T(8,128)(2,1)S(1)}) custom-call(bf16[4,128,2048]{2,1,0:T(8,128)(2,1)S(1)} %copy-done, bf16[256,512]{1,0:T(8,128)(2,1)S(1)} %get-tuple-element.51.joined), custom_call_target="tpu_custom_call" | custom-call | flops 402653184 | bytes 3145728 | tf_op jit(solution)/shard_map/pallas_call | solution.py:29
  34.4 0.0 collective-permute-done.13.refs_1_
  34.5 1.4 %collective-permute-done.14.refs_2_ = bf16[256,128]{1,0:T(8,128)(2,1)S(1)} collective-permute-done((bf16[256,128]{1,0:T(8,128)(2,1)S(1)}, bf16[256,128]{1,0:T(8,128)(2,1)S(1)}, u32[]{:S(2)}, u32[]{:S(2)}) %collective-permute-start.14) | collective-permute-done | bytes 65568 | tf_op jit(solution)/shard_map/ppermute | solution.py:193
  35.9 1.7 %collective-permute-done.15.refs_3_ = bf16[256,128]{1,0:T(8,128)(2,1)S(1)} collective-permute-done((bf16[256,128]{1,0:T(8,128)(2,1)S(1)}, bf16[256,128]{1,0:T(8,128)(2,1)S(1)}, u32[]{:S(2)}, u32[]{:S(2)}) %collective-permute-start.15) | collective-permute-done | bytes 65568 | tf_op jit(solution)/shard_map/ppermute | solution.py:193
  37.6 2.9 %shard_map.98 = (bf16[4,256,128]{2,1,0:T(8,128)(2,1)S(1)}, f32[4,2,256,128]{3,2,1,0:T(8,128)S(1)}, bf16[4,2,256,128]{3,2,1,0:T(8,128)(2,1)S(1)}) custom-call(s32[4,4]{1,0:T(4,128)S(1)} %copy-done.2, bf16[256,128]{1,0:T(8,128)(2,1)S(1)} %get-tuple-element.53.refs_0_, bf16[256,128]{1,0:T(8,128)(2,1)S(1)} %collective-permute-done.13.refs_1_, ...), custom_call_target="tpu_custom_call" | custom-call | flops 8589934592 | bytes 7340032 | tf_op jit(solution)/shard_map/pallas_call | solution.py:29
  40.5 0.1 collective-permute-start.16
  40.5 0.6 %collective-permute-start.20 = (bf16[256,512]{1,0:T(8,128)(2,1)S(1)}, bf16[256,512]{1,0:T(8,128)(2,1)S(1)}, u32[]{:S(2)}, u32[]{:S(2)}) collective-permute-start(bf16[256,512]{1,0:T(8,128)(2,1)S(1)} %get-tuple-element.74), channel_id=1, source_target_pairs={{0,1},{1,0},{2,3},{3,2},{4,5},{5,4},{6,7},{7,6},{8,9},{9,8},{10,11... | collective-permute-start | bytes 786440 | tf_op jit(solution)/shard_map/ppermute | solution.py:214
  41.1 0.0 collective-permute-done.21.refs_0_
  41.1 0.1 shard_map.101
  41.2 0.4 collective-permute-start.22
  41.6 0.8 %collective-permute-done.16.arrived = bf16[4,2,256,128]{3,2,1,0:T(8,128)(2,1)S(1)} collective-permute-done((bf16[4,2,256,128]{3,2,1,0:T(8,128)(2,1)S(1)}, bf16[4,2,256,128]{3,2,1,0:T(8,128)(2,1)S(1)}, u32[]{:S(2)}, u32[]{:S(2)}) %collective-permute-start.16) | collective-permute-done | bytes 524320 | tf_op jit(solution)/shard_map/ppermute | solution.py:196
  42.4 0.1 shard_map.99
  42.6 0.6 %collective-permute-start.17 = (bf16[3,256,128]{2,1,0:T(8,128)(2,1)S(1)}, bf16[3,256,128]{2,1,0:T(8,128)(2,1)S(1)}, u32[]{:S(2)}, u32[]{:S(2)}) collective-permute-start(bf16[3,256,128]{2,1,0:T(8,128)(2,1)S(1)} %get-tuple-element.66), channel_id=1, source_target_pairs={{0,8},{4,12},{8,0},{12,4},{16,24},{20,28},{24,16},{28,20},{1,9},{5... | collective-permute-start | bytes 589832 | tf_op jit(solution)/shard_map/ppermute | solution.py:193
  43.2 0.5 collective-permute-start.18
  43.7 2.4 %collective-permute-start.19 = (bf16[3,256,128]{2,1,0:T(8,128)(2,1)S(1)}, bf16[3,256,128]{2,1,0:T(8,128)(2,1)S(1)}, u32[]{:S(2)}, u32[]{:S(2)}) collective-permute-start(bf16[3,256,128]{2,1,0:T(8,128)(2,1)S(1)} %get-tuple-element.68), channel_id=1, source_target_pairs={{0,24},{4,28},{8,16},{12,20},{16,8},{20,12},{24,0},{28,4},{1,25},{... | collective-permute-start | bytes 589832 | tf_op jit(solution)/shard_map/ppermute | solution.py:193
  46.1 4.3 %collective-permute-done.17.refs_1_ = bf16[3,256,128]{2,1,0:T(8,128)(2,1)S(1)} collective-permute-done((bf16[3,256,128]{2,1,0:T(8,128)(2,1)S(1)}, bf16[3,256,128]{2,1,0:T(8,128)(2,1)S(1)}, u32[]{:S(2)}, u32[]{:S(2)}) %collective-permute-start.17) | collective-permute-done | bytes 196640 | tf_op jit(solution)/shard_map/ppermute | solution.py:193
  50.4 3.7 %collective-permute-done.18.refs_2_ = bf16[3,256,128]{2,1,0:T(8,128)(2,1)S(1)} collective-permute-done((bf16[3,256,128]{2,1,0:T(8,128)(2,1)S(1)}, bf16[3,256,128]{2,1,0:T(8,128)(2,1)S(1)}, u32[]{:S(2)}, u32[]{:S(2)}) %collective-permute-start.18) | collective-permute-done | bytes 196640 | tf_op jit(solution)/shard_map/ppermute | solution.py:193
  54.1 0.0 collective-permute-done.19.refs_3_
  54.1 0.9 %shard_map.100 = (bf16[4,256,128]{2,1,0:T(8,128)(2,1)}, bf16[4,256,128]{2,1,0:T(8,128)(2,1)}, bf16[4,256,128]{2,1,0:T(8,128)(2,1)}) custom-call(bf16[3,256,128]{2,1,0:T(8,128)(2,1)S(1)} %get-tuple-element.65.refs_0_, bf16[3,256,128]{2,1,0:T(8,128)(2,1)S(1)} %collective-permute-done.17.refs_1_, bf16[3,256,128]{2,1,0:T(8,128)(2,1)S(1)} %collective-permute-done.18.refs_2_, ...), custom_call_target="tpu_custom_call" | custom-call | bytes 1572864 | tf_op jit(solution)/shard_map/pallas_call | solution.py:29
  55.0 0.0 collective-permute-done.20.refs_1_
  55.0 1.2 %collective-permute-done.22.refs_2_ = bf16[256,512]{1,0:T(8,128)(2,1)S(1)} collective-permute-done((bf16[256,512]{1,0:T(8,128)(2,1)S(1)}, bf16[256,512]{1,0:T(8,128)(2,1)S(1)}, u32[]{:S(2)}, u32[]{:S(2)}) %collective-permute-start.22) | collective-permute-done | bytes 262176 | tf_op jit(solution)/shard_map/ppermute | solution.py:214
  56.2 0.8 %shard_map.102 = bf16[256,512]{1,0:T(8,128)(2,1)} custom-call(bf16[256,512]{1,0:T(8,128)(2,1)S(1)} %get-tuple-element.72.refs_0_, bf16[256,512]{1,0:T(8,128)(2,1)S(1)} %collective-permute-done.20.refs_1_, bf16[256,512]{1,0:T(8,128)(2,1)S(1)} %collective-permute-done.22.refs_2_), custom_call_target="tpu_custom_call" | custom-call | tf_op jit(solution)/shard_map/pallas_call | solution.py:29
  (9 shorter events, 0.2 us)
Async XLA Ops:
  0.6 19.4 %collective-permute-start.3 = (bf16[256,512]{1,0:T(8,128)(2,1)}, bf16[256,512]{1,0:T(8,128)(2,1)S(1)}, u32[]{:S(2)}, u32[]{:S(2)}) collective-permute-start(bf16[256,512]{1,0:T(8,128)(2,1)} %refs_0_), channel_id=1, source_target_pairs={{0,2},{1,3},{2,0},{3,1},{4,6},{5,7},{6,4},{7,5},{8,10},{9,11},{10,... | collective-permute-start | bytes 786440 | tf_op jit(solution)/shard_map/ppermute | solution.py:214
  4.7 15.3 %collective-permute-start.4 = (bf16[256,512]{1,0:T(8,128)(2,1)}, bf16[256,512]{1,0:T(8,128)(2,1)S(1)}, u32[]{:S(2)}, u32[]{:S(2)}) collective-permute-start(bf16[256,512]{1,0:T(8,128)(2,1)} %refs_0_), channel_id=1, source_target_pairs={{0,1},{1,0},{2,3},{3,2},{4,5},{5,4},{6,7},{7,6},{8,9},{9,8},{10,11... | collective-permute-start | bytes 786440 | tf_op jit(solution)/shard_map/ppermute | solution.py:214
  6.3 15.3 %copy-start.2 = (s32[4,4]{1,0:T(4,128)S(1)}, s32[4,4]{1,0:T(4,128)}, u32[]{:S(2)}) copy-start(s32[4,4]{1,0:T(4,128)} %perm.3) | copy-start | bytes 196
  8.4 6.8 %collective-permute-start.1 = (bf16[3,256,128]{2,1,0:T(8,128)(2,1)S(1)}, bf16[3,256,128]{2,1,0:T(8,128)(2,1)S(1)}, u32[]{:S(2)}, u32[]{:S(2)}) collective-permute-start(bf16[3,256,128]{2,1,0:T(8,128)(2,1)S(1)} %pad_maximum_fusion.2), channel_id=1, source_target_pairs={{0,16},{4,20},{8,24},{12,28},{16,0},{20,4},{24,8},{28,12},{1,17},{... | collective-permute-start | bytes 589832 | tf_op jit(solution)/shard_map/ppermute | solution.py:193
  10.0 7.9 %collective-permute-start = (bf16[3,256,128]{2,1,0:T(8,128)(2,1)S(1)}, bf16[3,256,128]{2,1,0:T(8,128)(2,1)S(1)}, u32[]{:S(2)}, u32[]{:S(2)}) collective-permute-start(bf16[3,256,128]{2,1,0:T(8,128)(2,1)S(1)} %pad_maximum_fusion.1), channel_id=1, source_target_pairs={{0,8},{4,12},{8,0},{12,4},{16,24},{20,28},{24,16},{28,20},{1,9},{5... | collective-permute-start | bytes 589832 | tf_op jit(solution)/shard_map/ppermute | solution.py:193
  11.6 16.1 %copy-start = (bf16[4,128,2048]{2,1,0:T(8,128)(2,1)S(1)}, bf16[4,128,2048]{2,1,0:T(8,128)(2,1)}, u32[]{:S(2)}) copy-start(bf16[4,128,2048]{2,1,0:T(8,128)(2,1)} %weight.7) | copy-start | bytes 6291460
  11.6 16.1 %copy-start.1 = (bf16[256,512]{1,0:T(8,128)(2,1)S(1)}, bf16[256,512]{1,0:T(8,128)(2,1)}, u32[]{:S(2)}) copy-start(bf16[256,512]{1,0:T(8,128)(2,1)} %refs_0_) | copy-start | bytes 786436
  11.6 8.4 %collective-permute-start.2 = (bf16[3,256,128]{2,1,0:T(8,128)(2,1)S(1)}, bf16[3,256,128]{2,1,0:T(8,128)(2,1)S(1)}, u32[]{:S(2)}, u32[]{:S(2)}) collective-permute-start(bf16[3,256,128]{2,1,0:T(8,128)(2,1)S(1)} %pad_maximum_fusion.3), channel_id=1, source_target_pairs={{0,24},{4,28},{8,16},{12,20},{16,8},{20,12},{24,0},{28,4},{1,25},{... | collective-permute-start | bytes 589832 | tf_op jit(solution)/shard_map/ppermute | solution.py:193
  15.2 6.0 %collective-permute-start.5 = (bf16[2,256,128]{2,1,0:T(8,128)(2,1)S(1)}, bf16[2,256,128]{2,1,0:T(8,128)(2,1)S(1)}, u32[]{:S(2)}, u32[]{:S(2)}) collective-permute-start(bf16[2,256,128]{2,1,0:T(8,128)(2,1)S(1)} %pad_maximum_fusion.4), channel_id=1, source_target_pairs={{0,4},{4,0},{8,12},{12,8},{16,20},{20,16},{24,28},{28,24},{1,5},{5... | collective-permute-start | bytes 393224 | tf_op jit(solution)/shard_map/ppermute | solution.py:196
  17.9 3.3 %collective-permute-start.7 = (bf16[2,256,128]{2,1,0:T(8,128)(2,1)S(1)}, bf16[2,256,128]{2,1,0:T(8,128)(2,1)S(1)}, u32[]{:S(2)}, u32[]{:S(2)}) collective-permute-start(bf16[2,256,128]{2,1,0:T(8,128)(2,1)S(1)} %slice.31), channel_id=1, source_target_pairs={{0,4},{4,0},{8,12},{12,8},{16,20},{20,16},{24,28},{28,24},{1,5},{5... | collective-permute-start | bytes 393224 | tf_op jit(solution)/shard_map/ppermute | solution.py:196
  20.1 1.3 %collective-permute-start.6 = (bf16[2,256,128]{2,1,0:T(8,128)(2,1)S(1)}, bf16[2,256,128]{2,1,0:T(8,128)(2,1)S(1)}, u32[]{:S(2)}, u32[]{:S(2)}) collective-permute-start(bf16[2,256,128]{2,1,0:T(8,128)(2,1)S(1)} %slice.30), channel_id=1, source_target_pairs={{0,4},{4,0},{8,12},{12,8},{16,20},{20,16},{24,28},{28,24},{1,5},{5... | collective-permute-start | bytes 393224 | tf_op jit(solution)/shard_map/ppermute | solution.py:196
  20.1 1.6 %collective-permute-start.8 = (bf16[2,256,128]{2,1,0:T(8,128)(2,1)S(1)}, bf16[2,256,128]{2,1,0:T(8,128)(2,1)S(1)}, u32[]{:S(2)}, u32[]{:S(2)}) collective-permute-start(bf16[2,256,128]{2,1,0:T(8,128)(2,1)S(1)} %slice.25), channel_id=1, source_target_pairs={{0,4},{4,0},{8,12},{12,8},{16,20},{20,16},{24,28},{28,24},{1,5},{5... | collective-permute-start | bytes 393224 | tf_op jit(solution)/shard_map/ppermute | solution.py:196
  20.7 8.3 %collective-permute-start.9 = (bf16[256,512]{1,0:T(8,128)(2,1)S(1)}, bf16[256,512]{1,0:T(8,128)(2,1)S(1)}, u32[]{:S(2)}, u32[]{:S(2)}) collective-permute-start(bf16[256,512]{1,0:T(8,128)(2,1)S(1)} %collective-permute-done.3.refs_2_), channel_id=1, source_target_pairs={{0,1},{1,0},{2,3},{3,2},{4,5},{5,4},{6,7},{7,6},{8,9},{9,8},{10,11... | collective-permute-start | bytes 786440 | tf_op jit(solution)/shard_map/ppermute | solution.py:214
  24.2 8.3 %collective-permute-start.12 = (bf16[256,128]{1,0:T(8,128)(2,1)S(1)}, bf16[256,128]{1,0:T(8,128)(2,1)S(1)}, u32[]{:S(2)}, u32[]{:S(2)}) collective-permute-start(bf16[256,128]{1,0:T(8,128)(2,1)S(1)} %get-tuple-element.80), channel_id=1, source_target_pairs={{0,24},{4,28},{8,16},{12,20},{16,8},{20,12},{24,0},{28,4},{1,25},{... | collective-permute-start | bytes 196616 | tf_op jit(solution)/shard_map/ppermute | solution.py:193
  26.7 6.2 %collective-permute-start.11 = (bf16[256,128]{1,0:T(8,128)(2,1)S(1)}, bf16[256,128]{1,0:T(8,128)(2,1)S(1)}, u32[]{:S(2)}, u32[]{:S(2)}) collective-permute-start(bf16[256,128]{1,0:T(8,128)(2,1)S(1)} %get-tuple-element.81), channel_id=1, source_target_pairs={{0,16},{4,20},{8,24},{12,28},{16,0},{20,4},{24,8},{28,12},{1,17},{... | collective-permute-start | bytes 196616 | tf_op jit(solution)/shard_map/ppermute | solution.py:193
  27.2 5.7 %collective-permute-start.10 = (bf16[256,128]{1,0:T(8,128)(2,1)S(1)}, bf16[256,128]{1,0:T(8,128)(2,1)S(1)}, u32[]{:S(2)}, u32[]{:S(2)}) collective-permute-start(bf16[256,128]{1,0:T(8,128)(2,1)S(1)} %get-tuple-element.82), channel_id=1, source_target_pairs={{0,8},{4,12},{8,0},{12,4},{16,24},{20,28},{24,16},{28,20},{1,9},{5... | collective-permute-start | bytes 196616 | tf_op jit(solution)/shard_map/ppermute | solution.py:193
  29.4 5.1 %collective-permute-start.13 = (bf16[256,128]{1,0:T(8,128)(2,1)S(1)}, bf16[256,128]{1,0:T(8,128)(2,1)S(1)}, u32[]{:S(2)}, u32[]{:S(2)}) collective-permute-start(bf16[256,128]{1,0:T(8,128)(2,1)S(1)} %get-tuple-element.54), channel_id=1, source_target_pairs={{0,8},{4,12},{8,0},{12,4},{16,24},{20,28},{24,16},{28,20},{1,9},{5... | collective-permute-start | bytes 196616 | tf_op jit(solution)/shard_map/ppermute | solution.py:193
  30.9 5.0 %collective-permute-start.14 = (bf16[256,128]{1,0:T(8,128)(2,1)S(1)}, bf16[256,128]{1,0:T(8,128)(2,1)S(1)}, u32[]{:S(2)}, u32[]{:S(2)}) collective-permute-start(bf16[256,128]{1,0:T(8,128)(2,1)S(1)} %get-tuple-element.55), channel_id=1, source_target_pairs={{0,16},{4,20},{8,24},{12,28},{16,0},{20,4},{24,8},{28,12},{1,17},{... | collective-permute-start | bytes 196616 | tf_op jit(solution)/shard_map/ppermute | solution.py:193
  32.4 5.2 %collective-permute-start.15 = (bf16[256,128]{1,0:T(8,128)(2,1)S(1)}, bf16[256,128]{1,0:T(8,128)(2,1)S(1)}, u32[]{:S(2)}, u32[]{:S(2)}) collective-permute-start(bf16[256,128]{1,0:T(8,128)(2,1)S(1)} %get-tuple-element.56), channel_id=1, source_target_pairs={{0,24},{4,28},{8,16},{12,20},{16,8},{20,12},{24,0},{28,4},{1,25},{... | collective-permute-start | bytes 196616 | tf_op jit(solution)/shard_map/ppermute | solution.py:193
  33.3 7.9 %collective-permute-start.21 = (bf16[256,512]{1,0:T(8,128)(2,1)S(1)}, bf16[256,512]{1,0:T(8,128)(2,1)S(1)}, u32[]{:S(2)}, u32[]{:S(2)}) collective-permute-start(bf16[256,512]{1,0:T(8,128)(2,1)S(1)} %get-tuple-element.75), channel_id=1, source_target_pairs={{0,1},{1,0},{2,3},{3,2},{4,5},{5,4},{6,7},{7,6},{8,9},{9,8},{10,11... | collective-permute-start | bytes 786440 | tf_op jit(solution)/shard_map/ppermute | solution.py:214
  40.5 2.0 %collective-permute-start.16 = (bf16[4,2,256,128]{3,2,1,0:T(8,128)(2,1)S(1)}, bf16[4,2,256,128]{3,2,1,0:T(8,128)(2,1)S(1)}, u32[]{:S(2)}, u32[]{:S(2)}) collective-permute-start(bf16[4,2,256,128]{3,2,1,0:T(8,128)(2,1)S(1)} %get-tuple-element.64), channel_id=1, source_target_pairs={{0,4},{4,0},{8,12},{12,8},{16,20},{20,16},{24,28},{28,24},{1,5},{5... | collective-permute-start | bytes 1572872 | tf_op jit(solution)/shard_map/ppermute | solution.py:196
  40.5 14.5 %collective-permute-start.20 = (bf16[256,512]{1,0:T(8,128)(2,1)S(1)}, bf16[256,512]{1,0:T(8,128)(2,1)S(1)}, u32[]{:S(2)}, u32[]{:S(2)}) collective-permute-start(bf16[256,512]{1,0:T(8,128)(2,1)S(1)} %get-tuple-element.74), channel_id=1, source_target_pairs={{0,1},{1,0},{2,3},{3,2},{4,5},{5,4},{6,7},{7,6},{8,9},{9,8},{10,11... | collective-permute-start | bytes 786440 | tf_op jit(solution)/shard_map/ppermute | solution.py:214
  41.2 15.0 %collective-permute-start.22 = (bf16[256,512]{1,0:T(8,128)(2,1)S(1)}, bf16[256,512]{1,0:T(8,128)(2,1)S(1)}, u32[]{:S(2)}, u32[]{:S(2)}) collective-permute-start(bf16[256,512]{1,0:T(8,128)(2,1)S(1)} %shard_map.101), channel_id=1, source_target_pairs={{0,2},{1,3},{2,0},{3,1},{4,6},{5,7},{6,4},{7,5},{8,10},{9,11},{10,... | collective-permute-start | bytes 786440 | tf_op jit(solution)/shard_map/ppermute | solution.py:214
  42.6 7.8 %collective-permute-start.17 = (bf16[3,256,128]{2,1,0:T(8,128)(2,1)S(1)}, bf16[3,256,128]{2,1,0:T(8,128)(2,1)S(1)}, u32[]{:S(2)}, u32[]{:S(2)}) collective-permute-start(bf16[3,256,128]{2,1,0:T(8,128)(2,1)S(1)} %get-tuple-element.66), channel_id=1, source_target_pairs={{0,8},{4,12},{8,0},{12,4},{16,24},{20,28},{24,16},{28,20},{1,9},{5... | collective-permute-start | bytes 589832 | tf_op jit(solution)/shard_map/ppermute | solution.py:193
  43.2 10.9 %collective-permute-start.18 = (bf16[3,256,128]{2,1,0:T(8,128)(2,1)S(1)}, bf16[3,256,128]{2,1,0:T(8,128)(2,1)S(1)}, u32[]{:S(2)}, u32[]{:S(2)}) collective-permute-start(bf16[3,256,128]{2,1,0:T(8,128)(2,1)S(1)} %get-tuple-element.67), channel_id=1, source_target_pairs={{0,16},{4,20},{8,24},{12,28},{16,0},{20,4},{24,8},{28,12},{1,17},{... | collective-permute-start | bytes 589832 | tf_op jit(solution)/shard_map/ppermute | solution.py:193
  43.7 10.4 %collective-permute-start.19 = (bf16[3,256,128]{2,1,0:T(8,128)(2,1)S(1)}, bf16[3,256,128]{2,1,0:T(8,128)(2,1)S(1)}, u32[]{:S(2)}, u32[]{:S(2)}) collective-permute-start(bf16[3,256,128]{2,1,0:T(8,128)(2,1)S(1)} %get-tuple-element.68), channel_id=1, source_target_pairs={{0,24},{4,28},{8,16},{12,20},{16,8},{20,12},{24,0},{28,4},{1,25},{... | collective-permute-start | bytes 589832 | tf_op jit(solution)/shard_map/ppermute | solution.py:193
